TPU v7x, 128 devices: a whole 4x4x4 slice. The times are simulated.
128 devices in a mesh: seq: 16 (over y, x), chan: 8 (over z, core).
Axes of the slice: x: 4, y: 4, z: 4, core: 2. Of those that a mesh axis runs over, the one named last changes fastest.
Arguments:
- gate_out: bfloat16 [16384, 2048], P('seq', 'chan'), may hold values from -6 to 6
- gate_in: bfloat16 [16384, 2048], P('seq', 'chan'), may hold values from -6 to 6
- value_in: bfloat16 [16384, 2048], P('seq', 'chan'), may hold values from -6 to 6
- filter_taps: float32 [16384, 2048], P('seq', 'chan'), may hold values from -1 to 1
- skip_bias: float32 [2048], P('chan'), may hold values from 0.5 to 1.5
- resume_at: int32 [1], replicated, may hold values from 0 to 8191
- out_weight: bfloat16 [2048, 4096], P('chan'), may hold values from -0.1875 to 0.1875
Outputs:
- projected: bfloat16 [16384, 4096], P('seq', 'chan')
Inputs may be any that keep to these rules, and one draw needn't show every extreme that they name: `resume_at`: a single position.
All inputs are finite; a program needn't handle non-finite values.
Results may differ from a plain program's by a relative error of at most 0.0049.
Values may be sent and summed in bfloat16 or wider, within the bound.
No kernel may reach another device: no remote copies, remote signals or barrier semaphores. Data moves between devices by JAX's collectives and lax.ppermute only.
A program may use at most 192 MiB of HBM per device.

v0:
```python
import math

import jax
import jax.numpy as jnp
from jax import lax
from jax.sharding import PartitionSpec as P

HIGHEST = lax.Precision.HIGHEST


def phase_pair(phase_turns, modulus):
    angles = phase_turns.astype(jnp.float32) * (2.0 * math.pi / modulus)
    return (jnp.cos(angles), jnp.sin(angles))


def spectrum(cosine_table, sine_table, real_part, imag_part):
    real_out = jnp.dot(cosine_table, real_part, precision=HIGHEST) + jnp.dot(
        sine_table, imag_part, precision=HIGHEST
    )
    imag_out = jnp.dot(cosine_table, imag_part, precision=HIGHEST) - jnp.dot(
        sine_table, real_part, precision=HIGHEST
    )
    return (real_out, imag_out)


def restore(cosine_table, sine_table, real_part, imag_part):
    real_out = jnp.einsum("ar,ac->rc", cosine_table, real_part, precision=HIGHEST) - jnp.einsum(
        "ar,ac->rc", sine_table, imag_part, precision=HIGHEST
    )
    imag_out = jnp.einsum("ar,ac->rc", cosine_table, imag_part, precision=HIGHEST) + jnp.einsum(
        "ar,ac->rc", sine_table, real_part, precision=HIGHEST
    )
    return (real_out, imag_out)


def on_device(gate_out, gate_in, value_in, filter_taps, skip_bias, resume_at, out_weight):
    shard_rows, channels = value_in.shape
    shards = lax.axis_size("seq")
    period = 2 * shard_rows * shards
    my_index = lax.axis_index("seq")
    signal = gate_in.astype(jnp.float32) * value_in.astype(jnp.float32)
    own_freq = 2 * my_index + jnp.arange(2, dtype=jnp.int32)
    exchanged = (
        lax.all_to_all(signal[None], "seq", split_axis=1, concat_axis=0, tiled=True),
        lax.all_to_all(filter_taps[None], "seq", split_axis=1, concat_axis=0, tiled=True),
    )
    grid_turns = (
        jnp.arange(2 * shards, dtype=jnp.int32)[:, None]
        * jnp.arange(shards, dtype=jnp.int32)[None, :]
        % (2 * shards)
    )
    cosine_table, sine_table = phase_pair(grid_turns, 2 * shards)
    signal_real = jnp.einsum("kp,prc->krc", cosine_table, exchanged[0], precision=HIGHEST)
    signal_imag = jnp.einsum("kp,prc->krc", -sine_table, exchanged[0], precision=HIGHEST)
    taps_real = jnp.einsum("kp,prc->krc", cosine_table, exchanged[1], precision=HIGHEST)
    taps_imag = jnp.einsum("kp,prc->krc", -sine_table, exchanged[1], precision=HIGHEST)
    regrouped = (
        lax.all_to_all(signal_real, "seq", split_axis=0, concat_axis=1, tiled=True),
        lax.all_to_all(signal_imag, "seq", split_axis=0, concat_axis=1, tiled=True),
        lax.all_to_all(taps_real, "seq", split_axis=0, concat_axis=1, tiled=True),
        lax.all_to_all(taps_imag, "seq", split_axis=0, concat_axis=1, tiled=True),
    )
    spectra = ((regrouped[0], regrouped[1]), (regrouped[2], regrouped[3]))
    positions = jnp.arange(shard_rows, dtype=jnp.int32)
    inverse_real = []
    inverse_imag = []
    for member in range(2):
        frequency = own_freq[member] + 2 * shards * positions
        cosine_table, sine_table = phase_pair(
            frequency[:, None] * positions[None, :] % period, period
        )
        signal_real, signal_imag = spectrum(
            cosine_table, sine_table, spectra[0][0][member], spectra[0][1][member]
        )
        taps_real, taps_imag = spectrum(
            cosine_table, sine_table, spectra[1][0][member], spectra[1][1][member]
        )
        product_real = signal_real * taps_real - signal_imag * taps_imag
        product_imag = signal_real * taps_imag + signal_imag * taps_real
        back_real, back_imag = restore(cosine_table, sine_table, product_real, product_imag)
        inverse_real.append(back_real)
        inverse_imag.append(back_imag)
    returned = (
        lax.all_to_all(jnp.stack(inverse_real), "seq", split_axis=1, concat_axis=0, tiled=True),
        lax.all_to_all(jnp.stack(inverse_imag), "seq", split_axis=1, concat_axis=0, tiled=True),
    )
    grid_turns = (
        jnp.arange(shards, dtype=jnp.int32)[:, None]
        * jnp.arange(2 * shards, dtype=jnp.int32)[None, :]
        % (2 * shards)
    )
    cosine_table, sine_table = phase_pair(grid_turns, 2 * shards)
    time_blocks = jnp.einsum(
        "pk,krc->prc", cosine_table, returned[0], precision=HIGHEST
    ) - jnp.einsum("pk,krc->prc", sine_table, returned[1], precision=HIGHEST)
    time_blocks = time_blocks * (1.0 / period)
    convolved = lax.all_to_all(time_blocks, "seq", split_axis=0, concat_axis=1, tiled=True)[0]
    kept_rows = (my_index * shard_rows + positions >= resume_at[0])[:, None]
    mixed = gate_out.astype(jnp.float32) * (convolved + skip_bias[None, :] * signal)
    mixed = jnp.where(kept_rows, mixed, jnp.zeros_like(mixed)).astype(jnp.bfloat16)
    summed = lax.psum_scatter(
        lax.dot_general(
            out_weight, mixed, (((0,), (1,)), ((), ())), preferred_element_type=jnp.float32
        ),
        "chan",
        scatter_dimension=0,
        tiled=True,
    )
    return summed.T.astype(jnp.bfloat16)


def solution(mesh):
    placed = (
        P("seq", "chan"),
        P("seq", "chan"),
        P("seq", "chan"),
        P("seq", "chan"),
        P("chan"),
        P(),
        P("chan", None),
    )
    return jax.shard_map(
        on_device, mesh=mesh, in_specs=placed, out_specs=P("seq", "chan"), check_vma=False
    )
```

profile of v0, /device:TPU:1, one launch (start us, length us, event | category | flops | bytes accessed | tf_op | source)
XLA Modules:
  0.0 934.5 jit_solution(13024414819948338647)
XLA Ops:
  107.5 27.5 %fusion.20 = f32[1024,256]{1,0:T(8,128)} fusion(f32[1024,256]{1,0:T(8,128)S(1)} %bitcast.116, s32[1024]{0:T(1024)S(1)} %fusion.151), kind=kOutput, calls=%fused_computation.28 | convolution fusion | flops 3235905536 | bytes 2101248 | tf_op jit(solution)/shard_map/dot_general | solution.py:20
  143.5 27.6 %fusion.24 = f32[1024,256]{1,0:T(8,128)} fusion(f32[1024,256]{1,0:T(8,128)S(1)} %bitcast.110, s32[1024]{0:T(1024)S(1)} %fusion.151), kind=kOutput, calls=%fused_computation.30 | convolution fusion | flops 3235905536 | bytes 2101248 | tf_op jit(solution)/shard_map/dot_general | solution.py:17
  171.1 27.6 %fusion.46 = f32[1024,256]{1,0:T(8,128)} fusion(f32[1024,256]{1,0:T(8,128)S(1)} %bitcast.114, s32[1024]{0:T(1024)S(1)} %fusion.152), kind=kOutput, calls=%fused_computation.42 | convolution fusion | flops 3235905536 | bytes 2101248 | tf_op jit(solution)/shard_map/dot_general | solution.py:20
  198.8 27.6 %fusion.50 = f32[1024,256]{1,0:T(8,128)} fusion(f32[1024,256]{1,0:T(8,128)S(1)} %bitcast.112, s32[1024]{0:T(1024)S(1)} %fusion.152), kind=kOutput, calls=%fused_computation.44 | convolution fusion | flops 3235905536 | bytes 2101248 | tf_op jit(solution)/shard_map/dot_general | solution.py:17
  235.2 27.6 %fusion.18 = f32[1024,256]{1,0:T(8,128)} fusion(f32[1024,256]{1,0:T(8,128)S(1)} %bitcast.120, s32[1024]{0:T(1024)S(1)} %fusion.151), kind=kOutput, calls=%fused_computation.27 | convolution fusion | flops 3235905536 | bytes 2101248 | tf_op jit(solution)/shard_map/dot_general | solution.py:20
  262.8 27.6 %fusion.44 = f32[1024,256]{1,0:T(8,128)} fusion(f32[1024,256]{1,0:T(8,128)S(1)} %bitcast.118, s32[1024]{0:T(1024)S(1)} %fusion.152), kind=kOutput, calls=%fused_computation.41 | convolution fusion | flops 3235905536 | bytes 2101248 | tf_op jit(solution)/shard_map/dot_general | solution.py:20
  290.5 27.8 %fusion.89 = f32[1024,256]{1,0:T(8,128)} fusion(f32[1024,256]{1,0:T(8,128)S(1)} %copy-done.26, f32[1024,256]{1,0:T(8,128)S(1)} %bitcast.117, s32[1024]{0:T(1024)S(1)} %fusion.151), kind=kOutput, calls=%fused_computation.61 | convolution fusion | flops 3236167680 | bytes 3149824 | tf_op jit(solution)/shard_map/dot_general | solution.py:17
  318.3 27.8 %fusion.65 = f32[1024,256]{1,0:T(8,128)} fusion(f32[1024,256]{1,0:T(8,128)S(1)} %copy-done.27, f32[1024,256]{1,0:T(8,128)S(1)} %bitcast.115, s32[1024]{0:T(1024)S(1)} %fusion.152), kind=kOutput, calls=%fused_computation.53 | convolution fusion | flops 3236167680 | bytes 3149824 | tf_op jit(solution)/shard_map/dot_general | solution.py:17
  347.7 26.9 %fusion.22 = f32[1024,256]{1,0:T(8,128)S(1)} fusion(f32[1024,256]{1,0:T(8,128)S(1)} %bitcast.124, s32[1024]{0:T(1024)S(1)} %fusion.151), kind=kOutput, calls=%fused_computation.29 | convolution fusion | flops 3235905536 | bytes 2101248 | tf_op jit(solution)/shard_map/dot_general | solution.py:17
  374.7 27.1 %fusion.98 = f32[1024,256]{1,0:T(8,128)S(1)} fusion(f32[1024,256]{1,0:T(8,128)S(1)} %copy-done.28, f32[1024,256]{1,0:T(8,128)S(1)} %bitcast.125, s32[1024]{0:T(1024)S(1)} %fusion.151), kind=kOutput, calls=%fused_computation.64 | convolution fusion | flops 3236167680 | bytes 3149824 | tf_op jit(solution)/shard_map/dot_general | solution.py:20
  401.8 27.1 %fusion.92 = f32[1024,256]{1,0:T(8,128)S(1)} fusion(f32[1024,256]{1,0:T(8,128)S(1)} %fusion.22, f32[1024,256]{1,0:T(8,128)S(1)} %bitcast.121, s32[1024]{0:T(1024)S(1)} %fusion.151), kind=kOutput, calls=%fused_computation.62 | convolution fusion | flops 3236167680 | bytes 3149824 | tf_op jit(solution)/shard_map/dot_general | solution.py:17
  428.9 27.1 %fusion.48 = f32[1024,256]{1,0:T(8,128)S(1)} fusion(f32[1024,256]{1,0:T(8,128)S(1)} %bitcast.122, s32[1024]{0:T(1024)S(1)} %fusion.152), kind=kOutput, calls=%fused_computation.43 | convolution fusion | flops 3235905536 | bytes 2101248 | tf_op jit(solution)/shard_map/dot_general | solution.py:17
  456.1 27.1 %fusion.74 = f32[1024,256]{1,0:T(8,128)S(1)} fusion(f32[1024,256]{1,0:T(8,128)S(1)} %copy-done.25, f32[1024,256]{1,0:T(8,128)S(1)} %bitcast.123, s32[1024]{0:T(1024)S(1)} %fusion.152), kind=kOutput, calls=%fused_computation.56 | convolution fusion | flops 3236167680 | bytes 3149824 | tf_op jit(solution)/shard_map/dot_general | solution.py:20
  483.2 27.1 %fusion.68 = f32[1024,256]{1,0:T(8,128)S(1)} fusion(f32[1024,256]{1,0:T(8,128)S(1)} %fusion.48, f32[1024,256]{1,0:T(8,128)S(1)} %bitcast.119, s32[1024]{0:T(1024)S(1)} %fusion.152), kind=kOutput, calls=%fused_computation.54 | convolution fusion | flops 3236167680 | bytes 3149824 | tf_op jit(solution)/shard_map/dot_general | solution.py:17
  510.4 27.2 %multiply_add_fusion.1 = (f32[1024,256]{1,0:T(8,128)S(1)}, f32[1024,256]{1,0:T(8,128)S(1)}) fusion(f32[1024,256]{1,0:T(8,128)S(1)} %fusion.68, f32[1024,256]{1,0:T(8,128)S(1)} %copy-done.24, f32[1024,256]{1,0:T(8,128)S(1)} %fusion.74, f32[1024,256]{1,0:T(8,128)S(1)} %copy-done.22, f32[1024,256]{1,0:T(8,128)S(1)} %bitcast.113, s32[1024]{0:T(1024)S(1)} %fusion.152), kind=kOutput, calls=%fused_computation.76 | convolution fusion | flops 3237740544 | bytes 7344128 | tf_op jit(solution)/shard_map/dot_general | solution.py:20
  537.6 21.9 %fusion.40 = f32[1024,256]{1,0:T(8,128)S(1)} fusion(f32[1024,256]{1,0:T(8,128)S(1)} %get-tuple-element.5, s32[1024]{0:T(1024)S(1)} %fusion.152), kind=kOutput, calls=%fused_computation.39 | convolution fusion | flops 3235905536 | bytes 2101248 | tf_op jit(solution)/shard_map/ar,ac->rc/dot_general | solution.py:30
  559.5 23.1 %fusion.42 = f32[1024,256]{1,0:T(8,128)} fusion(f32[1024,256]{1,0:T(8,128)S(1)} %get-tuple-element.6, s32[1024]{0:T(1024)S(1)} %fusion.152), kind=kOutput, calls=%fused_computation.40 | convolution fusion | flops 3235905536 | bytes 2101248 | tf_op jit(solution)/shard_map/ar,ac->rc/dot_general | solution.py:27
  582.6 22.2 %fusion.86 = f32[1,1024,256]{2,1,0:T(8,128)S(1)} fusion(f32[1024,256]{1,0:T(8,128)S(1)} %fusion.40, f32[1024,256]{1,0:T(8,128)S(1)} %get-tuple-element.6, s32[1024]{0:T(1024)S(1)} %fusion.152), kind=kOutput, calls=%fused_computation.60 | convolution fusion | flops 3236167680 | bytes 3149824 | tf_op jit(solution)/shard_map/ar,ac->rc/dot_general | solution.py:30
  604.8 27.4 %multiply_add_fusion = (f32[1024,256]{1,0:T(8,128)S(1)}, f32[1024,256]{1,0:T(8,128)S(1)}) fusion(f32[1024,256]{1,0:T(8,128)S(1)} %fusion.92, f32[1024,256]{1,0:T(8,128)S(1)} %copy-done.23, f32[1024,256]{1,0:T(8,128)S(1)} %fusion.98, f32[1024,256]{1,0:T(8,128)S(1)} %copy-done.21, f32[1024,256]{1,0:T(8,128)S(1)} %bitcast.111, s32[1024]{0:T(1024)S(1)} %fusion.151), kind=kOutput, calls=%fused_computation.74 | convolution fusion | flops 3237740544 | bytes 7344128 | tf_op jit(solution)/shard_map/dot_general | solution.py:20
  632.2 21.9 %fusion.14 = f32[1024,256]{1,0:T(8,128)S(1)} fusion(f32[1024,256]{1,0:T(8,128)S(1)} %get-tuple-element.7, s32[1024]{0:T(1024)S(1)} %fusion.151), kind=kOutput, calls=%fused_computation.25 | convolution fusion | flops 3235905536 | bytes 2101248 | tf_op jit(solution)/shard_map/ar,ac->rc/dot_general | solution.py:30
  654.2 22.7 %fusion.110 = f32[1,1024,256]{2,1,0:T(8,128)S(1)} fusion(f32[1024,256]{1,0:T(8,128)S(1)} %fusion.14, f32[1024,256]{1,0:T(8,128)S(1)} %get-tuple-element.8, s32[1024]{0:T(1024)S(1)} %fusion.151), kind=kOutput, calls=%fused_computation.68 | convolution fusion | flops 3236167680 | bytes 3149824 | tf_op jit(solution)/shard_map/ar,ac->rc/dot_general | solution.py:30
  708.8 22.2 %fusion.80 = f32[1,1024,256]{2,1,0:T(8,128)S(1)} fusion(f32[1024,256]{1,0:T(8,128)S(1)} %copy-done.16, f32[1024,256]{1,0:T(8,128)S(1)} %copy-done.15, s32[1024]{0:T(1024)S(1)} %fusion.152), kind=kOutput, calls=%fused_computation.58 | convolution fusion | flops 3236167680 | bytes 3149824 | tf_op jit(solution)/shard_map/ar,ac->rc/dot_general | solution.py:27
  731.0 22.6 %fusion.104 = f32[1,1024,256]{2,1,0:T(8,128)S(1)} fusion(f32[1024,256]{1,0:T(8,128)S(1)} %fusion.16, f32[1024,256]{1,0:T(8,128)S(1)} %copy-done.18, s32[1024]{0:T(1024)S(1)} %fusion.151), kind=kOutput, calls=%fused_computation.66 | convolution fusion | flops 3236167680 | bytes 3149824 | tf_op jit(solution)/shard_map/ar,ac->rc/dot_general | solution.py:27
  828.8 96.0 %reduce-scatter.2.cloned.1.call-done = f32[512,1024]{0,1:T(8,128)} async-done(((f32[4096,1024]{0,1:T(8,128)}), f32[512,1024]{0,1:T(8,128)}) %reduce-scatter.2.cloned.1.call-update) | async-done | bytes 2097168 | tf_op jit(solution)/shard_map/reduce_scatter | solution.py:101
  (115 shorter events, 228.7 us)
Async XLA Ops:
  6.5 814.0 %copy-start = (bf16[256,4096]{1,0:T(8,128)(2,1)S(1)}, bf16[256,4096]{1,0:T(8,128)(2,1)}, u32[]{:S(2)}) copy-start(bf16[256,4096]{1,0:T(8,128)(2,1)} %param.13) | copy-start | bytes 6291460
  10.1 23.6 %all-to-all-start = ((f32[1,1024,256]{2,0,1:T(1,128)}), f32[1,1024,256]{2,0,1:T(1,128)S(1)}, u32[]{:S(2)}, u32[]{:S(2)}) async-start(f32[1,1024,256]{2,0,1:T(1,128)} %copy.35), calls=%async_computation | async-start | bytes 2097152 | tf_op jit(solution)/shard_map/all_to_all | solution.py:44
  34.6 19.2 %all-to-all-start.3 = ((f32[1,1024,256]{2,0,1:T(1,128)}), f32[1,1024,256]{2,0,1:T(1,128)}, u32[]{:S(2)}, u32[]{:S(2)}) async-start(f32[1,1024,256]{2,0,1:T(1,128)} %broadcast_in_dim.13), calls=%async_computation.3 | async-start | bytes 2097152 | tf_op jit(solution)/shard_map/all_to_all | solution.py:45
  53.8 29.2 %all-to-all-start.2 = ((f32[32,64,256]{2,1,0:T(8,128)}), f32[32,64,256]{2,1,0:T(8,128)}, u32[]{:S(2)}, u32[]{:S(2)}) async-start(f32[32,64,256]{2,1,0:T(8,128)} %copy.39), calls=%async_computation.2 | async-start | bytes 4194304 | tf_op jit(solution)/shard_map/all_to_all | solution.py:59
  83.1 51.9 %all-to-all-start.1 = ((f32[32,64,256]{2,1,0:T(8,128)}), f32[32,64,256]{2,1,0:T(8,128)}, u32[]{:S(2)}, u32[]{:S(2)}) async-start(f32[32,64,256]{2,1,0:T(8,128)} %copy.37), calls=%async_computation.1 | async-start | bytes 4194304 | tf_op jit(solution)/shard_map/all_to_all | solution.py:58
  135.0 91.4 %all-to-all-start.5 = ((f32[32,64,256]{2,1,0:T(8,128)}), f32[32,64,256]{2,1,0:T(8,128)}, u32[]{:S(2)}, u32[]{:S(2)}) async-start(f32[32,64,256]{2,1,0:T(8,128)} %copy.43), calls=%async_computation.5 | async-start | bytes 4194304 | tf_op jit(solution)/shard_map/all_to_all | solution.py:61
  143.5 55.3 %copy-start.3 = (f32[1,16,64,256]{3,2,0,1:T(8,128)}, f32[1,16,64,256]{3,2,0,1:T(8,128)S(1)}, u32[]{:S(2)}) copy-start(f32[1,16,64,256]{3,2,0,1:T(8,128)S(1)} %get-tuple-element.13) | copy-start | bytes 3145732
  143.5 27.6 %copy-start.5 = (f32[1,16,64,256]{3,2,0,1:T(8,128)S(1)}, f32[1,16,64,256]{3,2,0,1:T(8,128)}, u32[]{:S(2)}) copy-start(f32[1,16,64,256]{3,2,0,1:T(8,128)} %get-tuple-element.15) | copy-start | bytes 3145732
  226.4 119.6 %all-to-all-start.4 = ((f32[32,64,256]{2,1,0:T(8,128)}), f32[32,64,256]{2,1,0:T(8,128)}, u32[]{:S(2)}, u32[]{:S(2)}) async-start(f32[32,64,256]{2,1,0:T(8,128)} %copy.41), calls=%async_computation.4 | async-start | bytes 4194304 | tf_op jit(solution)/shard_map/all_to_all | solution.py:60
  235.2 27.7 %copy-start.11 = (f32[1,16,64,256]{3,2,0,1:T(8,128)}, f32[1,16,64,256]{3,2,0,1:T(8,128)S(1)}, u32[]{:S(2)}) copy-start(f32[1,16,64,256]{3,2,0,1:T(8,128)S(1)} %get-tuple-element.12) | copy-start | bytes 3145732
  235.2 27.6 %copy-start.9 = (f32[1,16,64,256]{3,2,0,1:T(8,128)}, f32[1,16,64,256]{3,2,0,1:T(8,128)S(1)}, u32[]{:S(2)}) copy-start(f32[1,16,64,256]{3,2,0,1:T(8,128)S(1)} %get-tuple-element.11) | copy-start | bytes 3145732
  262.8 27.6 %copy-start.8 = (f32[1,16,64,256]{3,2,0,1:T(8,128)S(1)}, f32[1,16,64,256]{3,2,0,1:T(8,128)}, u32[]{:S(2)}) copy-start(f32[1,16,64,256]{3,2,0,1:T(8,128)} %copy-done.7) | copy-start | bytes 3145732
  262.8 27.6 %copy-start.26 = (f32[1024,256]{1,0:T(8,128)S(1)}, f32[1024,256]{1,0:T(8,128)}, u32[]{:S(2)}) copy-start(f32[1024,256]{1,0:T(8,128)} %fusion.24) | copy-start | bytes 3145732
  290.5 27.8 %copy-start.6 = (f32[1,16,64,256]{3,2,0,1:T(8,128)S(1)}, f32[1,16,64,256]{3,2,0,1:T(8,128)}, u32[]{:S(2)}) copy-start(f32[1,16,64,256]{3,2,0,1:T(8,128)} %get-tuple-element.15) | copy-start | bytes 3145732
  290.5 27.8 %copy-start.27 = (f32[1024,256]{1,0:T(8,128)S(1)}, f32[1024,256]{1,0:T(8,128)}, u32[]{:S(2)}) copy-start(f32[1024,256]{1,0:T(8,128)} %fusion.50) | copy-start | bytes 3145732
  374.7 27.1 %copy-start.12 = (f32[1,16,64,256]{3,2,0,1:T(8,128)S(1)}, f32[1,16,64,256]{3,2,0,1:T(8,128)}, u32[]{:S(2)}) copy-start(f32[1,16,64,256]{3,2,0,1:T(8,128)} %copy-done.11) | copy-start | bytes 3145732
  428.9 27.1 %copy-start.25 = (f32[1024,256]{1,0:T(8,128)S(1)}, f32[1024,256]{1,0:T(8,128)}, u32[]{:S(2)}) copy-start(f32[1024,256]{1,0:T(8,128)} %fusion.44) | copy-start | bytes 3145732
  456.1 27.1 %copy-start.10 = (f32[1,16,64,256]{3,2,0,1:T(8,128)S(1)}, f32[1,16,64,256]{3,2,0,1:T(8,128)}, u32[]{:S(2)}) copy-start(f32[1,16,64,256]{3,2,0,1:T(8,128)} %copy-done.9) | copy-start | bytes 3145732
  483.2 27.1 %copy-start.4 = (f32[1,16,64,256]{3,2,0,1:T(8,128)S(1)}, f32[1,16,64,256]{3,2,0,1:T(8,128)}, u32[]{:S(2)}) copy-start(f32[1,16,64,256]{3,2,0,1:T(8,128)} %copy-done.3) | copy-start | bytes 3145732
  483.2 27.1 %copy-start.22 = (f32[1024,256]{1,0:T(8,128)S(1)}, f32[1024,256]{1,0:T(8,128)}, u32[]{:S(2)}) copy-start(f32[1024,256]{1,0:T(8,128)} %fusion.46) | copy-start | bytes 3145732
  680.0 76.8 %all-to-all-start.7 = ((f32[2,1024,256]{2,0,1:T(2,128)}), f32[2,1024,256]{2,0,1:T(2,128)}, u32[]{:S(2)}, u32[]{:S(2)}) async-start(f32[2,1024,256]{2,0,1:T(2,128)} %copy.46), calls=%async_computation.7 | async-start | bytes 4194304 | tf_op jit(solution)/shard_map/all_to_all | solution.py:85
  756.8 30.9 %all-to-all-start.6 = ((f32[2,1024,256]{2,0,1:T(2,128)}), f32[2,1024,256]{2,0,1:T(2,128)}, u32[]{:S(2)}, u32[]{:S(2)}) async-start(f32[2,1024,256]{2,0,1:T(2,128)} %copy.44), calls=%async_computation.6 | async-start | bytes 4194304 | tf_op jit(solution)/shard_map/all_to_all | solution.py:84
  801.1 17.7 %all-to-all-start.8 = ((f32[16,64,256]{2,1,0:T(8,128)}), f32[16,64,256]{2,1,0:T(8,128)S(1)}, u32[]{:S(2)}, u32[]{:S(2)}) async-start(f32[16,64,256]{2,1,0:T(8,128)} %copy.48), calls=%async_computation.8 | async-start | bytes 2097152 | tf_op jit(solution)/shard_map/all_to_all | solution.py:97
  806.5 118.3 %reduce-scatter.2.cloned.1.call-start = ((), (), s32[]{:S(2)}) async-start(), calls=%async_computation.10 | async-start | bytes 18874368 | tf_op jit(solution)/shard_map/reduce_scatter | solution.py:101
  (15 other events, 265.5 us)
Sparse Core Ops, SparseCore 0:
  828.9 95.8 reduce-scatter.1
where the time goes:
time: 943 us; the launch traced here: 934 us
  matrix products  638 us (68%)
  waiting for transfers between devices  166 us (18%)
  starting transfers between devices  57 us (6%)
  local copies, waits for them, and re-layouts  51.5 us (5%)
  between operations  14.9 us (2%)
    dot_general x4, matrix products, spectrum(): jnp.dot(cosine_table, imag_part, precision=HIGHEST)  110 us
    dot_general x4, matrix products, spectrum(): jnp.dot(sine_table, imag_part, precision=HIGHEST)  110 us
    dot_general x4, matrix products, spectrum(): jnp.dot(cosine_table, real_part, precision=HIGHEST)  109 us
    dot_general x4, matrix products, spectrum(): jnp.dot(sine_table, real_part, precision=HIGHEST)  109 us
    reduce_scatter x1, waiting for transfers between devices, on_device(): lax.psum_scatter(lax.dot_general(out_weight, mixed, (((0,), (1,)), ((), (...  96 us
    dot_general x2, matrix products, restore(): jnp.einsum('ar,ac->rc', cosine_table, real_part, precision=HIGHEST)  45 us
    dot_general x2, matrix products, restore(): jnp.einsum('ar,ac->rc', sine_table, imag_part, precision=HIGHEST)  44.9 us
    dot_general x2, matrix products, restore(): jnp.einsum('ar,ac->rc', sine_table, real_part, precision=HIGHEST)  44.8 us
  transfers between devices with their start and end apart: 10, of which 6 were waited for; matrix products, arithmetic and copies ran while one was open for 35% of the time, Pallas kernels for 0%

commit v1 on v0

v1 whole, which is shorter than its diff:
```python
import functools
import math

import jax
import jax.numpy as jnp
import numpy as np
from jax import lax
from jax.experimental import pallas as pl
from jax.experimental.pallas import tpu as pltpu
from jax.sharding import PartitionSpec as P

BF16 = jnp.bfloat16
F32 = jnp.float32
TILE = 128
LENGTH = TILE * TILE


def split_table(table):
    high = table.astype(jnp.bfloat16)
    low = (table - high.astype(np.float64)).astype(jnp.bfloat16)
    return high, low


@functools.lru_cache(None)
def tables():
    index = np.arange(TILE, dtype=np.float64)
    outer = 2 * math.pi * np.outer(4 * index + 1, index)
    turn = outer / 512
    first = np.concatenate([np.cos(turn), -np.sin(turn)], 0)
    first_high, first_low = split_table(first)
    last_high, last_low = split_table(first.T / LENGTH)
    twist = outer / (4 * LENGTH)
    angle = 2 * math.pi * np.outer(index, index) / TILE
    cosine, sine = np.cos(angle), np.sin(angle)
    second = np.block([[cosine, -sine], [sine, cosine]])
    second_high, second_low = split_table(second)
    back_high, back_low = split_table(second.T)
    return (
        np.concatenate([first_high, first_low], 1),
        np.concatenate([second_high, second_high, second_low], 0),
        np.concatenate([back_high, back_high, back_low], 0),
        np.concatenate([last_high, last_high, last_low], 1),
        np.cos(twist).astype(np.float32),
        np.sin(twist).astype(np.float32),
    )


def halves(array):
    high = array.astype(BF16)
    return high, (array - high.astype(F32)).astype(BF16)


def matmul(left, right):
    return jnp.dot(left, right, preferred_element_type=F32)


def pack_kernel(gate_in, value_in, taps, out):
    signal = gate_in[...].astype(F32) * value_in[...].astype(F32)
    out[:, 0, 0] = signal.T.astype(BF16).reshape(16, 16, TILE)
    out[:, 1, 0] = taps[...].T.astype(BF16).reshape(16, 16, TILE)


def pack(gate_in, value_in, taps):
    rows, channels = value_in.shape
    block = pl.BlockSpec((TILE, channels), lambda b: (b, 0))
    return pl.pallas_call(
        pack_kernel,
        grid=(rows // TILE,),
        in_specs=[block] * 3,
        out_specs=pl.BlockSpec((16, 2, 1, 16, TILE), lambda b: (0, 0, b, 0, 0)),
        out_shape=jax.ShapeDtypeStruct((16, 2, rows // TILE, 16, TILE), BF16),
        name="pack",
    )(gate_in, value_in, taps)


def conv_kernel(group, data, first, second, back, last, cosine, sine, out, signal, taps, total):
    shards, _, blocks, channels, _ = data.shape
    rows = blocks * channels

    @pl.loop(0, shards)
    def _(a):
        part = pl.ds(pl.multiple_of(a * rows, rows), rows)
        signal[part, :] = data[a, 0].astype(F32).reshape(rows, TILE)
        taps[part, :] = data[a, 1].astype(F32).reshape(rows, TILE)

    @pl.loop(0, channels // group)
    def _(step):
        cos, sin = cosine[...], sine[...]
        picks = [pl.ds(step * group + g, TILE, stride=channels) for g in range(group)]
        pieces = []
        for pick in picks:
            pair = jnp.concatenate([signal[pick, :], taps[pick, :]], 1).astype(BF16)
            lifted = matmul(first[...], jnp.concatenate([pair, pair], 0))
            for side in range(2):
                real = lifted[:TILE, side * TILE : (side + 1) * TILE]
                imag = lifted[TILE:, side * TILE : (side + 1) * TILE]
                turned = jnp.concatenate([real * cos + imag * sin, imag * cos - real * sin], 1)
                high, low = halves(turned)
                pieces.append(jnp.concatenate([high, low, high], 1))
        spectra = matmul(jnp.concatenate(pieces, 0), second[...])
        pieces = []
        for g in range(group):
            left = spectra[2 * g * TILE : (2 * g + 1) * TILE]
            right = spectra[(2 * g + 1) * TILE : (2 * g + 2) * TILE]
            real = left[:, :TILE] * right[:, :TILE] - left[:, TILE:] * right[:, TILE:]
            imag = left[:, :TILE] * right[:, TILE:] + left[:, TILE:] * right[:, :TILE]
            high, low = halves(jnp.concatenate([real, imag], 1))
            pieces.append(jnp.concatenate([high, low, high], 1))
        restored = matmul(jnp.concatenate(pieces, 0), back[...])
        pieces = []
        for g in range(group):
            real = restored[g * TILE : (g + 1) * TILE, :TILE]
            imag = restored[g * TILE : (g + 1) * TILE, TILE:]
            turned = jnp.concatenate([real * cos - imag * sin, imag * cos + real * sin], 0)
            high, low = halves(turned)
            pieces.append(jnp.concatenate([high, low, high], 0))
        result = matmul(last[...], jnp.concatenate(pieces, 1))
        for g, pick in enumerate(picks):
            total[pick, :] = result[:, g * TILE : (g + 1) * TILE]

    @pl.loop(0, shards)
    def _(a):
        part = pl.ds(pl.multiple_of(a * rows, rows), rows)
        out[a] = total[part, :].astype(BF16).reshape(blocks, channels, TILE)


def convolve(data, group=4):
    shards, _, blocks, channels, _ = data.shape
    whole = pltpu.VMEM((shards * blocks * channels, TILE), F32)
    space = pl.BlockSpec(memory_space=pltpu.VMEM)
    return pl.pallas_call(
        functools.partial(conv_kernel, group),
        in_specs=[space] * 7,
        out_specs=space,
        out_shape=jax.ShapeDtypeStruct((shards, blocks, channels, TILE), BF16),
        scratch_shapes=[whole] * 3,
        compiler_params=pltpu.CompilerParams(vmem_limit_bytes=48 << 20),
        name="convolve",
    )(data, *(jnp.asarray(table) for table in tables()))


def mix_kernel(start, conv, gate_out, gate_in, value_in, skip, out):
    rows = TILE
    first = pl.program_id(0) * rows + lax.axis_index("seq") * (rows * pl.num_programs(0))
    position = first + lax.broadcasted_iota(jnp.int32, (rows, 1), 0)
    signal = gate_in[...].astype(F32) * value_in[...].astype(F32)
    convolved = conv[:, 0].astype(F32).reshape(-1, TILE).T
    mixed = gate_out[...].astype(F32) * (convolved + skip[...] * signal)
    out[...] = jnp.where(position >= start[0], mixed, 0.0).astype(BF16)


def mix(resume_at, conv, gate_out, gate_in, value_in, skip_bias):
    rows, channels = value_in.shape
    block = pl.BlockSpec((TILE, channels), lambda b: (b, 0))
    return pl.pallas_call(
        mix_kernel,
        grid=(rows // TILE,),
        in_specs=[
            pl.BlockSpec(memory_space=pltpu.SMEM),
            pl.BlockSpec((16, 1, 16, TILE), lambda b: (0, b, 0, 0)),
            block,
            block,
            block,
            pl.BlockSpec((1, channels), lambda b: (0, 0)),
        ],
        out_specs=block,
        out_shape=jax.ShapeDtypeStruct((rows, channels), BF16),
        name="mix",
    )(resume_at, conv, gate_out, gate_in, value_in, skip_bias[None, :])


def project_kernel(mixed, weight, out):
    total = matmul(mixed[0], weight[0])
    for k in range(1, mixed.shape[0]):
        total = total + matmul(mixed[k], weight[k])
    out[...] = total.astype(BF16)


def project(mixed, weight, tile=256):
    parts, rows, channels = mixed.shape
    features = weight.shape[-1]
    return pl.pallas_call(
        project_kernel,
        grid=(rows // tile,),
        in_specs=[
            pl.BlockSpec((parts, tile, channels), lambda i: (0, i, 0)),
            pl.BlockSpec((parts, channels, features), lambda i: (0, 0, 0)),
        ],
        out_specs=pl.BlockSpec((tile, features), lambda i: (i, 0)),
        out_shape=jax.ShapeDtypeStruct((rows, features), BF16),
        compiler_params=pltpu.CompilerParams(vmem_limit_bytes=32 << 20),
        name="project",
    )(mixed, weight)


def on_device(gate_out, gate_in, value_in, filter_taps, skip_bias, resume_at, out_weight):
    members = lax.axis_size("chan")
    channels, features = out_weight.shape
    weight = lax.all_to_all(
        out_weight.reshape(channels, members, features // members).swapaxes(0, 1),
        "chan",
        split_axis=0,
        concat_axis=0,
        tiled=True,
    )
    packed = pack(gate_in, value_in, filter_taps)
    data = lax.all_to_all(packed, "seq", split_axis=0, concat_axis=0, tiled=True)
    conv = lax.all_to_all(convolve(data), "seq", split_axis=0, concat_axis=0, tiled=True)
    mixed = mix(resume_at, conv, gate_out, gate_in, value_in, skip_bias)
    return project(lax.all_gather(mixed, "chan", axis=0), weight)


def solution(mesh):
    placed = (
        P("seq", "chan"),
        P("seq", "chan"),
        P("seq", "chan"),
        P("seq", "chan"),
        P("chan"),
        P(),
        P("chan", None),
    )
    return jax.shard_map(
        on_device, mesh=mesh, in_specs=placed, out_specs=P("seq", "chan"), check_vma=False
    )
```

time: 943 us -> 133 us (0.14)
  matrix products: 638 us -> 0 us
  waiting for transfers between devices: 166 us -> 9.62 us
  blocking collectives: 0 us -> 72.3 us
  starting transfers between devices: 57 us -> 3.61 us
  local copies, waits for them, and re-layouts: 51.5 us -> 8.69 us
  Pallas kernels: 0 us -> 23.9 us
    dot_general x31 -> x0, matrix products: 638 us -> none  [the longest x4 110 us: spectrum(): jnp.dot(cosine_table, imag_part, precision=HIGHEST)]
    reduce_scatter x1 -> x0, waiting for transfers between devices: 96 us -> none  [on_device(): lax.psum_scatter(lax.dot_general(out_weight, mixed, (((0,), (1,)), ((), (...]
    all_to_all x0 -> x2, blocking collectives: none -> 72.3 us  [the longest x1 48.6 us: on_device(): lax.all_to_all(out_weight.reshape(channels, members, features // members)...]
    all_to_all x9 -> x1, waiting for transfers between devices: 69.8 us -> 8.96 us  [on_device(): lax.all_to_all(convolve(data), 'seq', split_axis=0, concat_axis=0, tiled=...]
    all_to_all x9 -> x1, starting transfers between devices: 57 us -> 3.57 us  [on_device(): lax.all_to_all(convolve(data), 'seq', split_axis=0, concat_axis=0, tiled=...]
    pallas_call x0 -> x4, Pallas kernels: none -> 23.9 us  [the longest x1 8.51 us: convolve(): pl.pallas_call(functools.partial(conv_kernel, group), in_specs=[space] *...]
    all_to_all x4 -> x0, local copies, waits for them, and re-layouts: 15.6 us -> none  [the longest x2 7.82 us: on_device(): lax.all_to_all(jnp.stack(inverse_imag), 'seq', split_axis=1, concat_axis=...]
    dot_general x4 -> x0, local copies, waits for them, and re-layouts: 10.3 us -> none  [the longest x1 2.61 us: on_device(): jnp.einsum('kp,prc->krc', cosine_table, exchanged[0], precision=HIGHEST)]
  transfers between devices with their start and end apart: 10 -> 2, of which waited for: 6 -> 2; matrix products, arithmetic and copies ran while one was open for 35% -> 4% of each run, Pallas kernels for 0% -> 0%
where the time goes in v1:
time: 133 us; the launch traced here: 132 us
  blocking collectives  72.3 us (54%)
  Pallas kernels  23.9 us (18%)
  between operations  14.1 us (11%)
  waiting for transfers between devices  9.62 us (7%)
  local copies, waits for them, and re-layouts  8.69 us (7%)
  starting transfers between devices  3.61 us (3%)
    all_to_all x1, blocking collectives, on_device(): lax.all_to_all(out_weight.reshape(channels, members, features // members)...  48.6 us
    all_to_all x1, blocking collectives, on_device(): lax.all_to_all(packed, 'seq', split_axis=0, concat_axis=0, tiled=True)  23.7 us
    all_to_all x1, waiting for transfers between devices, on_device(): lax.all_to_all(convolve(data), 'seq', split_axis=0, concat_axis=0, tiled=...  8.96 us
    pallas_call x1, Pallas kernels, convolve(): pl.pallas_call(functools.partial(conv_kernel, group), in_specs=[space] *...  8.51 us
    unnamed x17, local copies, waits for them, and re-layouts  6.28 us
    pallas_call x1, Pallas kernels, pack(): pl.pallas_call(pack_kernel, grid=(rows // TILE,), in_specs=[block] * 3, o...  5.94 us
    pallas_call x1, Pallas kernels, mix(): pl.pallas_call(mix_kernel, grid=(rows // TILE,), in_specs=[pl.BlockSpec(m...  5.6 us
    pallas_call x1, Pallas kernels, project(): pl.pallas_call(project_kernel, grid=(rows // tile,), in_specs=[pl.BlockSp...  3.84 us
  transfers between devices with their start and end apart: 2, of which 2 were waited for; matrix products, arithmetic and copies ran while one was open for 4% of the time, Pallas kernels for 0%

profile of v1, /device:TPU:1, one launch (start us, length us, event | category | flops | bytes accessed | tf_op | source)
XLA Modules:
  0.0 132.2 jit_solution(17150419870209527465)
XLA Ops:
  6.5 0.0 copy-start.1
  6.5 0.0 copy-start.2
  6.6 0.0 copy-start.6
  6.6 5.9 %pack.1 = bf16[16,2,8,16,128]{4,3,2,1,0:T(8,128)(2,1)} custom-call(bf16[1024,256]{1,0:T(8,128)(2,1)} %gate_in.3, bf16[1024,256]{1,0:T(8,128)(2,1)} %value_in.3, f32[1024,256]{1,0:T(8,128)} %taps.1), custom_call_target="tpu_custom_call" | custom-call | tf_op jit(solution)/shard_map/pack/pallas_call | solution.py:66
  12.5 23.7 %all_to_all.15.data = bf16[16,2,8,16,128]{4,3,2,1,0:T(8,128)(2,1)S(1)} all-to-all(bf16[16,2,8,16,128]{4,3,2,1,0:T(8,128)(2,1)} %pack.1), channel_id=1, replica_groups=mesh['seq'=16,'chan'=8] {'seq'}, dimensions={0} | all-to-all | bytes 2097152 | tf_op jit(solution)/shard_map/all_to_all | solution.py:207
  36.2 0.0 copy-done.1
  36.2 0.0 copy-done.2
  36.2 0.0 copy-done.3
  36.2 0.0 copy-done.4
  36.2 0.0 copy-done.5
  36.2 0.0 copy-done.6
  36.3 8.5 %convolve.1 = bf16[16,8,16,128]{3,2,1,0:T(8,128)(2,1)} custom-call(bf16[16,2,8,16,128]{4,3,2,1,0:T(8,128)(2,1)S(1)} %all_to_all.15.data, bf16[256,256]{1,0:T(8,128)(2,1)S(1)} %copy-done.4, bf16[768,256]{1,0:T(8,128)(2,1)S(1)} %copy-done.1, bf16[768,256]{1,0:T(8,128)(2,1)S(1)} %copy-done.2, bf16[128,768]{1,0:T(8,128)(2,1)S(1)} %copy-done.3, ...), custom_call_target="tpu_custom_call" | custom-call | tf_op jit(solution)/shard_map/convolve/pallas_call | solution.py:131
  44.8 3.6 %all-to-all-start.1 = ((bf16[16,8,16,128]{3,2,1,0:T(8,128)(2,1)}), bf16[16,8,16,128]{3,2,1,0:T(8,128)(2,1)S(1)}, u32[]{:S(2)}, u32[]{:S(2)}) async-start(bf16[16,8,16,128]{3,2,1,0:T(8,128)(2,1)} %convolve.1), calls=%async_computation.1 | async-start | bytes 1048576 | tf_op jit(solution)/shard_map/all_to_all | solution.py:208
  48.4 0.0 all-gather.3.cloned.1.call-start
  49.0 9.0 %all-to-all-done.1.conv = bf16[16,8,16,128]{3,2,1,0:T(8,128)(2,1)S(1)} async-done(((bf16[16,8,16,128]{3,2,1,0:T(8,128)(2,1)}), bf16[16,8,16,128]{3,2,1,0:T(8,128)(2,1)S(1)}, u32[]{:S(2)}, u32[]{:S(2)}) %all-to-all-start.1) | async-done | bytes 524320 | tf_op jit(solution)/shard_map/all_to_all | solution.py:208
  58.0 0.8 copy-done.7
  58.8 5.6 %mix.1 = bf16[1024,256]{1,0:T(8,128)(2,1)} custom-call(s32[1]{0:T(128)S(6)} %copy.16.start, bf16[16,8,16,128]{3,2,1,0:T(8,128)(2,1)} %copy-done.7, bf16[1024,256]{1,0:T(8,128)(2,1)} %gate_out.1, bf16[1024,256]{1,0:T(8,128)(2,1)} %gate_in.3, bf16[1024,256]{1,0:T(8,128)(2,1)} %value_in.3, f32[1,256]{1,0:T(1,128)} %bitcast.7), custom_call_target="tpu_custom_call" | custom-call | tf_op jit(solution)/shard_map/mix/pallas_call | solution.py:155
  64.4 0.0 all-gather.3.cloned.1.call-update
  64.4 3.3 %copy.14 = bf16[256,4096]{0,1:T(8,128)(2,1)S(1)} copy(bf16[256,4096]{1,0:T(8,128)(2,1)} %param.19) | data formatting | bytes 4194304 | tf_op args[6]
  67.7 2.4 %copy.15 = bf16[256,8,512]{2,0,1:T(8,128)(2,1)} copy(bf16[256,8,512]{0,2,1:T(8,128)(2,1)S(1)} %bitcast.6) | data formatting | bytes 4194304 | tf_op jit(solution)/shard_map/reshape | solution.py:200
  70.1 48.6 %all_to_all.16.weight = bf16[8,256,512]{2,1,0:T(8,128)(2,1)S(1)} all-to-all(bf16[8,256,512]{2,1,0:T(8,128)(2,1)} %bitcast.5), channel_id=1, replica_groups=mesh['seq'=16,'chan'=8] {'chan'}, dimensions={0} | all-to-all | bytes 4194304 | tf_op jit(solution)/shard_map/all_to_all | solution.py:199
  118.7 0.6 all-gather.3.cloned.1.call-done
  119.4 2.2 %copy-done = bf16[8192,256]{1,0:T(8,128)(2,1)S(1)} copy-done((bf16[8192,256]{1,0:T(8,128)(2,1)S(1)}, bf16[8192,256]{1,0:T(8,128)(2,1)}, u32[]{:S(2)}) %copy-start) | copy-done | bytes 4194328
  121.5 3.8 %project.1 = bf16[1024,512]{1,0:T(8,128)(2,1)} custom-call(bf16[8,1024,256]{2,1,0:T(8,128)(2,1)S(1)} %bitcast.4, bf16[8,256,512]{2,1,0:T(8,128)(2,1)S(1)} %all_to_all.16.weight), custom_call_target="tpu_custom_call" | custom-call | tf_op jit(solution)/shard_map/project/pallas_call | solution.py:182
  (5 shorter events, 0.0 us)
Async XLA Ops:
  6.5 29.7 %copy-start.1 = (bf16[768,256]{1,0:T(8,128)(2,1)S(1)}, bf16[768,256]{1,0:T(8,128)(2,1)}, u32[]{:S(2)}) copy-start(bf16[768,256]{1,0:T(8,128)(2,1)} %constant.13.clone.second) | copy-start | bytes 1179652
  6.5 29.7 %copy-start.2 = (bf16[768,256]{1,0:T(8,128)(2,1)S(1)}, bf16[768,256]{1,0:T(8,128)(2,1)}, u32[]{:S(2)}) copy-start(bf16[768,256]{1,0:T(8,128)(2,1)} %constant.14.clone.back) | copy-start | bytes 1179652
  6.5 29.7 %copy-start.3 = (bf16[128,768]{1,0:T(8,128)(2,1)S(1)}, bf16[128,768]{1,0:T(8,128)(2,1)}, u32[]{:S(2)}) copy-start(bf16[128,768]{1,0:T(8,128)(2,1)} %constant.15.clone.last) | copy-start | bytes 589828
  6.5 29.7 %copy-start.4 = (bf16[256,256]{1,0:T(8,128)(2,1)S(1)}, bf16[256,256]{1,0:T(8,128)(2,1)}, u32[]{:S(2)}) copy-start(bf16[256,256]{1,0:T(8,128)(2,1)} %constant.12.clone.first) | copy-start | bytes 393220
  6.5 29.7 %copy-start.5 = (f32[128,128]{1,0:T(8,128)S(1)}, f32[128,128]{1,0:T(8,128)}, u32[]{:S(2)}) copy-start(f32[128,128]{1,0:T(8,128)} %constant.16.clone.cosine) | copy-start | bytes 196612
  6.6 29.7 %copy-start.6 = (f32[128,128]{1,0:T(8,128)S(1)}, f32[128,128]{1,0:T(8,128)}, u32[]{:S(2)}) copy-start(f32[128,128]{1,0:T(8,128)} %constant.17.clone.sine) | copy-start | bytes 196612
  44.8 13.2 %all-to-all-start.1 = ((bf16[16,8,16,128]{3,2,1,0:T(8,128)(2,1)}), bf16[16,8,16,128]{3,2,1,0:T(8,128)(2,1)S(1)}, u32[]{:S(2)}, u32[]{:S(2)}) async-start(bf16[16,8,16,128]{3,2,1,0:T(8,128)(2,1)} %convolve.1), calls=%async_computation.1 | async-start | bytes 1048576 | tf_op jit(solution)/shard_map/all_to_all | solution.py:208
  48.4 71.0 %all-gather.3.cloned.1.call-start = ((), (), s32[]{:S(2)}) async-start(), calls=%async_computation.3 | async-start | bytes 4718592 | tf_op jit(solution)/shard_map/all_gather | solution.py:210
  58.0 0.8 copy-start.7
  119.4 2.2 %copy-start = (bf16[8192,256]{1,0:T(8,128)(2,1)S(1)}, bf16[8192,256]{1,0:T(8,128)(2,1)}, u32[]{:S(2)}) copy-start(bf16[8192,256]{1,0:T(8,128)(2,1)} %all-gather.3.cloned.1.call-done) | copy-start | bytes 12582916
Sparse Core Ops, SparseCore 0:
  64.6 54.7 all-gather.2

commit v2 on v1

v2 whole, which is shorter than its diff:
```python
import functools
import math

import jax
import jax.numpy as jnp
import numpy as np
from jax import lax
from jax.experimental import pallas as pl
from jax.experimental.pallas import tpu as pltpu
from jax.sharding import PartitionSpec as P

BF16 = jnp.bfloat16
F32 = jnp.float32
TILE = 128
LENGTH = TILE * TILE


def split_table(table):
    high = table.astype(jnp.bfloat16)
    low = (table - high.astype(np.float64)).astype(jnp.bfloat16)
    return high, low


@functools.lru_cache(None)
def tables():
    index = np.arange(TILE, dtype=np.float64)
    outer = 2 * math.pi * np.outer(4 * index + 1, index)
    turn = outer / 512
    first = np.concatenate([np.cos(turn), -np.sin(turn)], 0)
    first_high, first_low = split_table(first)
    last_high, last_low = split_table(first.T / LENGTH)
    twist = outer / (4 * LENGTH)
    angle = 2 * math.pi * np.outer(index, index) / TILE
    cosine, sine = np.cos(angle), np.sin(angle)
    second = np.block([[cosine, -sine], [sine, cosine]])
    second_high, second_low = split_table(second)
    back_high, back_low = split_table(second.T)
    turns = np.concatenate(
        [
            np.concatenate([first_high, first_low], 1),
            second_high,
            second_high,
            second_low,
            back_high,
            back_high,
            back_low,
            last_high,
            last_high,
            last_low,
        ],
        0,
    )
    twists = np.concatenate([np.cos(twist), np.sin(twist)], 0).astype(np.float32)
    return turns, twists


def halves(array):
    high = array.astype(BF16)
    return high, (array - high.astype(F32)).astype(BF16)


def matmul(left, right):
    return jnp.dot(left, right, preferred_element_type=F32)


def pack_kernel(gate_in, value_in, taps, out):
    for b in range(out.shape[2]):
        rows = slice(b * TILE, (b + 1) * TILE)
        signal = gate_in[rows].astype(F32) * value_in[rows].astype(F32)
        out[:, 0, b] = signal.astype(BF16).T.reshape(16, 16, TILE)
        out[:, 1, b] = taps[rows].astype(BF16).T.reshape(16, 16, TILE)


def pack(gate_in, value_in, taps, blocks=4):
    rows, channels = value_in.shape
    block = pl.BlockSpec((blocks * TILE, channels), lambda b: (b, 0))
    return pl.pallas_call(
        pack_kernel,
        grid=(rows // (blocks * TILE),),
        in_specs=[block] * 3,
        out_specs=pl.BlockSpec((16, 2, blocks, 16, TILE), lambda b: (0, 0, b, 0, 0)),
        out_shape=jax.ShapeDtypeStruct((16, 2, rows // TILE, 16, TILE), BF16),
        name="pack",
    )(gate_in, value_in, taps)


def conv_kernel(group, data, turns, twists, out, signal, taps, total):
    shards, _, blocks, channels, _ = data.shape
    rows = blocks * channels
    span = 2 * TILE
    first, second, back = turns.at[:span], turns.at[span : 4 * span], turns.at[4 * span : 7 * span]
    cosine, sine = twists.at[:TILE], twists.at[TILE:]
    last = [turns[7 * span + k * TILE : 7 * span + (k + 1) * TILE, :] for k in range(3)]

    @pl.loop(0, shards)
    def _(a):
        part = pl.ds(pl.multiple_of(a * rows, rows), rows)
        signal[part, :] = data[a, 0].astype(F32).reshape(rows, TILE)
        taps[part, :] = data[a, 1].astype(F32).reshape(rows, TILE)

    @pl.loop(0, channels // group)
    def _(step):
        cos, sin = cosine[...], sine[...]
        picks = [pl.ds(step * group + g, TILE, stride=channels) for g in range(group)]
        pieces = []
        for pick in picks:
            pair = jnp.concatenate([signal[pick, :], taps[pick, :]], 1).astype(BF16)
            lifted = matmul(first[...], jnp.concatenate([pair, pair], 0))
            for side in range(2):
                real = lifted[:TILE, side * TILE : (side + 1) * TILE]
                imag = lifted[TILE:, side * TILE : (side + 1) * TILE]
                turned = jnp.concatenate([real * cos + imag * sin, imag * cos - real * sin], 1)
                high, low = halves(turned)
                pieces.append(jnp.concatenate([high, low, high], 1))
        spectra = matmul(jnp.concatenate(pieces, 0), second[...])
        pieces = []
        for g in range(group):
            left = spectra[2 * g * TILE : (2 * g + 1) * TILE]
            right = spectra[(2 * g + 1) * TILE : (2 * g + 2) * TILE]
            real = left[:, :TILE] * right[:, :TILE] - left[:, TILE:] * right[:, TILE:]
            imag = left[:, :TILE] * right[:, TILE:] + left[:, TILE:] * right[:, :TILE]
            high, low = halves(jnp.concatenate([real, imag], 1))
            pieces.append(jnp.concatenate([high, low, high], 1))
        restored = matmul(jnp.concatenate(pieces, 0), back[...])
        pieces = []
        for g in range(group):
            real = restored[g * TILE : (g + 1) * TILE, :TILE]
            imag = restored[g * TILE : (g + 1) * TILE, TILE:]
            turned = jnp.concatenate([real * cos - imag * sin, imag * cos + real * sin], 0)
            high, low = halves(turned)
            pieces.append(jnp.concatenate([high, low, high], 0))
        result = matmul(jnp.concatenate(last, 1), jnp.concatenate(pieces, 1))
        for g, pick in enumerate(picks):
            total[pick, :] = result[:, g * TILE : (g + 1) * TILE]

    @pl.loop(0, shards)
    def _(a):
        part = pl.ds(pl.multiple_of(a * rows, rows), rows)
        out[a] = total[part, :].astype(BF16).reshape(blocks, channels, TILE)


def convolve(data, group=8):
    shards, _, blocks, channels, _ = data.shape
    whole = pltpu.VMEM((shards * blocks * channels, TILE), F32)
    space = pl.BlockSpec(memory_space=pltpu.VMEM)
    return pl.pallas_call(
        functools.partial(conv_kernel, group),
        in_specs=[space] * 3,
        out_specs=space,
        out_shape=jax.ShapeDtypeStruct((shards, blocks, channels, TILE), BF16),
        scratch_shapes=[whole] * 3,
        compiler_params=pltpu.CompilerParams(vmem_limit_bytes=28 << 20),
        cost_estimate=pl.CostEstimate(flops=10**10, bytes_accessed=1 << 22, transcendentals=0),
        name="convolve",
    )(data, *(jnp.asarray(table) for table in tables()))


def mix_kernel(start, conv, gate_out, gate_in, value_in, skip, _, top, low):
    rows = gate_out.shape[0]
    step = pl.program_id(0)
    shard = lax.axis_index("seq") * (rows * pl.num_programs(0))

    def fill(out):
        for b in range(rows // TILE):
            part = slice(b * TILE, (b + 1) * TILE)
            first = shard + step * rows + b * TILE
            position = first + lax.broadcasted_iota(jnp.int32, (TILE, 1), 0)
            signal = gate_in[part].astype(F32) * value_in[part].astype(F32)
            convolved = conv[:, b].reshape(-1, TILE).T.astype(F32)
            mixed = gate_out[part].astype(F32) * (convolved + skip[...] * signal)
            out[part] = jnp.where(position >= start[0], mixed, 0.0).astype(BF16)

    @pl.when(step == 0)
    def _():
        fill(top)

    @pl.when(step == 1)
    def _():
        fill(low)


def mix(resume_at, conv, gate_out, gate_in, value_in, skip_bias, after):
    rows, channels = value_in.shape
    half = rows // 2
    block = pl.BlockSpec((half, channels), lambda i: (i, 0))
    kept = pl.BlockSpec((half, channels), lambda i: (0, 0))
    return pl.pallas_call(
        mix_kernel,
        grid=(2,),
        in_specs=[
            pl.BlockSpec(memory_space=pltpu.SMEM),
            pl.BlockSpec((16, half // TILE, 16, TILE), lambda i: (0, i, 0, 0)),
            block,
            block,
            block,
            pl.BlockSpec((1, channels), lambda i: (0, 0)),
            pl.BlockSpec(memory_space=pl.ANY),
        ],
        out_specs=[kept] * 2,
        out_shape=[jax.ShapeDtypeStruct((half, channels), BF16)] * 2,
        compiler_params=pltpu.CompilerParams(vmem_limit_bytes=12 << 20),
        name="mix",
    )(resume_at, conv, gate_out, gate_in, value_in, skip_bias[None, :], after)


def toward(array, step, swap):
    pairs = [(z * 2 + c, (z + step) % 4 * 2 + (c ^ swap)) for z in range(4) for c in range(2)]
    return lax.ppermute(array, "chan", pairs)


ROUTES = tuple((step, swap) for step in range(4) for swap in range(2))


def split_kernel(weight, _, *outs):
    me = lax.axis_index("chan")
    features = outs[0].shape[1]
    core = lax.rem(me, 2)
    for out, (step, swap) in zip(outs, ROUTES):
        target = lax.rem(me // 2 + step, 4) * 2 + (1 - core if swap else core)
        out[...] = weight[:, pl.ds(pl.multiple_of(target * features, features), features)]


def split_weight(weight, after, tile=128):
    channels, features = weight.shape
    members = len(ROUTES)
    width = features // members
    return pl.pallas_call(
        split_kernel,
        grid=(channels // tile,),
        in_specs=[
            pl.BlockSpec((tile, features), lambda i: (i, 0)),
            pl.BlockSpec(memory_space=pl.ANY),
        ],
        out_specs=[pl.BlockSpec((tile, width), lambda i: (i, 0))] * members,
        out_shape=[jax.ShapeDtypeStruct((channels, width), BF16)] * members,
        name="split_weight",
    )(weight, after)


def mark_kernel(*refs):
    refs[-1][...] = jnp.zeros_like(refs[-1])


def mark(arrays):
    return pl.pallas_call(
        mark_kernel,
        in_specs=[pl.BlockSpec(memory_space=pl.ANY)] * len(arrays),
        out_shape=jax.ShapeDtypeStruct((8, TILE), F32),
        cost_estimate=pl.CostEstimate(flops=10**10, bytes_accessed=0, transcendentals=0),
        name="mark",
    )(*arrays)


def tie_kernel(count, *refs):
    for source, target in zip(refs[:count], refs[-count:]):
        target[...] = source[...]


def tie(arrays, after):
    space = pl.BlockSpec(memory_space=pltpu.VMEM)
    count = len(arrays)
    return pl.pallas_call(
        functools.partial(tie_kernel, count),
        in_specs=[space] * count + [pl.BlockSpec(memory_space=pl.ANY)] * len(after),
        out_specs=[space] * count,
        out_shape=[jax.ShapeDtypeStruct(array.shape, array.dtype) for array in arrays],
        input_output_aliases={k: k for k in range(count)},
        compiler_params=pltpu.CompilerParams(vmem_limit_bytes=12 << 20),
        name="tie",
    )(*arrays, *after)


def project_kernel(*refs):
    mixed, weight, out = refs[:16], refs[16:24], refs[24]

    def fill(pieces):
        total = matmul(pieces[0][...], weight[0][...])
        for piece, part in zip(pieces[1:], weight[1:]):
            total = total + matmul(piece[...], part[...])
        out[...] = total.astype(BF16)

    for half in range(2):
        pl.when(pl.program_id(0) == half)(
            functools.partial(fill, mixed[8 * half : 8 * half + 8])
        )


def project(top, low, weight):
    rows = top[0].shape[0]
    features = weight[0].shape[1]
    return pl.pallas_call(
        project_kernel,
        grid=(2,),
        in_specs=[pl.BlockSpec(memory_space=pltpu.VMEM)] * 24,
        out_specs=pl.BlockSpec((rows, features), lambda i: (i, 0)),
        out_shape=jax.ShapeDtypeStruct((2 * rows, features), BF16),
        compiler_params=pltpu.CompilerParams(vmem_limit_bytes=16 << 20),
        name="project",
    )(*top, *low, *weight)


def on_device(gate_out, gate_in, value_in, filter_taps, skip_bias, resume_at, out_weight):
    packed = pack(gate_in, value_in, filter_taps)
    data = lax.all_to_all(packed, "seq", split_axis=0, concat_axis=0, tiled=True)
    weight = split_weight(out_weight, packed)
    weight = [toward(w, *route) if any(route) else w for w, route in zip(weight, ROUTES)]
    conv = lax.all_to_all(convolve(data), "seq", split_axis=0, concat_axis=0, tiled=True)
    top, low = mix(resume_at, conv, gate_out, gate_in, value_in, skip_bias, mark(weight))
    up_top, down_low = toward(top, 1, 0), toward(low, 3, 0)
    up_low, down_top = toward(low, 1, 0), toward(top, 3, 0)
    far_top, far_low = toward(up_top, 1, 0), toward(down_low, 3, 0)
    up_top_other, down_low_other = toward(up_top, 0, 1), toward(down_low, 0, 1)
    up_low, down_top = tie([up_low, down_top], [up_top_other, down_low_other])
    tops = [top, toward(top, 0, 1), up_top, up_top_other, far_top, toward(far_top, 0, 1)]
    tops += [down_top, toward(down_top, 0, 1)]
    lows = [low, toward(low, 0, 1), up_low, toward(up_low, 0, 1), far_low, toward(far_low, 0, 1)]
    lows += [down_low, down_low_other]
    return project(tops, lows, weight)


def solution(mesh):
    placed = (
        P("seq", "chan"),
        P("seq", "chan"),
        P("seq", "chan"),
        P("seq", "chan"),
        P("chan"),
        P(),
        P("chan", None),
    )
    return jax.shard_map(
        on_device, mesh=mesh, in_specs=placed, out_specs=P("seq", "chan"), check_vma=False
    )
```

time: 133 us -> 85.2 us (0.64)
  blocking collectives: 72.3 us -> 0 us
  starting transfers between devices: 3.61 us -> 40.9 us
  between operations: 14.1 us -> 0.95 us
  waiting for transfers between devices: 9.62 us -> 21.7 us
  Pallas kernels: 23.9 us -> 17.6 us
  local copies, waits for them, and re-layouts: 8.69 us -> 3.55 us
    all_to_all x2 -> x0, blocking collectives: 72.3 us -> none  [the longest x1 48.6 us: on_device(): lax.all_to_all(out_weight.reshape(channels, members, features // members)...]
    ppermute x0 -> x21, starting transfers between devices: none -> 26.4 us  [toward(): return lax.ppermute(array, 'chan', pairs)]
    ppermute x0 -> x21, waiting for transfers between devices: none -> 11.7 us  [toward(): return lax.ppermute(array, 'chan', pairs)]
    all_to_all x0 -> x1, starting transfers between devices: none -> 7.58 us  [on_device(): lax.all_to_all(packed, 'seq', split_axis=0, concat_axis=0, tiled=True)]
    pallas_call x3 -> x6, Pallas kernels: 15.4 us -> 9.78 us  [the longest x1 3.36 us: project(): pl.pallas_call(project_kernel, grid=(2,), in_specs=[pl.BlockSpec(memory_s...]
    all_to_all x1, starting transfers between devices: 3.57 us -> 6.94 us  [on_device(): lax.all_to_all(convolve(data), 'seq', split_axis=0, concat_axis=0, tiled=...]
    unnamed x17 -> x44, local copies, waits for them, and re-layouts: 6.28 us -> 3.55 us
    reshape x1 -> x0, local copies, waits for them, and re-layouts: 2.41 us -> none  [on_device(): out_weight.reshape(channels, members, features // members).swapaxes(0, 1)]
  transfers between devices with their start and end apart: 2 -> 23, of which waited for: 2 -> 7; matrix products, arithmetic and copies ran while one was open for 4% -> 0% of each run, Pallas kernels for 0% -> 13%
where the time goes in v2:
time: 85.2 us; the launch traced here: 84.8 us
  starting transfers between devices  40.9 us (48%)
  waiting for transfers between devices  21.7 us (25%)
  Pallas kernels  17.6 us (21%)
  local copies, waits for them, and re-layouts  3.55 us (4%)
  between operations  0.95 us (1%)
    ppermute x21, starting transfers between devices, toward(): return lax.ppermute(array, 'chan', pairs)  26.4 us
    ppermute x21, waiting for transfers between devices, toward(): return lax.ppermute(array, 'chan', pairs)  11.7 us
    all_to_all x1, waiting for transfers between devices, on_device(): lax.all_to_all(convolve(data), 'seq', split_axis=0, concat_axis=0, tiled=...  10 us
    pallas_call x1, Pallas kernels, convolve(): pl.pallas_call(functools.partial(conv_kernel, group), in_specs=[space] *...  7.84 us
    all_to_all x1, starting transfers between devices, on_device(): lax.all_to_all(packed, 'seq', split_axis=0, concat_axis=0, tiled=True)  7.58 us
    all_to_all x1, starting transfers between devices, on_device(): lax.all_to_all(convolve(data), 'seq', split_axis=0, concat_axis=0, tiled=...  6.94 us
    unnamed x44, local copies, waits for them, and re-layouts  3.55 us
    pallas_call x1, Pallas kernels, project(): pl.pallas_call(project_kernel, grid=(2,), in_specs=[pl.BlockSpec(memory_s...  3.36 us
  transfers between devices with their start and end apart: 23, of which 7 were waited for; matrix products, arithmetic and copies ran while one was open for 0% of the time, Pallas kernels for 13%

profile of v2, /device:TPU:1, one launch (start us, length us, event | category | flops | bytes accessed | tf_op | source)
XLA Modules:
  0.0 84.8 jit_solution(13036272387523679836)
XLA Ops:
  0.0 2.5 %pack.1._ = bf16[16,2,8,16,128]{4,3,2,1,0:T(8,128)(2,1)} custom-call(bf16[1024,256]{1,0:T(8,128)(2,1)} %gate_in.3, bf16[1024,256]{1,0:T(8,128)(2,1)} %value_in.3, f32[1024,256]{1,0:T(8,128)} %taps.1), custom_call_target="tpu_custom_call" | custom-call | tf_op jit(solution)/shard_map/pack/pallas_call | solution.py:77
  2.5 7.6 %all-to-all-start = ((bf16[16,2,8,16,128]{4,3,2,1,0:T(8,128)(2,1)}), bf16[16,2,8,16,128]{4,3,2,1,0:T(8,128)(2,1)S(1)}, u32[]{:S(2)}, u32[]{:S(2)}) async-start(bf16[16,2,8,16,128]{4,3,2,1,0:T(8,128)(2,1)} %pack.1._), calls=%async_computation | async-start | bytes 2097152 | tf_op jit(solution)/shard_map/all_to_all | solution.py:304
  10.1 2.7 %split_weight.1 = (bf16[256,512]{1,0:T(8,128)(2,1)}, bf16[256,512]{1,0:T(8,128)(2,1)}, bf16[256,512]{1,0:T(8,128)(2,1)}, bf16[256,512]{1,0:T(8,128)(2,1)}, bf16[...) custom-call(bf16[256,4096]{1,0:T(8,128)(2,1)} %weight.1, ...), custom_call_target="tpu_custom_call" | custom-call | tf_op jit(solution)/shard_map/split_weight/pallas_call | solution.py:227
  13.9 1.7 %collective-permute-start.1 = (bf16[256,512]{1,0:T(8,128)(2,1)}, bf16[256,512]{1,0:T(8,128)(2,1)S(1)}, u32[]{:S(2)}, u32[]{:S(2)}) collective-permute-start(bf16[256,512]{1,0:T(8,128)(2,1)} %get-tuple-element.19), channel_id=1, source_target_pairs={{0,2},{1,3},{2,4},{3,5},{4,6},{5,7},{6,0},{7,1},{8,10},{9,11},{10,... | collective-permute-start | bytes 786440 | tf_op jit(solution)/shard_map/ppermute | solution.py:208
  15.5 1.9 %collective-permute-start.2 = (bf16[256,512]{1,0:T(8,128)(2,1)}, bf16[256,512]{1,0:T(8,128)(2,1)S(1)}, u32[]{:S(2)}, u32[]{:S(2)}) collective-permute-start(bf16[256,512]{1,0:T(8,128)(2,1)} %get-tuple-element.20), channel_id=1, source_target_pairs={{0,3},{1,2},{2,5},{3,4},{4,7},{5,6},{6,1},{7,0},{8,11},{9,10},{10,... | collective-permute-start | bytes 786440 | tf_op jit(solution)/shard_map/ppermute | solution.py:208
  17.4 1.5 %collective-permute-start.3 = (bf16[256,512]{1,0:T(8,128)(2,1)}, bf16[256,512]{1,0:T(8,128)(2,1)S(1)}, u32[]{:S(2)}, u32[]{:S(2)}) collective-permute-start(bf16[256,512]{1,0:T(8,128)(2,1)} %get-tuple-element.21), channel_id=1, source_target_pairs={{0,4},{1,5},{2,6},{3,7},{4,0},{5,1},{6,2},{7,3},{8,12},{9,13},{10,... | collective-permute-start | bytes 786440 | tf_op jit(solution)/shard_map/ppermute | solution.py:208
  18.9 1.8 %collective-permute-start.4 = (bf16[256,512]{1,0:T(8,128)(2,1)}, bf16[256,512]{1,0:T(8,128)(2,1)S(1)}, u32[]{:S(2)}, u32[]{:S(2)}) collective-permute-start(bf16[256,512]{1,0:T(8,128)(2,1)} %get-tuple-element.22), channel_id=1, source_target_pairs={{0,5},{1,4},{2,7},{3,6},{4,1},{5,0},{6,3},{7,2},{8,13},{9,12},{10,... | collective-permute-start | bytes 786440 | tf_op jit(solution)/shard_map/ppermute | solution.py:208
  22.5 2.0 %collective-permute-done.1.refs_2_.refs_18_ = bf16[256,512]{1,0:T(8,128)(2,1)S(1)} collective-permute-done((bf16[256,512]{1,0:T(8,128)(2,1)}, bf16[256,512]{1,0:T(8,128)(2,1)S(1)}, u32[]{:S(2)}, u32[]{:S(2)}) %collective-permute-start.1) | collective-permute-done | bytes 262176 | tf_op jit(solution)/shard_map/ppermute | solution.py:208
  24.4 2.5 %collective-permute-start.6 = (bf16[256,512]{1,0:T(8,128)(2,1)}, bf16[256,512]{1,0:T(8,128)(2,1)S(1)}, u32[]{:S(2)}, u32[]{:S(2)}) collective-permute-start(bf16[256,512]{1,0:T(8,128)(2,1)} %get-tuple-element.24), channel_id=1, source_target_pairs={{0,7},{1,6},{2,1},{3,0},{4,3},{5,2},{6,5},{7,4},{8,15},{9,14},{10,... | collective-permute-start | bytes 786440 | tf_op jit(solution)/shard_map/ppermute | solution.py:208
  26.9 1.2 %copy-done.20 = bf16[2176,256]{1,0:T(8,128)(2,1)S(1)} copy-done((bf16[2176,256]{1,0:T(8,128)(2,1)S(1)}, bf16[2176,256]{1,0:T(8,128)(2,1)}, u32[]{:S(2)}) %copy-start.20) | copy-done | bytes 1114136
  28.2 7.8 %convolve.1 = bf16[16,8,16,128]{3,2,1,0:T(8,128)(2,1)} custom-call(bf16[16,2,8,16,128]{4,3,2,1,0:T(8,128)(2,1)S(1)} %all-to-all-done.data, bf16[2176,256]{1,0:T(8,128)(2,1)S(1)} %copy-done.20, f32[256,128]{1,0:T(8,128)S(1)} %copy-done.21), custom_call_target="tpu_custom_call" | custom-call | flops 10000000000 | bytes 4194304 | tf_op jit(solution)/shard_map/convolve/pallas_call | solution.py:146
  36.0 6.9 %all-to-all-start.1 = ((bf16[16,8,16,128]{3,2,1,0:T(8,128)(2,1)}), bf16[16,8,16,128]{3,2,1,0:T(8,128)(2,1)S(1)}, u32[]{:S(2)}, u32[]{:S(2)}) async-start(bf16[16,8,16,128]{3,2,1,0:T(8,128)(2,1)} %convolve.1), calls=%async_computation.1 | async-start | bytes 1048576 | tf_op jit(solution)/shard_map/all_to_all | solution.py:307
  45.2 10.0 %all-to-all-done.1.conv = bf16[16,8,16,128]{3,2,1,0:T(8,128)(2,1)S(1)} async-done(((bf16[16,8,16,128]{3,2,1,0:T(8,128)(2,1)}), bf16[16,8,16,128]{3,2,1,0:T(8,128)(2,1)S(1)}, u32[]{:S(2)}, u32[]{:S(2)}) %all-to-all-start.1) | async-done | bytes 524320 | tf_op jit(solution)/shard_map/all_to_all | solution.py:307
  56.6 2.7 %collective-permute-start.14 = (bf16[512,256]{1,0:T(8,128)(2,1)S(1)}, bf16[512,256]{1,0:T(8,128)(2,1)S(1)}, u32[]{:S(2)}, u32[]{:S(2)}) collective-permute-start(bf16[512,256]{1,0:T(8,128)(2,1)S(1)} %get-tuple-element.26.refs_8_), channel_id=1, source_target_pairs={{0,6},{1,7},{2,0},{3,1},{4,2},{5,3},{6,4},{7,5},{8,14},{9,15},{10,... | collective-permute-start | bytes 786440 | tf_op jit(solution)/shard_map/ppermute | solution.py:208
  59.3 1.4 %collective-permute-start.12 = (bf16[512,256]{1,0:T(8,128)(2,1)S(1)}, bf16[512,256]{1,0:T(8,128)(2,1)S(1)}, u32[]{:S(2)}, u32[]{:S(2)}) collective-permute-start(bf16[512,256]{1,0:T(8,128)(2,1)S(1)} %get-tuple-element.26.refs_8_), channel_id=1, source_target_pairs={{0,2},{1,3},{2,4},{3,5},{4,6},{5,7},{6,0},{7,1},{8,10},{9,11},{10,... | collective-permute-start | bytes 786440 | tf_op jit(solution)/shard_map/ppermute | solution.py:208
  60.8 4.6 %collective-permute-done.8.refs_2_ = bf16[512,256]{1,0:T(8,128)(2,1)S(1)} collective-permute-done((bf16[512,256]{1,0:T(8,128)(2,1)S(1)}, bf16[512,256]{1,0:T(8,128)(2,1)S(1)}, u32[]{:S(2)}, u32[]{:S(2)}) %collective-permute-start.8) | collective-permute-done | bytes 262176 | tf_op jit(solution)/shard_map/ppermute | solution.py:208
  65.3 2.1 %collective-permute-start.9 = (bf16[512,256]{1,0:T(8,128)(2,1)S(1)}, bf16[512,256]{1,0:T(8,128)(2,1)S(1)}, u32[]{:S(2)}, u32[]{:S(2)}) collective-permute-start(bf16[512,256]{1,0:T(8,128)(2,1)S(1)} %collective-permute-done.8.refs_2_), channel_id=1, source_target_pairs={{0,1},{1,0},{2,3},{3,2},{4,5},{5,4},{6,7},{7,6},{8,9},{9,8},{10,11... | collective-permute-start | bytes 786440 | tf_op jit(solution)/shard_map/ppermute | solution.py:208
  67.4 2.5 %collective-permute-done.13.refs_1_ = bf16[512,256]{1,0:T(8,128)(2,1)S(1)} collective-permute-done((bf16[512,256]{1,0:T(8,128)(2,1)S(1)}, bf16[512,256]{1,0:T(8,128)(2,1)S(1)}, u32[]{:S(2)}, u32[]{:S(2)}) %collective-permute-start.13) | collective-permute-done | bytes 262176 | tf_op jit(solution)/shard_map/ppermute | solution.py:208
  69.9 3.4 %collective-permute-start.19 = (bf16[512,256]{1,0:T(8,128)(2,1)S(1)}, bf16[512,256]{1,0:T(8,128)(2,1)S(1)}, u32[]{:S(2)}, u32[]{:S(2)}) collective-permute-start(bf16[512,256]{1,0:T(8,128)(2,1)S(1)} %collective-permute-done.14.refs_14_), channel_id=1, source_target_pairs={{0,6},{1,7},{2,0},{3,1},{4,2},{5,3},{6,4},{7,5},{8,14},{9,15},{10,... | collective-permute-start | bytes 786440 | tf_op jit(solution)/shard_map/ppermute | solution.py:208
  73.3 1.8 %collective-permute-start.7 = (bf16[512,256]{1,0:T(8,128)(2,1)S(1)}, bf16[512,256]{1,0:T(8,128)(2,1)S(1)}, u32[]{:S(2)}, u32[]{:S(2)}) collective-permute-start(bf16[512,256]{1,0:T(8,128)(2,1)S(1)} %get-tuple-element.25.refs_0_), channel_id=1, source_target_pairs={{0,1},{1,0},{2,3},{3,2},{4,5},{5,4},{6,7},{7,6},{8,9},{9,8},{10,11... | collective-permute-start | bytes 786440 | tf_op jit(solution)/shard_map/ppermute | solution.py:208
  75.8 1.1 %collective-permute-done.10.refs_4_ = bf16[512,256]{1,0:T(8,128)(2,1)S(1)} collective-permute-done((bf16[512,256]{1,0:T(8,128)(2,1)S(1)}, bf16[512,256]{1,0:T(8,128)(2,1)S(1)}, u32[]{:S(2)}, u32[]{:S(2)}) %collective-permute-start.10) | collective-permute-done | bytes 262176 | tf_op jit(solution)/shard_map/ppermute | solution.py:208
  77.8 2.0 %collective-permute-start.20 = (bf16[512,256]{1,0:T(8,128)(2,1)S(1)}, bf16[512,256]{1,0:T(8,128)(2,1)S(1)}, u32[]{:S(2)}, u32[]{:S(2)}) collective-permute-start(bf16[512,256]{1,0:T(8,128)(2,1)S(1)} %collective-permute-done.19.refs_12_), channel_id=1, source_target_pairs={{0,1},{1,0},{2,3},{3,2},{4,5},{5,4},{6,7},{7,6},{8,9},{9,8},{10,11... | collective-permute-start | bytes 786440 | tf_op jit(solution)/shard_map/ppermute | solution.py:208
  79.9 1.1 %collective-permute-done.20.refs_13_ = bf16[512,256]{1,0:T(8,128)(2,1)S(1)} collective-permute-done((bf16[512,256]{1,0:T(8,128)(2,1)S(1)}, bf16[512,256]{1,0:T(8,128)(2,1)S(1)}, u32[]{:S(2)}, u32[]{:S(2)}) %collective-permute-start.20) | collective-permute-done | bytes 262176 | tf_op jit(solution)/shard_map/ppermute | solution.py:208
  81.4 3.4 %project.1 = bf16[1024,512]{1,0:T(8,128)(2,1)} custom-call(bf16[512,256]{1,0:T(8,128)(2,1)S(1)} %get-tuple-element.25.refs_0_, bf16[512,256]{1,0:T(8,128)(2,1)S(1)} %collective-permute-done.7.refs_1_, bf16[512,256]{1,0:T(8,128)(2,1)S(1)} %collective-permute-done.8.refs_2_, bf16[512,256]{1,0:T(8,128)(2,1)S(1)} %collective-permute-done.9.refs_2_.refs_3_, ...), custom_call_target="tpu_custom_call" | custom-call | tf_op jit(solution)/shard_map/project/pallas_call | solution.py:291
  (73 shorter events, 7.6 us)
Async XLA Ops:
  2.5 24.4 %all-to-all-start = ((bf16[16,2,8,16,128]{4,3,2,1,0:T(8,128)(2,1)}), bf16[16,2,8,16,128]{4,3,2,1,0:T(8,128)(2,1)S(1)}, u32[]{:S(2)}, u32[]{:S(2)}) async-start(bf16[16,2,8,16,128]{4,3,2,1,0:T(8,128)(2,1)} %pack.1._), calls=%async_computation | async-start | bytes 2097152 | tf_op jit(solution)/shard_map/all_to_all | solution.py:304
  12.8 8.5 %collective-permute-start = (bf16[256,512]{1,0:T(8,128)(2,1)}, bf16[256,512]{1,0:T(8,128)(2,1)S(1)}, u32[]{:S(2)}, u32[]{:S(2)}) collective-permute-start(bf16[256,512]{1,0:T(8,128)(2,1)} %get-tuple-element.18), channel_id=1, source_target_pairs={{0,1},{1,0},{2,3},{3,2},{4,5},{5,4},{6,7},{7,6},{8,9},{9,8},{10,11... | collective-permute-start | bytes 786440 | tf_op jit(solution)/shard_map/ppermute | solution.py:208
  13.9 10.6 %collective-permute-start.1 = (bf16[256,512]{1,0:T(8,128)(2,1)}, bf16[256,512]{1,0:T(8,128)(2,1)S(1)}, u32[]{:S(2)}, u32[]{:S(2)}) collective-permute-start(bf16[256,512]{1,0:T(8,128)(2,1)} %get-tuple-element.19), channel_id=1, source_target_pairs={{0,2},{1,3},{2,4},{3,5},{4,6},{5,7},{6,0},{7,1},{8,10},{9,11},{10,... | collective-permute-start | bytes 786440 | tf_op jit(solution)/shard_map/ppermute | solution.py:208
  15.5 27.4 %collective-permute-start.2 = (bf16[256,512]{1,0:T(8,128)(2,1)}, bf16[256,512]{1,0:T(8,128)(2,1)S(1)}, u32[]{:S(2)}, u32[]{:S(2)}) collective-permute-start(bf16[256,512]{1,0:T(8,128)(2,1)} %get-tuple-element.20), channel_id=1, source_target_pairs={{0,3},{1,2},{2,5},{3,4},{4,7},{5,6},{6,1},{7,0},{8,11},{9,10},{10,... | collective-permute-start | bytes 786440 | tf_op jit(solution)/shard_map/ppermute | solution.py:208
  17.4 25.6 %collective-permute-start.3 = (bf16[256,512]{1,0:T(8,128)(2,1)}, bf16[256,512]{1,0:T(8,128)(2,1)S(1)}, u32[]{:S(2)}, u32[]{:S(2)}) collective-permute-start(bf16[256,512]{1,0:T(8,128)(2,1)} %get-tuple-element.21), channel_id=1, source_target_pairs={{0,4},{1,5},{2,6},{3,7},{4,0},{5,1},{6,2},{7,3},{8,12},{9,13},{10,... | collective-permute-start | bytes 786440 | tf_op jit(solution)/shard_map/ppermute | solution.py:208
  18.9 24.1 %collective-permute-start.4 = (bf16[256,512]{1,0:T(8,128)(2,1)}, bf16[256,512]{1,0:T(8,128)(2,1)S(1)}, u32[]{:S(2)}, u32[]{:S(2)}) collective-permute-start(bf16[256,512]{1,0:T(8,128)(2,1)} %get-tuple-element.22), channel_id=1, source_target_pairs={{0,5},{1,4},{2,7},{3,6},{4,1},{5,0},{6,3},{7,2},{8,13},{9,12},{10,... | collective-permute-start | bytes 786440 | tf_op jit(solution)/shard_map/ppermute | solution.py:208
  21.4 21.7 %collective-permute-start.5 = (bf16[256,512]{1,0:T(8,128)(2,1)}, bf16[256,512]{1,0:T(8,128)(2,1)S(1)}, u32[]{:S(2)}, u32[]{:S(2)}) collective-permute-start(bf16[256,512]{1,0:T(8,128)(2,1)} %get-tuple-element.23), channel_id=1, source_target_pairs={{0,6},{1,7},{2,0},{3,1},{4,2},{5,3},{6,4},{7,5},{8,14},{9,15},{10,... | collective-permute-start | bytes 786440 | tf_op jit(solution)/shard_map/ppermute | solution.py:208
  24.4 18.6 %collective-permute-start.6 = (bf16[256,512]{1,0:T(8,128)(2,1)}, bf16[256,512]{1,0:T(8,128)(2,1)S(1)}, u32[]{:S(2)}, u32[]{:S(2)}) collective-permute-start(bf16[256,512]{1,0:T(8,128)(2,1)} %get-tuple-element.24), channel_id=1, source_target_pairs={{0,7},{1,6},{2,1},{3,0},{4,3},{5,2},{6,5},{7,4},{8,15},{9,14},{10,... | collective-permute-start | bytes 786440 | tf_op jit(solution)/shard_map/ppermute | solution.py:208
  36.0 19.2 %all-to-all-start.1 = ((bf16[16,8,16,128]{3,2,1,0:T(8,128)(2,1)}), bf16[16,8,16,128]{3,2,1,0:T(8,128)(2,1)S(1)}, u32[]{:S(2)}, u32[]{:S(2)}) async-start(bf16[16,8,16,128]{3,2,1,0:T(8,128)(2,1)} %convolve.1), calls=%async_computation.1 | async-start | bytes 1048576 | tf_op jit(solution)/shard_map/all_to_all | solution.py:307
  45.2 36.2 %copy-start.11 = (bf16[256,512]{1,0:T(8,128)(2,1)S(1)}, bf16[256,512]{1,0:T(8,128)(2,1)}, u32[]{:S(2)}) copy-start(bf16[256,512]{1,0:T(8,128)(2,1)} %copy-done.10) | copy-start | bytes 786436
  56.6 8.8 %collective-permute-start.8 = (bf16[512,256]{1,0:T(8,128)(2,1)S(1)}, bf16[512,256]{1,0:T(8,128)(2,1)S(1)}, u32[]{:S(2)}, u32[]{:S(2)}) collective-permute-start(bf16[512,256]{1,0:T(8,128)(2,1)S(1)} %get-tuple-element.25.refs_0_), channel_id=1, source_target_pairs={{0,2},{1,3},{2,4},{3,5},{4,6},{5,7},{6,0},{7,1},{8,10},{9,11},{10,... | collective-permute-start | bytes 786440 | tf_op jit(solution)/shard_map/ppermute | solution.py:208
  56.6 10.8 %collective-permute-start.14 = (bf16[512,256]{1,0:T(8,128)(2,1)S(1)}, bf16[512,256]{1,0:T(8,128)(2,1)S(1)}, u32[]{:S(2)}, u32[]{:S(2)}) collective-permute-start(bf16[512,256]{1,0:T(8,128)(2,1)S(1)} %get-tuple-element.26.refs_8_), channel_id=1, source_target_pairs={{0,6},{1,7},{2,0},{3,1},{4,2},{5,3},{6,4},{7,5},{8,14},{9,15},{10,... | collective-permute-start | bytes 786440 | tf_op jit(solution)/shard_map/ppermute | solution.py:208
  59.3 10.6 %collective-permute-start.13 = (bf16[512,256]{1,0:T(8,128)(2,1)S(1)}, bf16[512,256]{1,0:T(8,128)(2,1)S(1)}, u32[]{:S(2)}, u32[]{:S(2)}) collective-permute-start(bf16[512,256]{1,0:T(8,128)(2,1)S(1)} %get-tuple-element.25.refs_0_), channel_id=1, source_target_pairs={{0,6},{1,7},{2,0},{3,1},{4,2},{5,3},{6,4},{7,5},{8,14},{9,15},{10,... | collective-permute-start | bytes 786440 | tf_op jit(solution)/shard_map/ppermute | solution.py:208
  59.3 14.0 %collective-permute-start.12 = (bf16[512,256]{1,0:T(8,128)(2,1)S(1)}, bf16[512,256]{1,0:T(8,128)(2,1)S(1)}, u32[]{:S(2)}, u32[]{:S(2)}) collective-permute-start(bf16[512,256]{1,0:T(8,128)(2,1)S(1)} %get-tuple-element.26.refs_8_), channel_id=1, source_target_pairs={{0,2},{1,3},{2,4},{3,5},{4,6},{5,7},{6,0},{7,1},{8,10},{9,11},{10,... | collective-permute-start | bytes 786440 | tf_op jit(solution)/shard_map/ppermute | solution.py:208
  65.3 9.8 %collective-permute-start.9 = (bf16[512,256]{1,0:T(8,128)(2,1)S(1)}, bf16[512,256]{1,0:T(8,128)(2,1)S(1)}, u32[]{:S(2)}, u32[]{:S(2)}) collective-permute-start(bf16[512,256]{1,0:T(8,128)(2,1)S(1)} %collective-permute-done.8.refs_2_), channel_id=1, source_target_pairs={{0,1},{1,0},{2,3},{3,2},{4,5},{5,4},{6,7},{7,6},{8,9},{9,8},{10,11... | collective-permute-start | bytes 786440 | tf_op jit(solution)/shard_map/ppermute | solution.py:208
  67.4 7.8 %collective-permute-start.15 = (bf16[512,256]{1,0:T(8,128)(2,1)S(1)}, bf16[512,256]{1,0:T(8,128)(2,1)S(1)}, u32[]{:S(2)}, u32[]{:S(2)}) collective-permute-start(bf16[512,256]{1,0:T(8,128)(2,1)S(1)} %collective-permute-done.14.refs_14_), channel_id=1, source_target_pairs={{0,1},{1,0},{2,3},{3,2},{4,5},{5,4},{6,7},{7,6},{8,9},{9,8},{10,11... | collective-permute-start | bytes 786440 | tf_op jit(solution)/shard_map/ppermute | solution.py:208
  67.4 9.5 %collective-permute-start.10 = (bf16[512,256]{1,0:T(8,128)(2,1)S(1)}, bf16[512,256]{1,0:T(8,128)(2,1)S(1)}, u32[]{:S(2)}, u32[]{:S(2)}) collective-permute-start(bf16[512,256]{1,0:T(8,128)(2,1)S(1)} %collective-permute-done.8.refs_2_), channel_id=1, source_target_pairs={{0,2},{1,3},{2,4},{3,5},{4,6},{5,7},{6,0},{7,1},{8,10},{9,11},{10,... | collective-permute-start | bytes 786440 | tf_op jit(solution)/shard_map/ppermute | solution.py:208
  69.9 7.9 %collective-permute-start.19 = (bf16[512,256]{1,0:T(8,128)(2,1)S(1)}, bf16[512,256]{1,0:T(8,128)(2,1)S(1)}, u32[]{:S(2)}, u32[]{:S(2)}) collective-permute-start(bf16[512,256]{1,0:T(8,128)(2,1)S(1)} %collective-permute-done.14.refs_14_), channel_id=1, source_target_pairs={{0,6},{1,7},{2,0},{3,1},{4,2},{5,3},{6,4},{7,5},{8,14},{9,15},{10,... | collective-permute-start | bytes 786440 | tf_op jit(solution)/shard_map/ppermute | solution.py:208
  73.3 6.5 %collective-permute-start.7 = (bf16[512,256]{1,0:T(8,128)(2,1)S(1)}, bf16[512,256]{1,0:T(8,128)(2,1)S(1)}, u32[]{:S(2)}, u32[]{:S(2)}) collective-permute-start(bf16[512,256]{1,0:T(8,128)(2,1)S(1)} %get-tuple-element.25.refs_0_), channel_id=1, source_target_pairs={{0,1},{1,0},{2,3},{3,2},{4,5},{5,4},{6,7},{7,6},{8,9},{9,8},{10,11... | collective-permute-start | bytes 786440 | tf_op jit(solution)/shard_map/ppermute | solution.py:208
  75.1 4.7 %collective-permute-start.17 = (bf16[512,256]{1,0:T(8,128)(2,1)S(1)}, bf16[512,256]{1,0:T(8,128)(2,1)S(1)}, u32[]{:S(2)}, u32[]{:S(2)}) collective-permute-start(bf16[512,256]{1,0:T(8,128)(2,1)S(1)} %get-tuple-element.26.refs_8_), channel_id=1, source_target_pairs={{0,1},{1,0},{2,3},{3,2},{4,5},{5,4},{6,7},{7,6},{8,9},{9,8},{10,11... | collective-permute-start | bytes 786440 | tf_op jit(solution)/shard_map/ppermute | solution.py:208
  75.3 5.7 %collective-permute-start.16 = (bf16[512,256]{1,0:T(8,128)(2,1)S(1)}, bf16[512,256]{1,0:T(8,128)(2,1)S(1)}, u32[]{:S(2)}, u32[]{:S(2)}) collective-permute-start(bf16[512,256]{1,0:T(8,128)(2,1)S(1)} %get-tuple-element.27.refs_6_), channel_id=1, source_target_pairs={{0,1},{1,0},{2,3},{3,2},{4,5},{5,4},{6,7},{7,6},{8,9},{9,8},{10,11... | collective-permute-start | bytes 786440 | tf_op jit(solution)/shard_map/ppermute | solution.py:208
  77.0 2.9 %collective-permute-start.11 = (bf16[512,256]{1,0:T(8,128)(2,1)S(1)}, bf16[512,256]{1,0:T(8,128)(2,1)S(1)}, u32[]{:S(2)}, u32[]{:S(2)}) collective-permute-start(bf16[512,256]{1,0:T(8,128)(2,1)S(1)} %collective-permute-done.10.refs_4_), channel_id=1, source_target_pairs={{0,1},{1,0},{2,3},{3,2},{4,5},{5,4},{6,7},{7,6},{8,9},{9,8},{10,11... | collective-permute-start | bytes 786440 | tf_op jit(solution)/shard_map/ppermute | solution.py:208
  77.8 3.2 %collective-permute-start.20 = (bf16[512,256]{1,0:T(8,128)(2,1)S(1)}, bf16[512,256]{1,0:T(8,128)(2,1)S(1)}, u32[]{:S(2)}, u32[]{:S(2)}) collective-permute-start(bf16[512,256]{1,0:T(8,128)(2,1)S(1)} %collective-permute-done.19.refs_12_), channel_id=1, source_target_pairs={{0,1},{1,0},{2,3},{3,2},{4,5},{5,4},{6,7},{7,6},{8,9},{9,8},{10,11... | collective-permute-start | bytes 786440 | tf_op jit(solution)/shard_map/ppermute | solution.py:208
  79.8 1.5 %collective-permute-start.18 = (bf16[512,256]{1,0:T(8,128)(2,1)S(1)}, bf16[512,256]{1,0:T(8,128)(2,1)S(1)}, u32[]{:S(2)}, u32[]{:S(2)}) collective-permute-start(bf16[512,256]{1,0:T(8,128)(2,1)S(1)} %get-tuple-element.28.refs_10_), channel_id=1, source_target_pairs={{0,1},{1,0},{2,3},{3,2},{4,5},{5,4},{6,7},{7,6},{8,9},{9,8},{10,11... | collective-permute-start | bytes 786440 | tf_op jit(solution)/shard_map/ppermute | solution.py:208
  (21 other events, 317.3 us)

commit v3 on v2

--- a/solution.py
+++ b/solution.py
@@ -208,7 +208,7 @@
     return lax.ppermute(array, "chan", pairs)
 
 
-ROUTES = tuple((step, swap) for step in range(4) for swap in range(2))
+ROUTES = ((1, 0), (3, 0), (1, 1), (3, 1), (2, 0), (2, 1), (0, 1), (0, 0))
 
 
 def split_kernel(weight, _, *outs):
@@ -233,6 +233,7 @@
         ],
         out_specs=[pl.BlockSpec((tile, width), lambda i: (i, 0))] * members,
         out_shape=[jax.ShapeDtypeStruct((channels, width), BF16)] * members,
+        compiler_params=pltpu.CompilerParams(vmem_limit_bytes=12 << 20),
         name="split_weight",
     )(weight, after)
 
@@ -246,6 +247,7 @@
         mark_kernel,
         in_specs=[pl.BlockSpec(memory_space=pl.ANY)] * len(arrays),
         out_shape=jax.ShapeDtypeStruct((8, TILE), F32),
+        compiler_params=pltpu.CompilerParams(vmem_limit_bytes=2 << 20),
         cost_estimate=pl.CostEstimate(flops=10**10, bytes_accessed=0, transcendentals=0),
         name="mark",
     )(*arrays)
@@ -315,6 +317,7 @@
     tops += [down_top, toward(down_top, 0, 1)]
     lows = [low, toward(low, 0, 1), up_low, toward(up_low, 0, 1), far_low, toward(far_low, 0, 1)]
     lows += [down_low, down_low_other]
+    weight = [weight[ROUTES.index((step, swap))] for step in range(4) for swap in range(2)]
     return project(tops, lows, weight)
 
 

time: 85.2 us -> 82.2 us (0.965)
  waiting for transfers between devices: 21.7 us -> 14.5 us
  local copies, waits for them, and re-layouts: 3.55 us -> 6.25 us
  starting transfers between devices: 40.9 us -> 43.2 us
    all_to_all x1, waiting for transfers between devices: 10 us -> 5.53 us  [on_device(): lax.all_to_all(convolve(data), 'seq', split_axis=0, concat_axis=0, tiled=...]
    ppermute x21, waiting for transfers between devices: 11.7 us -> 7.86 us  [toward(): return lax.ppermute(array, 'chan', pairs)]
    ppermute x21, starting transfers between devices: 26.4 us -> 29.7 us  [toward(): return lax.ppermute(array, 'chan', pairs)]
    unnamed x44 -> x34, local copies, waits for them, and re-layouts: 3.55 us -> 6.25 us
    pallas_call x1, Pallas kernels: 2.72 us -> 1.19 us  [split_weight(): pl.pallas_call(split_kernel, grid=(channels // tile,), in_specs=[pl.Block...]
    pallas_call x1, Pallas kernels: 7.84 us -> 9.06 us  [convolve(): pl.pallas_call(functools.partial(conv_kernel, group), in_specs=[space] *...]
    all_to_all x1, starting transfers between devices: 6.94 us -> 5.77 us  [on_device(): lax.all_to_all(convolve(data), 'seq', split_axis=0, concat_axis=0, tiled=...]
    all_to_all x1, waiting for transfers between devices: 0.01 us -> 1.14 us  [on_device(): lax.all_to_all(packed, 'seq', split_axis=0, concat_axis=0, tiled=True)]
  transfers between devices with their start and end apart: 23 -> 23, of which waited for: 7 -> 8; matrix products, arithmetic and copies ran while one was open for 0% -> 0% of each run, Pallas kernels for 13% -> 13%
where the time goes in v3:
time: 82.2 us; the launch traced here: 81.7 us
  starting transfers between devices  43.2 us (53%)
  Pallas kernels  16.9 us (21%)
  waiting for transfers between devices  14.5 us (18%)
  local copies, waits for them, and re-layouts  6.25 us (8%)
    ppermute x21, starting transfers between devices, toward(): return lax.ppermute(array, 'chan', pairs)  29.7 us
    pallas_call x1, Pallas kernels, convolve(): pl.pallas_call(functools.partial(conv_kernel, group), in_specs=[space] *...  9.06 us
    ppermute x21, waiting for transfers between devices, toward(): return lax.ppermute(array, 'chan', pairs)  7.86 us
    all_to_all x1, starting transfers between devices, on_device(): lax.all_to_all(packed, 'seq', split_axis=0, concat_axis=0, tiled=True)  7.77 us
    unnamed x34, local copies, waits for them, and re-layouts  6.25 us
    all_to_all x1, starting transfers between devices, on_device(): lax.all_to_all(convolve(data), 'seq', split_axis=0, concat_axis=0, tiled=...  5.77 us
    all_to_all x1, waiting for transfers between devices, on_device(): lax.all_to_all(convolve(data), 'seq', split_axis=0, concat_axis=0, tiled=...  5.53 us
    pallas_call x1, Pallas kernels, project(): pl.pallas_call(project_kernel, grid=(2,), in_specs=[pl.BlockSpec(memory_s...  3.36 us
  transfers between devices with their start and end apart: 23, of which 8 were waited for; matrix products, arithmetic and copies ran while one was open for 0% of the time, Pallas kernels for 13%

profile of v3, /device:TPU:1, one launch (start us, length us, event | category | flops | bytes accessed | tf_op | source)
XLA Modules:
  0.0 81.7 jit_solution(9057493102210898254)
XLA Ops:
  0.0 2.7 %pack.1._ = bf16[16,2,8,16,128]{4,3,2,1,0:T(8,128)(2,1)} custom-call(bf16[1024,256]{1,0:T(8,128)(2,1)} %gate_in.3, bf16[1024,256]{1,0:T(8,128)(2,1)} %value_in.3, f32[1024,256]{1,0:T(8,128)} %taps.1), custom_call_target="tpu_custom_call" | custom-call | tf_op jit(solution)/shard_map/pack/pallas_call | solution.py:77
  2.7 7.8 %all-to-all-start = ((bf16[16,2,8,16,128]{4,3,2,1,0:T(8,128)(2,1)}), bf16[16,2,8,16,128]{4,3,2,1,0:T(8,128)(2,1)}, u32[]{:S(2)}, u32[]{:S(2)}) async-start(bf16[16,2,8,16,128]{4,3,2,1,0:T(8,128)(2,1)} %pack.1._), calls=%async_computation | async-start | bytes 2097152 | tf_op jit(solution)/shard_map/all_to_all | solution.py:306
  10.5 1.2 %split_weight.1 = (bf16[256,512]{1,0:T(8,128)(2,1)S(1)}, bf16[256,512]{1,0:T(8,128)(2,1)S(1)}, bf16[256,512]{1,0:T(8,128)(2,1)}, bf16[256,512]{1,0:T(8,128)(2,1)...) custom-call(bf16[256,4096]{1,0:T(8,128)(2,1)S(1)} %copy-done.1, ...), custom_call_target="tpu_custom_call" | custom-call | tf_op jit(solution)/shard_map/split_weight/pallas_call | solution.py:227
  11.7 1.6 %collective-permute-start = (bf16[256,512]{1,0:T(8,128)(2,1)S(1)}, bf16[256,512]{1,0:T(8,128)(2,1)S(1)}, u32[]{:S(2)}, u32[]{:S(2)}) collective-permute-start(bf16[256,512]{1,0:T(8,128)(2,1)S(1)} %get-tuple-element.17), channel_id=1, source_target_pairs={{0,2},{1,3},{2,4},{3,5},{4,6},{5,7},{6,0},{7,1},{8,10},{9,11},{10,... | collective-permute-start | bytes 786440 | tf_op jit(solution)/shard_map/ppermute | solution.py:208
  13.3 2.2 %collective-permute-start.1 = (bf16[256,512]{1,0:T(8,128)(2,1)S(1)}, bf16[256,512]{1,0:T(8,128)(2,1)S(1)}, u32[]{:S(2)}, u32[]{:S(2)}) collective-permute-start(bf16[256,512]{1,0:T(8,128)(2,1)S(1)} %get-tuple-element.18), channel_id=1, source_target_pairs={{0,6},{1,7},{2,0},{3,1},{4,2},{5,3},{6,4},{7,5},{8,14},{9,15},{10,... | collective-permute-start | bytes 786440 | tf_op jit(solution)/shard_map/ppermute | solution.py:208
  16.2 2.2 %collective-permute-start.3 = (bf16[256,512]{1,0:T(8,128)(2,1)}, bf16[256,512]{1,0:T(8,128)(2,1)S(1)}, u32[]{:S(2)}, u32[]{:S(2)}) collective-permute-start(bf16[256,512]{1,0:T(8,128)(2,1)} %get-tuple-element.20), channel_id=1, source_target_pairs={{0,7},{1,6},{2,1},{3,0},{4,3},{5,2},{6,5},{7,4},{8,15},{9,14},{10,... | collective-permute-start | bytes 786440 | tf_op jit(solution)/shard_map/ppermute | solution.py:208
  18.4 1.1 %collective-permute-start.4 = (bf16[256,512]{1,0:T(8,128)(2,1)}, bf16[256,512]{1,0:T(8,128)(2,1)S(1)}, u32[]{:S(2)}, u32[]{:S(2)}) collective-permute-start(bf16[256,512]{1,0:T(8,128)(2,1)} %get-tuple-element.21), channel_id=1, source_target_pairs={{0,4},{1,5},{2,6},{3,7},{4,0},{5,1},{6,2},{7,3},{8,12},{9,13},{10,... | collective-permute-start | bytes 786440 | tf_op jit(solution)/shard_map/ppermute | solution.py:208
  20.1 1.1 %collective-permute-done.refs_0_.refs_18_ = bf16[256,512]{1,0:T(8,128)(2,1)S(1)} collective-permute-done((bf16[256,512]{1,0:T(8,128)(2,1)S(1)}, bf16[256,512]{1,0:T(8,128)(2,1)S(1)}, u32[]{:S(2)}, u32[]{:S(2)}) %collective-permute-start) | collective-permute-done | bytes 262176 | tf_op jit(solution)/shard_map/ppermute | solution.py:208
  21.2 4.1 %collective-permute-start.5 = (bf16[256,512]{1,0:T(8,128)(2,1)}, bf16[256,512]{1,0:T(8,128)(2,1)S(1)}, u32[]{:S(2)}, u32[]{:S(2)}) collective-permute-start(bf16[256,512]{1,0:T(8,128)(2,1)} %get-tuple-element.22), channel_id=1, source_target_pairs={{0,5},{1,4},{2,7},{3,6},{4,1},{5,0},{6,3},{7,2},{8,13},{9,12},{10,... | collective-permute-start | bytes 786440 | tf_op jit(solution)/shard_map/ppermute | solution.py:208
  25.3 1.1 %all-to-all-done.data = bf16[16,2,8,16,128]{4,3,2,1,0:T(8,128)(2,1)} async-done(((bf16[16,2,8,16,128]{4,3,2,1,0:T(8,128)(2,1)}), bf16[16,2,8,16,128]{4,3,2,1,0:T(8,128)(2,1)}, u32[]{:S(2)}, u32[]{:S(2)}) %all-to-all-start) | async-done | bytes 1048608 | tf_op jit(solution)/shard_map/all_to_all | solution.py:306
  26.5 1.2 %copy-done.15 = bf16[2176,256]{1,0:T(8,128)(2,1)S(1)} copy-done((bf16[2176,256]{1,0:T(8,128)(2,1)S(1)}, bf16[2176,256]{1,0:T(8,128)(2,1)}, u32[]{:S(2)}) %copy-start.15) | copy-done | bytes 1114136
  27.7 9.1 %convolve.1 = bf16[16,8,16,128]{3,2,1,0:T(8,128)(2,1)} custom-call(bf16[16,2,8,16,128]{4,3,2,1,0:T(8,128)(2,1)} %all-to-all-done.data, bf16[2176,256]{1,0:T(8,128)(2,1)S(1)} %copy-done.15, f32[256,128]{1,0:T(8,128)S(1)} %copy-done.16), custom_call_target="tpu_custom_call" | custom-call | flops 10000000000 | bytes 4194304 | tf_op jit(solution)/shard_map/convolve/pallas_call | solution.py:146
  36.8 5.8 %all-to-all-start.1 = ((bf16[16,8,16,128]{3,2,1,0:T(8,128)(2,1)}), bf16[16,8,16,128]{3,2,1,0:T(8,128)(2,1)S(1)}, u32[]{:S(2)}, u32[]{:S(2)}) async-start(bf16[16,8,16,128]{3,2,1,0:T(8,128)(2,1)} %convolve.1), calls=%async_computation.1 | async-start | bytes 1048576 | tf_op jit(solution)/shard_map/all_to_all | solution.py:309
  44.7 0.9 %copy-done.6 = bf16[256,512]{1,0:T(8,128)(2,1)S(1)} copy-done((bf16[256,512]{1,0:T(8,128)(2,1)S(1)}, bf16[256,512]{1,0:T(8,128)(2,1)}, u32[]{:S(2)}) %copy-start.6) | copy-done | bytes 262168
  47.6 5.5 %all-to-all-done.1.conv = bf16[16,8,16,128]{3,2,1,0:T(8,128)(2,1)S(1)} async-done(((bf16[16,8,16,128]{3,2,1,0:T(8,128)(2,1)}), bf16[16,8,16,128]{3,2,1,0:T(8,128)(2,1)S(1)}, u32[]{:S(2)}, u32[]{:S(2)}) %all-to-all-start.1) | async-done | bytes 524320 | tf_op jit(solution)/shard_map/all_to_all | solution.py:309
  54.3 2.2 %collective-permute-start.14 = (bf16[512,256]{1,0:T(8,128)(2,1)S(1)}, bf16[512,256]{1,0:T(8,128)(2,1)S(1)}, u32[]{:S(2)}, u32[]{:S(2)}) collective-permute-start(bf16[512,256]{1,0:T(8,128)(2,1)S(1)} %get-tuple-element.26.refs_8_), channel_id=1, source_target_pairs={{0,6},{1,7},{2,0},{3,1},{4,2},{5,3},{6,4},{7,5},{8,14},{9,15},{10,... | collective-permute-start | bytes 786440 | tf_op jit(solution)/shard_map/ppermute | solution.py:208
  56.7 1.3 %collective-permute-start.12 = (bf16[512,256]{1,0:T(8,128)(2,1)S(1)}, bf16[512,256]{1,0:T(8,128)(2,1)S(1)}, u32[]{:S(2)}, u32[]{:S(2)}) collective-permute-start(bf16[512,256]{1,0:T(8,128)(2,1)S(1)} %get-tuple-element.26.refs_8_), channel_id=1, source_target_pairs={{0,2},{1,3},{2,4},{3,5},{4,6},{5,7},{6,0},{7,1},{8,10},{9,11},{10,... | collective-permute-start | bytes 786440 | tf_op jit(solution)/shard_map/ppermute | solution.py:208
  58.0 2.9 %collective-permute-done.8.refs_2_ = bf16[512,256]{1,0:T(8,128)(2,1)S(1)} collective-permute-done((bf16[512,256]{1,0:T(8,128)(2,1)S(1)}, bf16[512,256]{1,0:T(8,128)(2,1)S(1)}, u32[]{:S(2)}, u32[]{:S(2)}) %collective-permute-start.8) | collective-permute-done | bytes 262176 | tf_op jit(solution)/shard_map/ppermute | solution.py:208
  60.9 5.3 %collective-permute-start.9 = (bf16[512,256]{1,0:T(8,128)(2,1)S(1)}, bf16[512,256]{1,0:T(8,128)(2,1)S(1)}, u32[]{:S(2)}, u32[]{:S(2)}) collective-permute-start(bf16[512,256]{1,0:T(8,128)(2,1)S(1)} %collective-permute-done.8.refs_2_), channel_id=1, source_target_pairs={{0,1},{1,0},{2,3},{3,2},{4,5},{5,4},{6,7},{7,6},{8,9},{9,8},{10,11... | collective-permute-start | bytes 786440 | tf_op jit(solution)/shard_map/ppermute | solution.py:208
  66.3 2.9 %collective-permute-start.19 = (bf16[512,256]{1,0:T(8,128)(2,1)S(1)}, bf16[512,256]{1,0:T(8,128)(2,1)S(1)}, u32[]{:S(2)}, u32[]{:S(2)}) collective-permute-start(bf16[512,256]{1,0:T(8,128)(2,1)S(1)} %collective-permute-done.14.refs_14_), channel_id=1, source_target_pairs={{0,6},{1,7},{2,0},{3,1},{4,2},{5,3},{6,4},{7,5},{8,14},{9,15},{10,... | collective-permute-start | bytes 786440 | tf_op jit(solution)/shard_map/ppermute | solution.py:208
  69.2 3.2 %collective-permute-start.7 = (bf16[512,256]{1,0:T(8,128)(2,1)S(1)}, bf16[512,256]{1,0:T(8,128)(2,1)S(1)}, u32[]{:S(2)}, u32[]{:S(2)}) collective-permute-start(bf16[512,256]{1,0:T(8,128)(2,1)S(1)} %get-tuple-element.25.refs_0_), channel_id=1, source_target_pairs={{0,1},{1,0},{2,3},{3,2},{4,5},{5,4},{6,7},{7,6},{8,9},{9,8},{10,11... | collective-permute-start | bytes 786440 | tf_op jit(solution)/shard_map/ppermute | solution.py:208
  73.0 2.4 %collective-permute-done.10.refs_4_ = bf16[512,256]{1,0:T(8,128)(2,1)S(1)} collective-permute-done((bf16[512,256]{1,0:T(8,128)(2,1)S(1)}, bf16[512,256]{1,0:T(8,128)(2,1)S(1)}, u32[]{:S(2)}, u32[]{:S(2)}) %collective-permute-start.10) | collective-permute-done | bytes 262176 | tf_op jit(solution)/shard_map/ppermute | solution.py:208
  75.4 1.0 %collective-permute-start.11 = (bf16[512,256]{1,0:T(8,128)(2,1)S(1)}, bf16[512,256]{1,0:T(8,128)(2,1)S(1)}, u32[]{:S(2)}, u32[]{:S(2)}) collective-permute-start(bf16[512,256]{1,0:T(8,128)(2,1)S(1)} %collective-permute-done.10.refs_4_), channel_id=1, source_target_pairs={{0,1},{1,0},{2,3},{3,2},{4,5},{5,4},{6,7},{7,6},{8,9},{9,8},{10,11... | collective-permute-start | bytes 786440 | tf_op jit(solution)/shard_map/ppermute | solution.py:208
  78.3 3.4 %project.1 = bf16[1024,512]{1,0:T(8,128)(2,1)} custom-call(bf16[512,256]{1,0:T(8,128)(2,1)S(1)} %get-tuple-element.25.refs_0_, bf16[512,256]{1,0:T(8,128)(2,1)S(1)} %collective-permute-done.7.refs_1_, bf16[512,256]{1,0:T(8,128)(2,1)S(1)} %collective-permute-done.8.refs_2_, bf16[512,256]{1,0:T(8,128)(2,1)S(1)} %collective-permute-done.9.refs_2_.refs_3_, ...), custom_call_target="tpu_custom_call" | custom-call | tf_op jit(solution)/shard_map/project/pallas_call | solution.py:293
  (63 shorter events, 8.7 us)
Async XLA Ops:
  2.7 23.8 %all-to-all-start = ((bf16[16,2,8,16,128]{4,3,2,1,0:T(8,128)(2,1)}), bf16[16,2,8,16,128]{4,3,2,1,0:T(8,128)(2,1)}, u32[]{:S(2)}, u32[]{:S(2)}) async-start(bf16[16,2,8,16,128]{4,3,2,1,0:T(8,128)(2,1)} %pack.1._), calls=%async_computation | async-start | bytes 2097152 | tf_op jit(solution)/shard_map/all_to_all | solution.py:306
  11.7 9.6 %collective-permute-start = (bf16[256,512]{1,0:T(8,128)(2,1)S(1)}, bf16[256,512]{1,0:T(8,128)(2,1)S(1)}, u32[]{:S(2)}, u32[]{:S(2)}) collective-permute-start(bf16[256,512]{1,0:T(8,128)(2,1)S(1)} %get-tuple-element.17), channel_id=1, source_target_pairs={{0,2},{1,3},{2,4},{3,5},{4,6},{5,7},{6,0},{7,1},{8,10},{9,11},{10,... | collective-permute-start | bytes 786440 | tf_op jit(solution)/shard_map/ppermute | solution.py:208
  13.3 12.0 %collective-permute-start.1 = (bf16[256,512]{1,0:T(8,128)(2,1)S(1)}, bf16[256,512]{1,0:T(8,128)(2,1)S(1)}, u32[]{:S(2)}, u32[]{:S(2)}) collective-permute-start(bf16[256,512]{1,0:T(8,128)(2,1)S(1)} %get-tuple-element.18), channel_id=1, source_target_pairs={{0,6},{1,7},{2,0},{3,1},{4,2},{5,3},{6,4},{7,5},{8,14},{9,15},{10,... | collective-permute-start | bytes 786440 | tf_op jit(solution)/shard_map/ppermute | solution.py:208
  15.5 27.1 %collective-permute-start.2 = (bf16[256,512]{1,0:T(8,128)(2,1)}, bf16[256,512]{1,0:T(8,128)(2,1)S(1)}, u32[]{:S(2)}, u32[]{:S(2)}) collective-permute-start(bf16[256,512]{1,0:T(8,128)(2,1)} %get-tuple-element.19), channel_id=1, source_target_pairs={{0,3},{1,2},{2,5},{3,4},{4,7},{5,6},{6,1},{7,0},{8,11},{9,10},{10,... | collective-permute-start | bytes 786440 | tf_op jit(solution)/shard_map/ppermute | solution.py:208
  16.2 26.4 %collective-permute-start.3 = (bf16[256,512]{1,0:T(8,128)(2,1)}, bf16[256,512]{1,0:T(8,128)(2,1)S(1)}, u32[]{:S(2)}, u32[]{:S(2)}) collective-permute-start(bf16[256,512]{1,0:T(8,128)(2,1)} %get-tuple-element.20), channel_id=1, source_target_pairs={{0,7},{1,6},{2,1},{3,0},{4,3},{5,2},{6,5},{7,4},{8,15},{9,14},{10,... | collective-permute-start | bytes 786440 | tf_op jit(solution)/shard_map/ppermute | solution.py:208
  18.4 24.2 %collective-permute-start.4 = (bf16[256,512]{1,0:T(8,128)(2,1)}, bf16[256,512]{1,0:T(8,128)(2,1)S(1)}, u32[]{:S(2)}, u32[]{:S(2)}) collective-permute-start(bf16[256,512]{1,0:T(8,128)(2,1)} %get-tuple-element.21), channel_id=1, source_target_pairs={{0,4},{1,5},{2,6},{3,7},{4,0},{5,1},{6,2},{7,3},{8,12},{9,13},{10,... | collective-permute-start | bytes 786440 | tf_op jit(solution)/shard_map/ppermute | solution.py:208
  21.2 22.1 %collective-permute-start.5 = (bf16[256,512]{1,0:T(8,128)(2,1)}, bf16[256,512]{1,0:T(8,128)(2,1)S(1)}, u32[]{:S(2)}, u32[]{:S(2)}) collective-permute-start(bf16[256,512]{1,0:T(8,128)(2,1)} %get-tuple-element.22), channel_id=1, source_target_pairs={{0,5},{1,4},{2,7},{3,6},{4,1},{5,0},{6,3},{7,2},{8,13},{9,12},{10,... | collective-permute-start | bytes 786440 | tf_op jit(solution)/shard_map/ppermute | solution.py:208
  25.3 18.7 %collective-permute-start.6 = (bf16[256,512]{1,0:T(8,128)(2,1)}, bf16[256,512]{1,0:T(8,128)(2,1)S(1)}, u32[]{:S(2)}, u32[]{:S(2)}) collective-permute-start(bf16[256,512]{1,0:T(8,128)(2,1)} %get-tuple-element.23), channel_id=1, source_target_pairs={{0,1},{1,0},{2,3},{3,2},{4,5},{5,4},{6,7},{7,6},{8,9},{9,8},{10,11... | collective-permute-start | bytes 786440 | tf_op jit(solution)/shard_map/ppermute | solution.py:208
  36.8 16.4 %all-to-all-start.1 = ((bf16[16,8,16,128]{3,2,1,0:T(8,128)(2,1)}), bf16[16,8,16,128]{3,2,1,0:T(8,128)(2,1)S(1)}, u32[]{:S(2)}, u32[]{:S(2)}) async-start(bf16[16,8,16,128]{3,2,1,0:T(8,128)(2,1)} %convolve.1), calls=%async_computation.1 | async-start | bytes 1048576 | tf_op jit(solution)/shard_map/all_to_all | solution.py:309
  53.1 25.2 %copy-start.13 = (bf16[256,512]{1,0:T(8,128)(2,1)S(1)}, bf16[256,512]{1,0:T(8,128)(2,1)}, u32[]{:S(2)}) copy-start(bf16[256,512]{1,0:T(8,128)(2,1)} %copy-done.11) | copy-start | bytes 786436
  53.7 7.2 %collective-permute-start.8 = (bf16[512,256]{1,0:T(8,128)(2,1)S(1)}, bf16[512,256]{1,0:T(8,128)(2,1)S(1)}, u32[]{:S(2)}, u32[]{:S(2)}) collective-permute-start(bf16[512,256]{1,0:T(8,128)(2,1)S(1)} %get-tuple-element.25.refs_0_), channel_id=1, source_target_pairs={{0,2},{1,3},{2,4},{3,5},{4,6},{5,7},{6,0},{7,1},{8,10},{9,11},{10,... | collective-permute-start | bytes 786440 | tf_op jit(solution)/shard_map/ppermute | solution.py:208
  54.3 11.9 %collective-permute-start.14 = (bf16[512,256]{1,0:T(8,128)(2,1)S(1)}, bf16[512,256]{1,0:T(8,128)(2,1)S(1)}, u32[]{:S(2)}, u32[]{:S(2)}) collective-permute-start(bf16[512,256]{1,0:T(8,128)(2,1)S(1)} %get-tuple-element.26.refs_8_), channel_id=1, source_target_pairs={{0,6},{1,7},{2,0},{3,1},{4,2},{5,3},{6,4},{7,5},{8,14},{9,15},{10,... | collective-permute-start | bytes 786440 | tf_op jit(solution)/shard_map/ppermute | solution.py:208
  56.5 9.8 %collective-permute-start.13 = (bf16[512,256]{1,0:T(8,128)(2,1)S(1)}, bf16[512,256]{1,0:T(8,128)(2,1)S(1)}, u32[]{:S(2)}, u32[]{:S(2)}) collective-permute-start(bf16[512,256]{1,0:T(8,128)(2,1)S(1)} %get-tuple-element.25.refs_0_), channel_id=1, source_target_pairs={{0,6},{1,7},{2,0},{3,1},{4,2},{5,3},{6,4},{7,5},{8,14},{9,15},{10,... | collective-permute-start | bytes 786440 | tf_op jit(solution)/shard_map/ppermute | solution.py:208
  56.7 12.5 %collective-permute-start.12 = (bf16[512,256]{1,0:T(8,128)(2,1)S(1)}, bf16[512,256]{1,0:T(8,128)(2,1)S(1)}, u32[]{:S(2)}, u32[]{:S(2)}) collective-permute-start(bf16[512,256]{1,0:T(8,128)(2,1)S(1)} %get-tuple-element.26.refs_8_), channel_id=1, source_target_pairs={{0,2},{1,3},{2,4},{3,5},{4,6},{5,7},{6,0},{7,1},{8,10},{9,11},{10,... | collective-permute-start | bytes 786440 | tf_op jit(solution)/shard_map/ppermute | solution.py:208
  60.9 11.4 %collective-permute-start.9 = (bf16[512,256]{1,0:T(8,128)(2,1)S(1)}, bf16[512,256]{1,0:T(8,128)(2,1)S(1)}, u32[]{:S(2)}, u32[]{:S(2)}) collective-permute-start(bf16[512,256]{1,0:T(8,128)(2,1)S(1)} %collective-permute-done.8.refs_2_), channel_id=1, source_target_pairs={{0,1},{1,0},{2,3},{3,2},{4,5},{5,4},{6,7},{7,6},{8,9},{9,8},{10,11... | collective-permute-start | bytes 786440 | tf_op jit(solution)/shard_map/ppermute | solution.py:208
  66.2 6.2 %collective-permute-start.15 = (bf16[512,256]{1,0:T(8,128)(2,1)S(1)}, bf16[512,256]{1,0:T(8,128)(2,1)S(1)}, u32[]{:S(2)}, u32[]{:S(2)}) collective-permute-start(bf16[512,256]{1,0:T(8,128)(2,1)S(1)} %collective-permute-done.14.refs_14_), channel_id=1, source_target_pairs={{0,1},{1,0},{2,3},{3,2},{4,5},{5,4},{6,7},{7,6},{8,9},{9,8},{10,11... | collective-permute-start | bytes 786440 | tf_op jit(solution)/shard_map/ppermute | solution.py:208
  66.2 9.2 %collective-permute-start.10 = (bf16[512,256]{1,0:T(8,128)(2,1)S(1)}, bf16[512,256]{1,0:T(8,128)(2,1)S(1)}, u32[]{:S(2)}, u32[]{:S(2)}) collective-permute-start(bf16[512,256]{1,0:T(8,128)(2,1)S(1)} %collective-permute-done.8.refs_2_), channel_id=1, source_target_pairs={{0,2},{1,3},{2,4},{3,5},{4,6},{5,7},{6,0},{7,1},{8,10},{9,11},{10,... | collective-permute-start | bytes 786440 | tf_op jit(solution)/shard_map/ppermute | solution.py:208
  66.3 10.2 %collective-permute-start.19 = (bf16[512,256]{1,0:T(8,128)(2,1)S(1)}, bf16[512,256]{1,0:T(8,128)(2,1)S(1)}, u32[]{:S(2)}, u32[]{:S(2)}) collective-permute-start(bf16[512,256]{1,0:T(8,128)(2,1)S(1)} %collective-permute-done.14.refs_14_), channel_id=1, source_target_pairs={{0,6},{1,7},{2,0},{3,1},{4,2},{5,3},{6,4},{7,5},{8,14},{9,15},{10,... | collective-permute-start | bytes 786440 | tf_op jit(solution)/shard_map/ppermute | solution.py:208
  69.2 7.3 %collective-permute-start.7 = (bf16[512,256]{1,0:T(8,128)(2,1)S(1)}, bf16[512,256]{1,0:T(8,128)(2,1)S(1)}, u32[]{:S(2)}, u32[]{:S(2)}) collective-permute-start(bf16[512,256]{1,0:T(8,128)(2,1)S(1)} %get-tuple-element.25.refs_0_), channel_id=1, source_target_pairs={{0,1},{1,0},{2,3},{3,2},{4,5},{5,4},{6,7},{7,6},{8,9},{9,8},{10,11... | collective-permute-start | bytes 786440 | tf_op jit(solution)/shard_map/ppermute | solution.py:208
  72.3 4.6 %collective-permute-start.17 = (bf16[512,256]{1,0:T(8,128)(2,1)S(1)}, bf16[512,256]{1,0:T(8,128)(2,1)S(1)}, u32[]{:S(2)}, u32[]{:S(2)}) collective-permute-start(bf16[512,256]{1,0:T(8,128)(2,1)S(1)} %get-tuple-element.26.refs_8_), channel_id=1, source_target_pairs={{0,1},{1,0},{2,3},{3,2},{4,5},{5,4},{6,7},{7,6},{8,9},{9,8},{10,11... | collective-permute-start | bytes 786440 | tf_op jit(solution)/shard_map/ppermute | solution.py:208
  72.5 5.5 %collective-permute-start.16 = (bf16[512,256]{1,0:T(8,128)(2,1)S(1)}, bf16[512,256]{1,0:T(8,128)(2,1)S(1)}, u32[]{:S(2)}, u32[]{:S(2)}) collective-permute-start(bf16[512,256]{1,0:T(8,128)(2,1)S(1)} %get-tuple-element.27.refs_6_), channel_id=1, source_target_pairs={{0,1},{1,0},{2,3},{3,2},{4,5},{5,4},{6,7},{7,6},{8,9},{9,8},{10,11... | collective-permute-start | bytes 786440 | tf_op jit(solution)/shard_map/ppermute | solution.py:208
  75.4 2.2 %collective-permute-start.11 = (bf16[512,256]{1,0:T(8,128)(2,1)S(1)}, bf16[512,256]{1,0:T(8,128)(2,1)S(1)}, u32[]{:S(2)}, u32[]{:S(2)}) collective-permute-start(bf16[512,256]{1,0:T(8,128)(2,1)S(1)} %collective-permute-done.10.refs_4_), channel_id=1, source_target_pairs={{0,1},{1,0},{2,3},{3,2},{4,5},{5,4},{6,7},{7,6},{8,9},{9,8},{10,11... | collective-permute-start | bytes 786440 | tf_op jit(solution)/shard_map/ppermute | solution.py:208
  76.4 1.5 %collective-permute-start.20 = (bf16[512,256]{1,0:T(8,128)(2,1)S(1)}, bf16[512,256]{1,0:T(8,128)(2,1)S(1)}, u32[]{:S(2)}, u32[]{:S(2)}) collective-permute-start(bf16[512,256]{1,0:T(8,128)(2,1)S(1)} %collective-permute-done.19.refs_12_), channel_id=1, source_target_pairs={{0,1},{1,0},{2,3},{3,2},{4,5},{5,4},{6,7},{7,6},{8,9},{9,8},{10,11... | collective-permute-start | bytes 786440 | tf_op jit(solution)/shard_map/ppermute | solution.py:208
  76.4 1.9 %collective-permute-start.18 = (bf16[512,256]{1,0:T(8,128)(2,1)S(1)}, bf16[512,256]{1,0:T(8,128)(2,1)S(1)}, u32[]{:S(2)}, u32[]{:S(2)}) collective-permute-start(bf16[512,256]{1,0:T(8,128)(2,1)S(1)} %get-tuple-element.28.refs_10_), channel_id=1, source_target_pairs={{0,1},{1,0},{2,3},{3,2},{4,5},{5,4},{6,7},{7,6},{8,9},{9,8},{10,11... | collective-permute-start | bytes 786440 | tf_op jit(solution)/shard_map/ppermute | solution.py:208
  (16 other events, 113.1 us)

commit v4 on v3

--- a/solution.py
+++ b/solution.py
@@ -63,7 +63,8 @@
     return jnp.dot(left, right, preferred_element_type=F32)
 
 
-def pack_kernel(gate_in, value_in, taps, out):
+def pack_kernel(gate_in, value_in, taps, out, token):
+    token[...] = jnp.zeros_like(token)
     for b in range(out.shape[2]):
         rows = slice(b * TILE, (b + 1) * TILE)
         signal = gate_in[rows].astype(F32) * value_in[rows].astype(F32)
@@ -78,8 +79,14 @@
         pack_kernel,
         grid=(rows // (blocks * TILE),),
         in_specs=[block] * 3,
-        out_specs=pl.BlockSpec((16, 2, blocks, 16, TILE), lambda b: (0, 0, b, 0, 0)),
-        out_shape=jax.ShapeDtypeStruct((16, 2, rows // TILE, 16, TILE), BF16),
+        out_specs=[
+            pl.BlockSpec((16, 2, blocks, 16, TILE), lambda b: (0, 0, b, 0, 0)),
+            pl.BlockSpec((8, TILE), lambda b: (0, 0)),
+        ],
+        out_shape=[
+            jax.ShapeDtypeStruct((16, 2, rows // TILE, 16, TILE), BF16),
+            jax.ShapeDtypeStruct((8, TILE), F32),
+        ],
         name="pack",
     )(gate_in, value_in, taps)
 
@@ -253,58 +260,68 @@
     )(*arrays)
 
 
-def tie_kernel(count, *refs):
-    for source, target in zip(refs[:count], refs[-count:]):
-        target[...] = source[...]
-
-
-def tie(arrays, after):
-    space = pl.BlockSpec(memory_space=pltpu.VMEM)
-    count = len(arrays)
-    return pl.pallas_call(
-        functools.partial(tie_kernel, count),
-        in_specs=[space] * count + [pl.BlockSpec(memory_space=pl.ANY)] * len(after),
-        out_specs=[space] * count,
-        out_shape=[jax.ShapeDtypeStruct(array.shape, array.dtype) for array in arrays],
-        input_output_aliases={k: k for k in range(count)},
-        compiler_params=pltpu.CompilerParams(vmem_limit_bytes=12 << 20),
-        name="tie",
-    )(*arrays, *after)
-
-
-def project_kernel(*refs):
-    mixed, weight, out = refs[:16], refs[16:24], refs[24]
-
-    def fill(pieces):
-        total = matmul(pieces[0][...], weight[0][...])
-        for piece, part in zip(pieces[1:], weight[1:]):
-            total = total + matmul(piece[...], part[...])
-        out[...] = total.astype(BF16)
-
-    for half in range(2):
-        pl.when(pl.program_id(0) == half)(
-            functools.partial(fill, mixed[8 * half : 8 * half + 8])
-        )
-
-
-def project(top, low, weight):
+def fold_kernel(*refs):
+    top, low, weight = refs[:4], refs[4:8], refs[8:13]
+    partial, first, second = refs[13:]
+    rows = top[0].shape[0]
+    for half, pieces in enumerate((top, low)):
+        total = None
+        for piece, k in zip(pieces, ((0, 1, 2, 3), (0, 3, 4, 1))[half]):
+            term = matmul(piece[...], weight[k][...])
+            total = term if total is None else total + term
+        partial[half * rows : half * rows + rows] = total
+    first[...] = top[3][...]
+    second[...] = low[3][...]
+
+
+def fold(top, low, weight):
     rows = top[0].shape[0]
     features = weight[0].shape[1]
+    space = pl.BlockSpec(memory_space=pltpu.VMEM)
+    piece = jax.ShapeDtypeStruct(top[0].shape, BF16)
+    return pl.pallas_call(
+        fold_kernel,
+        in_specs=[space] * 13,
+        out_specs=[space] * 3,
+        out_shape=[jax.ShapeDtypeStruct((2 * rows, features), F32), piece, piece],
+        compiler_params=pltpu.CompilerParams(vmem_limit_bytes=12 << 20),
+        name="fold",
+    )(*top, *low, *weight)
+
+
+def project_kernel(*refs):
+    mixed, weight, partial, out = refs[:8], refs[8:13], refs[13], refs[14]
+    rows = out.shape[0]
+
+    def fill(half):
+        total = partial[half * rows : half * rows + rows]
+        places = ((0, 1, 2, 3), (0, 1, 2, 4))[half]
+        for piece, k in zip(mixed[4 * half : 4 * half + 4], places):
+            total = total + matmul(piece[...], weight[k][...])
+        out[...] = total.astype(BF16)
+
+    for half in range(2):
+        pl.when(pl.program_id(0) == half)(functools.partial(fill, half))
+
+
+def project(top, low, weight, partial):
+    rows = top[0].shape[0]
+    features = weight[0].shape[1]
     return pl.pallas_call(
         project_kernel,
         grid=(2,),
-        in_specs=[pl.BlockSpec(memory_space=pltpu.VMEM)] * 24,
+        in_specs=[pl.BlockSpec(memory_space=pltpu.VMEM)] * 14,
         out_specs=pl.BlockSpec((rows, features), lambda i: (i, 0)),
         out_shape=jax.ShapeDtypeStruct((2 * rows, features), BF16),
-        compiler_params=pltpu.CompilerParams(vmem_limit_bytes=16 << 20),
+        compiler_params=pltpu.CompilerParams(vmem_limit_bytes=12 << 20),
         name="project",
-    )(*top, *low, *weight)
+    )(*top, *low, *weight, partial)
 
 
 def on_device(gate_out, gate_in, value_in, filter_taps, skip_bias, resume_at, out_weight):
-    packed = pack(gate_in, value_in, filter_taps)
+    packed, token = pack(gate_in, value_in, filter_taps)
     data = lax.all_to_all(packed, "seq", split_axis=0, concat_axis=0, tiled=True)
-    weight = split_weight(out_weight, packed)
+    weight = split_weight(out_weight, token)
     weight = [toward(w, *route) if any(route) else w for w, route in zip(weight, ROUTES)]
     conv = lax.all_to_all(convolve(data), "seq", split_axis=0, concat_axis=0, tiled=True)
     top, low = mix(resume_at, conv, gate_out, gate_in, value_in, skip_bias, mark(weight))
@@ -312,13 +329,15 @@
     up_low, down_top = toward(low, 1, 0), toward(top, 3, 0)
     far_top, far_low = toward(up_top, 1, 0), toward(down_low, 3, 0)
     up_top_other, down_low_other = toward(up_top, 0, 1), toward(down_low, 0, 1)
-    up_low, down_top = tie([up_low, down_top], [up_top_other, down_low_other])
-    tops = [top, toward(top, 0, 1), up_top, up_top_other, far_top, toward(far_top, 0, 1)]
-    tops += [down_top, toward(down_top, 0, 1)]
-    lows = [low, toward(low, 0, 1), up_low, toward(up_low, 0, 1), far_low, toward(far_low, 0, 1)]
-    lows += [down_low, down_low_other]
-    weight = [weight[ROUTES.index((step, swap))] for step in range(4) for swap in range(2)]
-    return project(tops, lows, weight)
+    weight = {route: weight[ROUTES.index(route)] for route in ROUTES}
+    factors = [weight[route] for route in ((0, 0), (1, 0), (1, 1), (3, 0), (3, 1))]
+    partial, down_top, up_low = fold(
+        [top, up_top, up_top_other, down_top], [low, down_low, down_low_other, up_low], factors
+    )
+    tops = [toward(top, 0, 1), far_top, toward(far_top, 0, 1), toward(down_top, 0, 1)]
+    lows = [toward(low, 0, 1), far_low, toward(far_low, 0, 1), toward(up_low, 0, 1)]
+    factors = [weight[route] for route in ((0, 1), (2, 0), (2, 1), (3, 1), (1, 1))]
+    return project(tops, lows, factors, partial)
 
 
 def solution(mesh):

time: 82.2 us -> 79.7 us (0.970)
  local copies, waits for them, and re-layouts: 6.25 us -> 9.56 us
  starting transfers between devices: 43.2 us -> 40.8 us
  waiting for transfers between devices: 14.5 us -> 12.3 us
  Pallas kernels: 16.9 us -> 15.7 us
    unnamed x34 -> x42, local copies, waits for them, and re-layouts: 6.25 us -> 9.56 us
    all_to_all x1, waiting for transfers between devices: 5.53 us -> 2.93 us  [on_device(): lax.all_to_all(convolve(data), 'seq', split_axis=0, concat_axis=0, tiled=...]
    ppermute x21, starting transfers between devices: 29.7 us -> 27.2 us  [toward(): return lax.ppermute(array, 'chan', pairs)]
    pallas_call x1, Pallas kernels: 9.06 us -> 7.84 us  [convolve(): pl.pallas_call(functools.partial(conv_kernel, group), in_specs=[space] *...]
    pallas_call x1, Pallas kernels: 0.06 us -> 1.25 us  [fold(): pl.pallas_call(fold_kernel, in_specs=[space] * 13, out_specs=[space] * 3,...]
    pallas_call x1, Pallas kernels: 3.36 us -> 2.23 us  [project(): pl.pallas_call(project_kernel, grid=(2,), in_specs=[pl.BlockSpec(memory_s...]
  transfers between devices with their start and end apart: 23 -> 23, of which waited for: 8 -> 6; matrix products, arithmetic and copies ran while one was open for 0% -> 0% of each run, Pallas kernels for 13% -> 13%
where the time goes in v4:
time: 79.7 us; the launch traced here: 79.2 us
  starting transfers between devices  40.8 us (51%)
  Pallas kernels  15.7 us (20%)
  waiting for transfers between devices  12.3 us (15%)
  local copies, waits for them, and re-layouts  9.56 us (12%)
  between operations  0.83 us (1%)
    ppermute x21, starting transfers between devices, toward(): return lax.ppermute(array, 'chan', pairs)  27.2 us
    unnamed x42, local copies, waits for them, and re-layouts  9.56 us
    ppermute x21, waiting for transfers between devices, toward(): return lax.ppermute(array, 'chan', pairs)  8.33 us
    pallas_call x1, Pallas kernels, convolve(): pl.pallas_call(functools.partial(conv_kernel, group), in_specs=[space] *...  7.84 us
    all_to_all x1, starting transfers between devices, on_device(): lax.all_to_all(packed, 'seq', split_axis=0, concat_axis=0, tiled=True)  7.72 us
    all_to_all x1, starting transfers between devices, on_device(): lax.all_to_all(convolve(data), 'seq', split_axis=0, concat_axis=0, tiled=...  5.87 us
    all_to_all x1, waiting for transfers between devices, on_device(): lax.all_to_all(convolve(data), 'seq', split_axis=0, concat_axis=0, tiled=...  2.93 us
    pallas_call x1, Pallas kernels, pack(): pl.pallas_call(pack_kernel, grid=(rows // (blocks * TILE),), in_specs=[bl...  2.66 us
  transfers between devices with their start and end apart: 23, of which 6 were waited for; matrix products, arithmetic and copies ran while one was open for 0% of the time, Pallas kernels for 13%

profile of v4, /device:TPU:1, one launch (start us, length us, event | category | flops | bytes accessed | tf_op | source)
XLA Modules:
  0.0 79.2 jit_solution(14187258495457845675)
XLA Ops:
  0.0 2.7 %pack.1 = (bf16[16,2,8,16,128]{4,3,2,1,0:T(8,128)(2,1)}, f32[8,128]{1,0:T(8,128)}) custom-call(bf16[1024,256]{1,0:T(8,128)(2,1)} %gate_in.3, bf16[1024,256]{1,0:T(8,128)(2,1)} %value_in.3, f32[1024,256]{1,0:T(8,128)} %taps.1), custom_call_target="tpu_custom_call" | custom-call | tf_op jit(solution)/shard_map/pack/pallas_call | solution.py:78
  2.7 7.7 %all-to-all-start = ((bf16[16,2,8,16,128]{4,3,2,1,0:T(8,128)(2,1)}), bf16[16,2,8,16,128]{4,3,2,1,0:T(8,128)(2,1)S(1)}, u32[]{:S(2)}, u32[]{:S(2)}) async-start(bf16[16,2,8,16,128]{4,3,2,1,0:T(8,128)(2,1)} %get-tuple-element.20), calls=%async_computation | async-start | bytes 2097152 | tf_op jit(solution)/shard_map/all_to_all | solution.py:323
  10.4 1.2 %split_weight.1 = (bf16[256,512]{1,0:T(8,128)(2,1)}, bf16[256,512]{1,0:T(8,128)(2,1)}, bf16[256,512]{1,0:T(8,128)(2,1)S(1)}, bf16[256,512]{1,0:T(8,128)(2,1)S(1)...) custom-call(bf16[256,4096]{1,0:T(8,128)(2,1)S(1)} %copy-done, ...), custom_call_target="tpu_custom_call" | custom-call | tf_op jit(solution)/shard_map/split_weight/pallas_call | solution.py:234
  12.3 2.5 %collective-permute-start.2 = (bf16[256,512]{1,0:T(8,128)(2,1)S(1)}, bf16[256,512]{1,0:T(8,128)(2,1)S(1)}, u32[]{:S(2)}, u32[]{:S(2)}) collective-permute-start(bf16[256,512]{1,0:T(8,128)(2,1)S(1)} %get-tuple-element.24), channel_id=1, source_target_pairs={{0,3},{1,2},{2,5},{3,4},{4,7},{5,6},{6,1},{7,0},{8,11},{9,10},{10,... | collective-permute-start | bytes 786440 | tf_op jit(solution)/shard_map/ppermute | solution.py:215
  14.8 2.1 %collective-permute-start.3 = (bf16[256,512]{1,0:T(8,128)(2,1)S(1)}, bf16[256,512]{1,0:T(8,128)(2,1)S(1)}, u32[]{:S(2)}, u32[]{:S(2)}) collective-permute-start(bf16[256,512]{1,0:T(8,128)(2,1)S(1)} %get-tuple-element.25), channel_id=1, source_target_pairs={{0,7},{1,6},{2,1},{3,0},{4,3},{5,2},{6,5},{7,4},{8,15},{9,14},{10,... | collective-permute-start | bytes 786440 | tf_op jit(solution)/shard_map/ppermute | solution.py:215
  16.9 2.7 %collective-permute-start.1 = (bf16[256,512]{1,0:T(8,128)(2,1)}, bf16[256,512]{1,0:T(8,128)(2,1)S(1)}, u32[]{:S(2)}, u32[]{:S(2)}) collective-permute-start(bf16[256,512]{1,0:T(8,128)(2,1)} %get-tuple-element.23), channel_id=1, source_target_pairs={{0,6},{1,7},{2,0},{3,1},{4,2},{5,3},{6,4},{7,5},{8,14},{9,15},{10,... | collective-permute-start | bytes 786440 | tf_op jit(solution)/shard_map/ppermute | solution.py:215
  20.2 3.8 %collective-permute-done.2.refs_2_.refs_10_.refs_12_ = bf16[256,512]{1,0:T(8,128)(2,1)S(1)} collective-permute-done((bf16[256,512]{1,0:T(8,128)(2,1)S(1)}, bf16[256,512]{1,0:T(8,128)(2,1)S(1)}, u32[]{:S(2)}, u32[]{:S(2)}) %collective-permute-start.2) | collective-permute-done | bytes 262176 | tf_op jit(solution)/shard_map/ppermute | solution.py:215
  24.1 1.3 %collective-permute-start.5 = (bf16[256,512]{1,0:T(8,128)(2,1)}, bf16[256,512]{1,0:T(8,128)(2,1)S(1)}, u32[]{:S(2)}, u32[]{:S(2)}) collective-permute-start(bf16[256,512]{1,0:T(8,128)(2,1)} %get-tuple-element.27), channel_id=1, source_target_pairs={{0,5},{1,4},{2,7},{3,6},{4,1},{5,0},{6,3},{7,2},{8,13},{9,12},{10,... | collective-permute-start | bytes 786440 | tf_op jit(solution)/shard_map/ppermute | solution.py:215
  25.4 1.0 %all-to-all-done.data = bf16[16,2,8,16,128]{4,3,2,1,0:T(8,128)(2,1)S(1)} async-done(((bf16[16,2,8,16,128]{4,3,2,1,0:T(8,128)(2,1)}), bf16[16,2,8,16,128]{4,3,2,1,0:T(8,128)(2,1)S(1)}, u32[]{:S(2)}, u32[]{:S(2)}) %all-to-all-start) | async-done | bytes 1048608 | tf_op jit(solution)/shard_map/all_to_all | solution.py:323
  26.4 1.2 %copy-done.19 = bf16[2176,256]{1,0:T(8,128)(2,1)S(1)} copy-done((bf16[2176,256]{1,0:T(8,128)(2,1)S(1)}, bf16[2176,256]{1,0:T(8,128)(2,1)}, u32[]{:S(2)}) %copy-start.19) | copy-done | bytes 1114136
  27.6 7.8 %convolve.1 = bf16[16,8,16,128]{3,2,1,0:T(8,128)(2,1)} custom-call(bf16[16,2,8,16,128]{4,3,2,1,0:T(8,128)(2,1)S(1)} %all-to-all-done.data, bf16[2176,256]{1,0:T(8,128)(2,1)S(1)} %copy-done.19, f32[256,128]{1,0:T(8,128)S(1)} %copy-done.20), custom_call_target="tpu_custom_call" | custom-call | flops 10000000000 | bytes 4194304 | tf_op jit(solution)/shard_map/convolve/pallas_call | solution.py:153
  35.5 5.9 %all-to-all-start.1 = ((bf16[16,8,16,128]{3,2,1,0:T(8,128)(2,1)}), bf16[16,8,16,128]{3,2,1,0:T(8,128)(2,1)S(1)}, u32[]{:S(2)}, u32[]{:S(2)}) async-start(bf16[16,8,16,128]{3,2,1,0:T(8,128)(2,1)} %convolve.1), calls=%async_computation.1 | async-start | bytes 1048576 | tf_op jit(solution)/shard_map/all_to_all | solution.py:326
  44.2 0.9 %copy-done.5 = bf16[256,512]{1,0:T(8,128)(2,1)S(1)} copy-done((bf16[256,512]{1,0:T(8,128)(2,1)S(1)}, bf16[256,512]{1,0:T(8,128)(2,1)}, u32[]{:S(2)}) %copy-start.5) | copy-done | bytes 262168
  49.0 2.9 %all-to-all-done.1.conv = bf16[16,8,16,128]{3,2,1,0:T(8,128)(2,1)S(1)} async-done(((bf16[16,8,16,128]{3,2,1,0:T(8,128)(2,1)}), bf16[16,8,16,128]{3,2,1,0:T(8,128)(2,1)S(1)}, u32[]{:S(2)}, u32[]{:S(2)}) %all-to-all-start.1) | async-done | bytes 524320 | tf_op jit(solution)/shard_map/all_to_all | solution.py:326
  53.2 2.1 %collective-permute-start.13 = (bf16[512,256]{1,0:T(8,128)(2,1)S(1)}, bf16[512,256]{1,0:T(8,128)(2,1)S(1)}, u32[]{:S(2)}, u32[]{:S(2)}) collective-permute-start(bf16[512,256]{1,0:T(8,128)(2,1)S(1)} %get-tuple-element.31.refs_4_), channel_id=1, source_target_pairs={{0,6},{1,7},{2,0},{3,1},{4,2},{5,3},{6,4},{7,5},{8,14},{9,15},{10,... | collective-permute-start | bytes 786440 | tf_op jit(solution)/shard_map/ppermute | solution.py:215
  55.3 1.4 %collective-permute-start.15 = (bf16[512,256]{1,0:T(8,128)(2,1)S(1)}, bf16[512,256]{1,0:T(8,128)(2,1)S(1)}, u32[]{:S(2)}, u32[]{:S(2)}) collective-permute-start(bf16[512,256]{1,0:T(8,128)(2,1)S(1)} %get-tuple-element.31.refs_4_), channel_id=1, source_target_pairs={{0,2},{1,3},{2,4},{3,5},{4,6},{5,7},{6,0},{7,1},{8,10},{9,11},{10,... | collective-permute-start | bytes 786440 | tf_op jit(solution)/shard_map/ppermute | solution.py:215
  56.7 2.9 %collective-permute-done.8.refs_1_ = bf16[512,256]{1,0:T(8,128)(2,1)S(1)} collective-permute-done((bf16[512,256]{1,0:T(8,128)(2,1)S(1)}, bf16[512,256]{1,0:T(8,128)(2,1)S(1)}, u32[]{:S(2)}, u32[]{:S(2)}) %collective-permute-start.8) | collective-permute-done | bytes 262176 | tf_op jit(solution)/shard_map/ppermute | solution.py:215
  59.7 5.3 %collective-permute-start.11 = (bf16[512,256]{1,0:T(8,128)(2,1)S(1)}, bf16[512,256]{1,0:T(8,128)(2,1)S(1)}, u32[]{:S(2)}, u32[]{:S(2)}) collective-permute-start(bf16[512,256]{1,0:T(8,128)(2,1)S(1)} %collective-permute-done.8.refs_1_), channel_id=1, source_target_pairs={{0,1},{1,0},{2,3},{3,2},{4,5},{5,4},{6,7},{7,6},{8,9},{9,8},{10,11... | collective-permute-start | bytes 786440 | tf_op jit(solution)/shard_map/ppermute | solution.py:215
  65.5 2.7 %collective-permute-start.18 = (bf16[512,256]{1,0:T(8,128)(2,1)S(1)}, bf16[512,256]{1,0:T(8,128)(2,1)S(1)}, u32[]{:S(2)}, u32[]{:S(2)}) collective-permute-start(bf16[512,256]{1,0:T(8,128)(2,1)S(1)} %collective-permute-done.13.refs_5_), channel_id=1, source_target_pairs={{0,6},{1,7},{2,0},{3,1},{4,2},{5,3},{6,4},{7,5},{8,14},{9,15},{10,... | collective-permute-start | bytes 786440 | tf_op jit(solution)/shard_map/ppermute | solution.py:215
  68.2 2.9 %collective-permute-start.7 = (bf16[512,256]{1,0:T(8,128)(2,1)S(1)}, bf16[512,256]{1,0:T(8,128)(2,1)S(1)}, u32[]{:S(2)}, u32[]{:S(2)}) collective-permute-start(bf16[512,256]{1,0:T(8,128)(2,1)S(1)} %get-tuple-element.30.refs_0_), channel_id=1, source_target_pairs={{0,1},{1,0},{2,3},{3,2},{4,5},{5,4},{6,7},{7,6},{8,9},{9,8},{10,11... | collective-permute-start | bytes 786440 | tf_op jit(solution)/shard_map/ppermute | solution.py:215
  71.1 1.2 %fold.1 = (f32[1024,512]{1,0:T(8,128)S(1)}, bf16[512,256]{1,0:T(8,128)(2,1)S(1)}, bf16[512,256]{1,0:T(8,128)(2,1)S(1)}) custom-call(bf16[512,256]{1,0:T(8,128)(2,1)S(1)} %get-tuple-element.30.refs_0_, bf16[512,256]{1,0:T(8,128)(2,1)S(1)} %collective-permute-done.8.refs_1_, bf16[512,256]{1,0:T(8,128)(2,1)S(1)} %collective-permute-done.11.refs_2_, ...), custom_call_target="tpu_custom_call" | custom-call | tf_op jit(solution)/shard_map/fold/pallas_call | solution.py:282
  73.0 2.5 %collective-permute-start.10 = (bf16[512,256]{1,0:T(8,128)(2,1)S(1)}, bf16[512,256]{1,0:T(8,128)(2,1)S(1)}, u32[]{:S(2)}, u32[]{:S(2)}) collective-permute-start(bf16[512,256]{1,0:T(8,128)(2,1)S(1)} %collective-permute-done.9.refs_1_), channel_id=1, source_target_pairs={{0,1},{1,0},{2,3},{3,2},{4,5},{5,4},{6,7},{7,6},{8,9},{9,8},{10,11... | collective-permute-start | bytes 786440 | tf_op jit(solution)/shard_map/ppermute | solution.py:215
  75.5 1.1 %collective-permute-done.10.refs_2_ = bf16[512,256]{1,0:T(8,128)(2,1)S(1)} collective-permute-done((bf16[512,256]{1,0:T(8,128)(2,1)S(1)}, bf16[512,256]{1,0:T(8,128)(2,1)S(1)}, u32[]{:S(2)}, u32[]{:S(2)}) %collective-permute-start.10) | collective-permute-done | bytes 262176 | tf_op jit(solution)/shard_map/ppermute | solution.py:215
  77.0 2.2 %project.1 = bf16[1024,512]{1,0:T(8,128)(2,1)} custom-call(bf16[512,256]{1,0:T(8,128)(2,1)S(1)} %collective-permute-done.7.refs_0_, bf16[512,256]{1,0:T(8,128)(2,1)S(1)} %collective-permute-done.9.refs_1_, bf16[512,256]{1,0:T(8,128)(2,1)S(1)} %collective-permute-done.10.refs_2_, bf16[512,256]{1,0:T(8,128)(2,1)S(1)} %collective-permute-done.16.refs_3_, ...), custom_call_target="tpu_custom_call" | custom-call | tf_op jit(solution)/shard_map/project/pallas_call | solution.py:310
  (71 shorter events, 10.2 us)
Async XLA Ops:
  2.7 23.7 %copy-start.20 = (f32[256,128]{1,0:T(8,128)S(1)}, f32[256,128]{1,0:T(8,128)}, u32[]{:S(2)}) copy-start(f32[256,128]{1,0:T(8,128)} %constant.5.clone.twists) | copy-start | bytes 393220
  2.7 23.7 %all-to-all-start = ((bf16[16,2,8,16,128]{4,3,2,1,0:T(8,128)(2,1)}), bf16[16,2,8,16,128]{4,3,2,1,0:T(8,128)(2,1)S(1)}, u32[]{:S(2)}, u32[]{:S(2)}) async-start(bf16[16,2,8,16,128]{4,3,2,1,0:T(8,128)(2,1)} %get-tuple-element.20), calls=%async_computation | async-start | bytes 2097152 | tf_op jit(solution)/shard_map/all_to_all | solution.py:323
  12.3 11.8 %collective-permute-start.2 = (bf16[256,512]{1,0:T(8,128)(2,1)S(1)}, bf16[256,512]{1,0:T(8,128)(2,1)S(1)}, u32[]{:S(2)}, u32[]{:S(2)}) collective-permute-start(bf16[256,512]{1,0:T(8,128)(2,1)S(1)} %get-tuple-element.24), channel_id=1, source_target_pairs={{0,3},{1,2},{2,5},{3,4},{4,7},{5,6},{6,1},{7,0},{8,11},{9,10},{10,... | collective-permute-start | bytes 786440 | tf_op jit(solution)/shard_map/ppermute | solution.py:215
  14.8 10.6 %collective-permute-start.3 = (bf16[256,512]{1,0:T(8,128)(2,1)S(1)}, bf16[256,512]{1,0:T(8,128)(2,1)S(1)}, u32[]{:S(2)}, u32[]{:S(2)}) collective-permute-start(bf16[256,512]{1,0:T(8,128)(2,1)S(1)} %get-tuple-element.25), channel_id=1, source_target_pairs={{0,7},{1,6},{2,1},{3,0},{4,3},{5,2},{6,5},{7,4},{8,15},{9,14},{10,... | collective-permute-start | bytes 786440 | tf_op jit(solution)/shard_map/ppermute | solution.py:215
  16.9 24.4 %collective-permute-start = (bf16[256,512]{1,0:T(8,128)(2,1)}, bf16[256,512]{1,0:T(8,128)(2,1)S(1)}, u32[]{:S(2)}, u32[]{:S(2)}) collective-permute-start(bf16[256,512]{1,0:T(8,128)(2,1)} %get-tuple-element.22), channel_id=1, source_target_pairs={{0,2},{1,3},{2,4},{3,5},{4,6},{5,7},{6,0},{7,1},{8,10},{9,11},{10,... | collective-permute-start | bytes 786440 | tf_op jit(solution)/shard_map/ppermute | solution.py:215
  16.9 25.2 %collective-permute-start.1 = (bf16[256,512]{1,0:T(8,128)(2,1)}, bf16[256,512]{1,0:T(8,128)(2,1)S(1)}, u32[]{:S(2)}, u32[]{:S(2)}) collective-permute-start(bf16[256,512]{1,0:T(8,128)(2,1)} %get-tuple-element.23), channel_id=1, source_target_pairs={{0,6},{1,7},{2,0},{3,1},{4,2},{5,3},{6,4},{7,5},{8,14},{9,15},{10,... | collective-permute-start | bytes 786440 | tf_op jit(solution)/shard_map/ppermute | solution.py:215
  19.6 23.2 %collective-permute-start.4 = (bf16[256,512]{1,0:T(8,128)(2,1)}, bf16[256,512]{1,0:T(8,128)(2,1)S(1)}, u32[]{:S(2)}, u32[]{:S(2)}) collective-permute-start(bf16[256,512]{1,0:T(8,128)(2,1)} %get-tuple-element.26), channel_id=1, source_target_pairs={{0,4},{1,5},{2,6},{3,7},{4,0},{5,1},{6,2},{7,3},{8,12},{9,13},{10,... | collective-permute-start | bytes 786440 | tf_op jit(solution)/shard_map/ppermute | solution.py:215
  24.1 18.7 %collective-permute-start.5 = (bf16[256,512]{1,0:T(8,128)(2,1)}, bf16[256,512]{1,0:T(8,128)(2,1)S(1)}, u32[]{:S(2)}, u32[]{:S(2)}) collective-permute-start(bf16[256,512]{1,0:T(8,128)(2,1)} %get-tuple-element.27), channel_id=1, source_target_pairs={{0,5},{1,4},{2,7},{3,6},{4,1},{5,0},{6,3},{7,2},{8,13},{9,12},{10,... | collective-permute-start | bytes 786440 | tf_op jit(solution)/shard_map/ppermute | solution.py:215
  25.4 18.1 %collective-permute-start.6 = (bf16[256,512]{1,0:T(8,128)(2,1)}, bf16[256,512]{1,0:T(8,128)(2,1)S(1)}, u32[]{:S(2)}, u32[]{:S(2)}) collective-permute-start(bf16[256,512]{1,0:T(8,128)(2,1)} %get-tuple-element.28), channel_id=1, source_target_pairs={{0,1},{1,0},{2,3},{3,2},{4,5},{5,4},{6,7},{7,6},{8,9},{9,8},{10,11... | collective-permute-start | bytes 786440 | tf_op jit(solution)/shard_map/ppermute | solution.py:215
  35.5 16.4 %all-to-all-start.1 = ((bf16[16,8,16,128]{3,2,1,0:T(8,128)(2,1)}), bf16[16,8,16,128]{3,2,1,0:T(8,128)(2,1)S(1)}, u32[]{:S(2)}, u32[]{:S(2)}) async-start(bf16[16,8,16,128]{3,2,1,0:T(8,128)(2,1)} %convolve.1), calls=%async_computation.1 | async-start | bytes 1048576 | tf_op jit(solution)/shard_map/all_to_all | solution.py:326
  52.5 7.2 %collective-permute-start.8 = (bf16[512,256]{1,0:T(8,128)(2,1)S(1)}, bf16[512,256]{1,0:T(8,128)(2,1)S(1)}, u32[]{:S(2)}, u32[]{:S(2)}) collective-permute-start(bf16[512,256]{1,0:T(8,128)(2,1)S(1)} %get-tuple-element.30.refs_0_), channel_id=1, source_target_pairs={{0,2},{1,3},{2,4},{3,5},{4,6},{5,7},{6,0},{7,1},{8,10},{9,11},{10,... | collective-permute-start | bytes 786440 | tf_op jit(solution)/shard_map/ppermute | solution.py:215
  53.2 11.8 %collective-permute-start.13 = (bf16[512,256]{1,0:T(8,128)(2,1)S(1)}, bf16[512,256]{1,0:T(8,128)(2,1)S(1)}, u32[]{:S(2)}, u32[]{:S(2)}) collective-permute-start(bf16[512,256]{1,0:T(8,128)(2,1)S(1)} %get-tuple-element.31.refs_4_), channel_id=1, source_target_pairs={{0,6},{1,7},{2,0},{3,1},{4,2},{5,3},{6,4},{7,5},{8,14},{9,15},{10,... | collective-permute-start | bytes 786440 | tf_op jit(solution)/shard_map/ppermute | solution.py:215
  55.3 10.2 %collective-permute-start.12 = (bf16[512,256]{1,0:T(8,128)(2,1)S(1)}, bf16[512,256]{1,0:T(8,128)(2,1)S(1)}, u32[]{:S(2)}, u32[]{:S(2)}) collective-permute-start(bf16[512,256]{1,0:T(8,128)(2,1)S(1)} %get-tuple-element.30.refs_0_), channel_id=1, source_target_pairs={{0,6},{1,7},{2,0},{3,1},{4,2},{5,3},{6,4},{7,5},{8,14},{9,15},{10,... | collective-permute-start | bytes 786440 | tf_op jit(solution)/shard_map/ppermute | solution.py:215
  55.3 10.1 %collective-permute-start.15 = (bf16[512,256]{1,0:T(8,128)(2,1)S(1)}, bf16[512,256]{1,0:T(8,128)(2,1)S(1)}, u32[]{:S(2)}, u32[]{:S(2)}) collective-permute-start(bf16[512,256]{1,0:T(8,128)(2,1)S(1)} %get-tuple-element.31.refs_4_), channel_id=1, source_target_pairs={{0,2},{1,3},{2,4},{3,5},{4,6},{5,7},{6,0},{7,1},{8,10},{9,11},{10,... | collective-permute-start | bytes 786440 | tf_op jit(solution)/shard_map/ppermute | solution.py:215
  59.7 8.5 %collective-permute-start.11 = (bf16[512,256]{1,0:T(8,128)(2,1)S(1)}, bf16[512,256]{1,0:T(8,128)(2,1)S(1)}, u32[]{:S(2)}, u32[]{:S(2)}) collective-permute-start(bf16[512,256]{1,0:T(8,128)(2,1)S(1)} %collective-permute-done.8.refs_1_), channel_id=1, source_target_pairs={{0,1},{1,0},{2,3},{3,2},{4,5},{5,4},{6,7},{7,6},{8,9},{9,8},{10,11... | collective-permute-start | bytes 786440 | tf_op jit(solution)/shard_map/ppermute | solution.py:215
  65.0 6.1 %collective-permute-start.14 = (bf16[512,256]{1,0:T(8,128)(2,1)S(1)}, bf16[512,256]{1,0:T(8,128)(2,1)S(1)}, u32[]{:S(2)}, u32[]{:S(2)}) collective-permute-start(bf16[512,256]{1,0:T(8,128)(2,1)S(1)} %collective-permute-done.13.refs_5_), channel_id=1, source_target_pairs={{0,1},{1,0},{2,3},{3,2},{4,5},{5,4},{6,7},{7,6},{8,9},{9,8},{10,11... | collective-permute-start | bytes 786440 | tf_op jit(solution)/shard_map/ppermute | solution.py:215
  65.0 7.5 %collective-permute-start.17 = (bf16[512,256]{1,0:T(8,128)(2,1)S(1)}, bf16[512,256]{1,0:T(8,128)(2,1)S(1)}, u32[]{:S(2)}, u32[]{:S(2)}) collective-permute-start(bf16[512,256]{1,0:T(8,128)(2,1)S(1)} %get-tuple-element.31.refs_4_), channel_id=1, source_target_pairs={{0,1},{1,0},{2,3},{3,2},{4,5},{5,4},{6,7},{7,6},{8,9},{9,8},{10,11... | collective-permute-start | bytes 786440 | tf_op jit(solution)/shard_map/ppermute | solution.py:215
  65.5 7.5 %collective-permute-start.9 = (bf16[512,256]{1,0:T(8,128)(2,1)S(1)}, bf16[512,256]{1,0:T(8,128)(2,1)S(1)}, u32[]{:S(2)}, u32[]{:S(2)}) collective-permute-start(bf16[512,256]{1,0:T(8,128)(2,1)S(1)} %collective-permute-done.8.refs_1_), channel_id=1, source_target_pairs={{0,2},{1,3},{2,4},{3,5},{4,6},{5,7},{6,0},{7,1},{8,10},{9,11},{10,... | collective-permute-start | bytes 786440 | tf_op jit(solution)/shard_map/ppermute | solution.py:215
  65.5 10.0 %collective-permute-start.18 = (bf16[512,256]{1,0:T(8,128)(2,1)S(1)}, bf16[512,256]{1,0:T(8,128)(2,1)S(1)}, u32[]{:S(2)}, u32[]{:S(2)}) collective-permute-start(bf16[512,256]{1,0:T(8,128)(2,1)S(1)} %collective-permute-done.13.refs_5_), channel_id=1, source_target_pairs={{0,6},{1,7},{2,0},{3,1},{4,2},{5,3},{6,4},{7,5},{8,14},{9,15},{10,... | collective-permute-start | bytes 786440 | tf_op jit(solution)/shard_map/ppermute | solution.py:215
  68.2 7.3 %collective-permute-start.7 = (bf16[512,256]{1,0:T(8,128)(2,1)S(1)}, bf16[512,256]{1,0:T(8,128)(2,1)S(1)}, u32[]{:S(2)}, u32[]{:S(2)}) collective-permute-start(bf16[512,256]{1,0:T(8,128)(2,1)S(1)} %get-tuple-element.30.refs_0_), channel_id=1, source_target_pairs={{0,1},{1,0},{2,3},{3,2},{4,5},{5,4},{6,7},{7,6},{8,9},{9,8},{10,11... | collective-permute-start | bytes 786440 | tf_op jit(solution)/shard_map/ppermute | solution.py:215
  72.4 3.1 %collective-permute-start.16 = (bf16[512,256]{1,0:T(8,128)(2,1)S(1)}, bf16[512,256]{1,0:T(8,128)(2,1)S(1)}, u32[]{:S(2)}, u32[]{:S(2)}) collective-permute-start(bf16[512,256]{1,0:T(8,128)(2,1)S(1)} %get-tuple-element.32), channel_id=1, source_target_pairs={{0,1},{1,0},{2,3},{3,2},{4,5},{5,4},{6,7},{7,6},{8,9},{9,8},{10,11... | collective-permute-start | bytes 786440 | tf_op jit(solution)/shard_map/ppermute | solution.py:215
  72.5 3.0 %collective-permute-start.20 = (bf16[512,256]{1,0:T(8,128)(2,1)S(1)}, bf16[512,256]{1,0:T(8,128)(2,1)S(1)}, u32[]{:S(2)}, u32[]{:S(2)}) collective-permute-start(bf16[512,256]{1,0:T(8,128)(2,1)S(1)} %get-tuple-element.33), channel_id=1, source_target_pairs={{0,1},{1,0},{2,3},{3,2},{4,5},{5,4},{6,7},{7,6},{8,9},{9,8},{10,11... | collective-permute-start | bytes 786440 | tf_op jit(solution)/shard_map/ppermute | solution.py:215
  73.0 3.6 %collective-permute-start.10 = (bf16[512,256]{1,0:T(8,128)(2,1)S(1)}, bf16[512,256]{1,0:T(8,128)(2,1)S(1)}, u32[]{:S(2)}, u32[]{:S(2)}) collective-permute-start(bf16[512,256]{1,0:T(8,128)(2,1)S(1)} %collective-permute-done.9.refs_1_), channel_id=1, source_target_pairs={{0,1},{1,0},{2,3},{3,2},{4,5},{5,4},{6,7},{7,6},{8,9},{9,8},{10,11... | collective-permute-start | bytes 786440 | tf_op jit(solution)/shard_map/ppermute | solution.py:215
  75.4 1.5 %collective-permute-start.19 = (bf16[512,256]{1,0:T(8,128)(2,1)S(1)}, bf16[512,256]{1,0:T(8,128)(2,1)S(1)}, u32[]{:S(2)}, u32[]{:S(2)}) collective-permute-start(bf16[512,256]{1,0:T(8,128)(2,1)S(1)} %collective-permute-done.18.refs_5_), channel_id=1, source_target_pairs={{0,1},{1,0},{2,3},{3,2},{4,5},{5,4},{6,7},{7,6},{8,9},{9,8},{10,11... | collective-permute-start | bytes 786440 | tf_op jit(solution)/shard_map/ppermute | solution.py:215
  (20 other events, 97.1 us)

commit v5 on v4

--- a/solution.py
+++ b/solution.py
@@ -91,27 +91,52 @@
     )(gate_in, value_in, taps)
 
 
-def conv_kernel(group, data, turns, twists, out, signal, taps, total):
+def unpack_kernel(data, *rest):
+    out, signal, taps = rest[-3:]
     shards, _, blocks, channels, _ = data.shape
+    rows = blocks * channels
+
+    @pl.loop(0, shards)
+    def _(a):
+        part = pl.ds(pl.multiple_of(a * rows, rows), rows)
+        signal[part, :] = data[a, 0].astype(F32).reshape(rows, TILE)
+        taps[part, :] = data[a, 1].astype(F32).reshape(rows, TILE)
+
+    for c in range(channels):
+        pick = pl.ds(c, TILE, stride=channels)
+        out[c] = jnp.concatenate([signal[pick, :], taps[pick, :]], 1).astype(BF16)
+
+
+def unpack(data, after):
+    shards, _, blocks, channels, _ = data.shape
+    whole = pltpu.VMEM((shards * blocks * channels, TILE), F32)
+    space = pl.BlockSpec(memory_space=pltpu.VMEM)
+    return pl.pallas_call(
+        unpack_kernel,
+        in_specs=[space] + [pl.BlockSpec(memory_space=pl.ANY)] * len(after),
+        out_specs=space,
+        out_shape=jax.ShapeDtypeStruct((channels, TILE, 2 * TILE), BF16),
+        scratch_shapes=[whole] * 2,
+        compiler_params=pltpu.CompilerParams(vmem_limit_bytes=8 << 20),
+        name="unpack",
+    )(data, *after)
+
+
+def conv_kernel(group, pairs, turns, twists, out, total):
+    shards, blocks, channels, _ = out.shape
     rows = blocks * channels
     span = 2 * TILE
     first, second, back = turns.at[:span], turns.at[span : 4 * span], turns.at[4 * span : 7 * span]
     cosine, sine = twists.at[:TILE], twists.at[TILE:]
     last = [turns[7 * span + k * TILE : 7 * span + (k + 1) * TILE, :] for k in range(3)]
 
-    @pl.loop(0, shards)
-    def _(a):
-        part = pl.ds(pl.multiple_of(a * rows, rows), rows)
-        signal[part, :] = data[a, 0].astype(F32).reshape(rows, TILE)
-        taps[part, :] = data[a, 1].astype(F32).reshape(rows, TILE)
-
     @pl.loop(0, channels // group)
     def _(step):
         cos, sin = cosine[...], sine[...]
         picks = [pl.ds(step * group + g, TILE, stride=channels) for g in range(group)]
         pieces = []
-        for pick in picks:
-            pair = jnp.concatenate([signal[pick, :], taps[pick, :]], 1).astype(BF16)
+        for g in range(group):
+            pair = pairs[step * group + g]
             lifted = matmul(first[...], jnp.concatenate([pair, pair], 0))
             for side in range(2):
                 real = lifted[:TILE, side * TILE : (side + 1) * TILE]
@@ -146,20 +171,19 @@
         out[a] = total[part, :].astype(BF16).reshape(blocks, channels, TILE)
 
 
-def convolve(data, group=8):
-    shards, _, blocks, channels, _ = data.shape
-    whole = pltpu.VMEM((shards * blocks * channels, TILE), F32)
+def convolve(pairs, blocks, group=8):
+    channels, rows, _ = pairs.shape
     space = pl.BlockSpec(memory_space=pltpu.VMEM)
     return pl.pallas_call(
         functools.partial(conv_kernel, group),
         in_specs=[space] * 3,
         out_specs=space,
-        out_shape=jax.ShapeDtypeStruct((shards, blocks, channels, TILE), BF16),
-        scratch_shapes=[whole] * 3,
+        out_shape=jax.ShapeDtypeStruct((rows // blocks, blocks, channels, TILE), BF16),
+        scratch_shapes=[pltpu.VMEM((rows * channels, TILE), F32)],
         compiler_params=pltpu.CompilerParams(vmem_limit_bytes=28 << 20),
         cost_estimate=pl.CostEstimate(flops=10**10, bytes_accessed=1 << 22, transcendentals=0),
         name="convolve",
-    )(data, *(jnp.asarray(table) for table in tables()))
+    )(pairs, *(jnp.asarray(table) for table in tables()))
 
 
 def mix_kernel(start, conv, gate_out, gate_in, value_in, skip, _, top, low):
@@ -285,6 +309,7 @@
         out_specs=[space] * 3,
         out_shape=[jax.ShapeDtypeStruct((2 * rows, features), F32), piece, piece],
         compiler_params=pltpu.CompilerParams(vmem_limit_bytes=12 << 20),
+        cost_estimate=pl.CostEstimate(flops=0, bytes_accessed=0, transcendentals=0),
         name="fold",
     )(*top, *low, *weight)
 
@@ -323,7 +348,7 @@
     data = lax.all_to_all(packed, "seq", split_axis=0, concat_axis=0, tiled=True)
     weight = split_weight(out_weight, token)
     weight = [toward(w, *route) if any(route) else w for w, route in zip(weight, ROUTES)]
-    conv = lax.all_to_all(convolve(data), "seq", split_axis=0, concat_axis=0, tiled=True)
+    conv = lax.all_to_all(convolve(unpack(data, weight[:2]), packed.shape[2]), "seq", split_axis=0, concat_axis=0, tiled=True)
     top, low = mix(resume_at, conv, gate_out, gate_in, value_in, skip_bias, mark(weight))
     up_top, down_low = toward(top, 1, 0), toward(low, 3, 0)
     up_low, down_top = toward(low, 1, 0), toward(top, 3, 0)

time: 79.7 us -> 79.8 us (level)
  local copies, waits for them, and re-layouts: 9.56 us -> 5.2 us
  starting transfers between devices: 40.8 us -> 45 us
    unnamed x42 -> x34, local copies, waits for them, and re-layouts: 9.56 us -> 5.2 us
    ppermute x21, starting transfers between devices: 27.2 us -> 30.7 us  [toward(): return lax.ppermute(array, 'chan', pairs)]
    all_to_all x1, waiting for transfers between devices: 2.93 us -> 6.21 us  [on_device(): lax.all_to_all(convolve(unpack(data, weight[:2]), packed.shape[2]), 'seq'...]
    ppermute x21, waiting for transfers between devices: 8.33 us -> 5.5 us  [toward(): return lax.ppermute(array, 'chan', pairs)]
    pallas_call x0 -> x1, Pallas kernels: none -> 1.04 us  [unpack(): pl.pallas_call(unpack_kernel, in_specs=[space] + [pl.BlockSpec(memory_spa...]
  transfers between devices with their start and end apart: 23 -> 23, of which waited for: 6 -> 6; matrix products, arithmetic and copies ran while one was open for 0% -> 0% of each run, Pallas kernels for 13% -> 14%
where the time goes in v5:
time: 79.8 us; the launch traced here: 79.4 us
  starting transfers between devices  45 us (56%)
  Pallas kernels  16.2 us (20%)
  waiting for transfers between devices  12.1 us (15%)
  local copies, waits for them, and re-layouts  5.2 us (7%)
  between operations  0.85 us (1%)
    ppermute x21, starting transfers between devices, toward(): return lax.ppermute(array, 'chan', pairs)  30.7 us
    all_to_all x1, starting transfers between devices, on_device(): lax.all_to_all(packed, 'seq', split_axis=0, concat_axis=0, tiled=True)  7.72 us
    pallas_call x1, Pallas kernels, convolve(): pl.pallas_call(functools.partial(conv_kernel, group), in_specs=[space] *...  7.28 us
    all_to_all x1, starting transfers between devices, on_device(): lax.all_to_all(convolve(unpack(data, weight[:2]), packed.shape[2]), 'seq'...  6.59 us
    all_to_all x1, waiting for transfers between devices, on_device(): lax.all_to_all(convolve(unpack(data, weight[:2]), packed.shape[2]), 'seq'...  6.21 us
    ppermute x21, waiting for transfers between devices, toward(): return lax.ppermute(array, 'chan', pairs)  5.5 us
    unnamed x34, local copies, waits for them, and re-layouts  5.2 us
    pallas_call x1, Pallas kernels, pack(): pl.pallas_call(pack_kernel, grid=(rows // (blocks * TILE),), in_specs=[bl...  2.66 us
  transfers between devices with their start and end apart: 23, of which 6 were waited for; matrix products, arithmetic and copies ran while one was open for 0% of the time, Pallas kernels for 14%

profile of v5, /device:TPU:1, one launch (start us, length us, event | category | flops | bytes accessed | tf_op | source)
XLA Modules:
  0.0 79.4 jit_solution(649039593814861033)
XLA Ops:
  0.0 2.7 %pack.1 = (bf16[16,2,8,16,128]{4,3,2,1,0:T(8,128)(2,1)}, f32[8,128]{1,0:T(8,128)}) custom-call(bf16[1024,256]{1,0:T(8,128)(2,1)} %gate_in.3, bf16[1024,256]{1,0:T(8,128)(2,1)} %value_in.3, f32[1024,256]{1,0:T(8,128)} %taps.1), custom_call_target="tpu_custom_call" | custom-call | tf_op jit(solution)/shard_map/pack/pallas_call | solution.py:78
  2.7 7.7 %all-to-all-start = ((bf16[16,2,8,16,128]{4,3,2,1,0:T(8,128)(2,1)}), bf16[16,2,8,16,128]{4,3,2,1,0:T(8,128)(2,1)S(1)}, u32[]{:S(2)}, u32[]{:S(2)}) async-start(bf16[16,2,8,16,128]{4,3,2,1,0:T(8,128)(2,1)} %get-tuple-element.20), calls=%async_computation | async-start | bytes 2097152 | tf_op jit(solution)/shard_map/all_to_all | solution.py:348
  10.4 1.2 %split_weight.1 = (bf16[256,512]{1,0:T(8,128)(2,1)S(1)}, bf16[256,512]{1,0:T(8,128)(2,1)S(1)}, bf16[256,512]{1,0:T(8,128)(2,1)}, bf16[256,512]{1,0:T(8,128)(2,1)...) custom-call(bf16[256,4096]{1,0:T(8,128)(2,1)S(1)} %copy-done, ...), custom_call_target="tpu_custom_call" | custom-call | tf_op jit(solution)/shard_map/split_weight/pallas_call | solution.py:258
  12.3 1.6 %collective-permute-start = (bf16[256,512]{1,0:T(8,128)(2,1)S(1)}, bf16[256,512]{1,0:T(8,128)(2,1)S(1)}, u32[]{:S(2)}, u32[]{:S(2)}) collective-permute-start(bf16[256,512]{1,0:T(8,128)(2,1)S(1)} %get-tuple-element.22), channel_id=1, source_target_pairs={{0,2},{1,3},{2,4},{3,5},{4,6},{5,7},{6,0},{7,1},{8,10},{9,11},{10,... | collective-permute-start | bytes 786440 | tf_op jit(solution)/shard_map/ppermute | solution.py:239
  14.0 2.1 %collective-permute-start.1 = (bf16[256,512]{1,0:T(8,128)(2,1)S(1)}, bf16[256,512]{1,0:T(8,128)(2,1)S(1)}, u32[]{:S(2)}, u32[]{:S(2)}) collective-permute-start(bf16[256,512]{1,0:T(8,128)(2,1)S(1)} %get-tuple-element.23), channel_id=1, source_target_pairs={{0,6},{1,7},{2,0},{3,1},{4,2},{5,3},{6,4},{7,5},{8,14},{9,15},{10,... | collective-permute-start | bytes 786440 | tf_op jit(solution)/shard_map/ppermute | solution.py:239
  16.8 2.2 %collective-permute-start.3 = (bf16[256,512]{1,0:T(8,128)(2,1)}, bf16[256,512]{1,0:T(8,128)(2,1)S(1)}, u32[]{:S(2)}, u32[]{:S(2)}) collective-permute-start(bf16[256,512]{1,0:T(8,128)(2,1)} %get-tuple-element.25), channel_id=1, source_target_pairs={{0,7},{1,6},{2,1},{3,0},{4,3},{5,2},{6,5},{7,4},{8,15},{9,14},{10,... | collective-permute-start | bytes 786440 | tf_op jit(solution)/shard_map/ppermute | solution.py:239
  19.1 1.1 %collective-permute-start.4 = (bf16[256,512]{1,0:T(8,128)(2,1)}, bf16[256,512]{1,0:T(8,128)(2,1)S(1)}, u32[]{:S(2)}, u32[]{:S(2)}) collective-permute-start(bf16[256,512]{1,0:T(8,128)(2,1)} %get-tuple-element.26), channel_id=1, source_target_pairs={{0,4},{1,5},{2,6},{3,7},{4,0},{5,1},{6,2},{7,3},{8,12},{9,13},{10,... | collective-permute-start | bytes 786440 | tf_op jit(solution)/shard_map/ppermute | solution.py:239
  20.8 1.0 %collective-permute-done.rest_0_.refs_0_.refs_9_ = bf16[256,512]{1,0:T(8,128)(2,1)S(1)} collective-permute-done((bf16[256,512]{1,0:T(8,128)(2,1)S(1)}, bf16[256,512]{1,0:T(8,128)(2,1)S(1)}, u32[]{:S(2)}, u32[]{:S(2)}) %collective-permute-start) | collective-permute-done | bytes 262176 | tf_op jit(solution)/shard_map/ppermute | solution.py:239
  21.8 4.2 %collective-permute-start.5 = (bf16[256,512]{1,0:T(8,128)(2,1)}, bf16[256,512]{1,0:T(8,128)(2,1)S(1)}, u32[]{:S(2)}, u32[]{:S(2)}) collective-permute-start(bf16[256,512]{1,0:T(8,128)(2,1)} %get-tuple-element.27), channel_id=1, source_target_pairs={{0,5},{1,4},{2,7},{3,6},{4,1},{5,0},{6,3},{7,2},{8,13},{9,12},{10,... | collective-permute-start | bytes 786440 | tf_op jit(solution)/shard_map/ppermute | solution.py:239
  26.4 1.0 %unpack.1.pairs = bf16[16,128,256]{2,1,0:T(8,128)(2,1)S(1)} custom-call(bf16[16,2,8,16,128]{4,3,2,1,0:T(8,128)(2,1)S(1)} %all-to-all-done.data, bf16[256,512]{1,0:T(8,128)(2,1)S(1)} %collective-permute-done.rest_0_.refs_0_.refs_9_, bf16[256,512]{1,0:T(8,128)(2,1)S(1)} %collective-permute-done.1.rest_1_.refs_1_.refs_11_), custom_call_target="tpu_custom_call" | custom-call | tf_op jit(solution)/shard_map/unpack/pallas_call | solution.py:114
  27.6 7.3 %convolve.1 = bf16[16,8,16,128]{3,2,1,0:T(8,128)(2,1)} custom-call(bf16[16,128,256]{2,1,0:T(8,128)(2,1)S(1)} %unpack.1.pairs, bf16[2176,256]{1,0:T(8,128)(2,1)S(1)} %copy-done.15, f32[256,128]{1,0:T(8,128)S(1)} %copy-done.16), custom_call_target="tpu_custom_call" | custom-call | flops 10000000000 | bytes 4194304 | tf_op jit(solution)/shard_map/convolve/pallas_call | solution.py:177
  34.9 6.6 %all-to-all-start.1 = ((bf16[16,8,16,128]{3,2,1,0:T(8,128)(2,1)}), bf16[16,8,16,128]{3,2,1,0:T(8,128)(2,1)S(1)}, u32[]{:S(2)}, u32[]{:S(2)}) async-start(bf16[16,8,16,128]{3,2,1,0:T(8,128)(2,1)} %convolve.1), calls=%async_computation.1 | async-start | bytes 1048576 | tf_op jit(solution)/shard_map/all_to_all | solution.py:351
  43.0 0.9 %copy-done.5 = bf16[256,512]{1,0:T(8,128)(2,1)S(1)} copy-done((bf16[256,512]{1,0:T(8,128)(2,1)S(1)}, bf16[256,512]{1,0:T(8,128)(2,1)}, u32[]{:S(2)}) %copy-start.5) | copy-done | bytes 262168
  45.8 6.2 %all-to-all-done.1.conv = bf16[16,8,16,128]{3,2,1,0:T(8,128)(2,1)S(1)} async-done(((bf16[16,8,16,128]{3,2,1,0:T(8,128)(2,1)}), bf16[16,8,16,128]{3,2,1,0:T(8,128)(2,1)S(1)}, u32[]{:S(2)}, u32[]{:S(2)}) %all-to-all-start.1) | async-done | bytes 524320 | tf_op jit(solution)/shard_map/all_to_all | solution.py:351
  53.5 1.9 %collective-permute-start.13 = (bf16[512,256]{1,0:T(8,128)(2,1)S(1)}, bf16[512,256]{1,0:T(8,128)(2,1)S(1)}, u32[]{:S(2)}, u32[]{:S(2)}) collective-permute-start(bf16[512,256]{1,0:T(8,128)(2,1)S(1)} %get-tuple-element.31.refs_4_), channel_id=1, source_target_pairs={{0,6},{1,7},{2,0},{3,1},{4,2},{5,3},{6,4},{7,5},{8,14},{9,15},{10,... | collective-permute-start | bytes 786440 | tf_op jit(solution)/shard_map/ppermute | solution.py:239
  55.4 1.4 %collective-permute-start.15 = (bf16[512,256]{1,0:T(8,128)(2,1)S(1)}, bf16[512,256]{1,0:T(8,128)(2,1)S(1)}, u32[]{:S(2)}, u32[]{:S(2)}) collective-permute-start(bf16[512,256]{1,0:T(8,128)(2,1)S(1)} %get-tuple-element.31.refs_4_), channel_id=1, source_target_pairs={{0,2},{1,3},{2,4},{3,5},{4,6},{5,7},{6,0},{7,1},{8,10},{9,11},{10,... | collective-permute-start | bytes 786440 | tf_op jit(solution)/shard_map/ppermute | solution.py:239
  56.9 2.9 %collective-permute-done.8.refs_1_ = bf16[512,256]{1,0:T(8,128)(2,1)S(1)} collective-permute-done((bf16[512,256]{1,0:T(8,128)(2,1)S(1)}, bf16[512,256]{1,0:T(8,128)(2,1)S(1)}, u32[]{:S(2)}, u32[]{:S(2)}) %collective-permute-start.8) | collective-permute-done | bytes 262176 | tf_op jit(solution)/shard_map/ppermute | solution.py:239
  59.8 5.3 %collective-permute-start.11 = (bf16[512,256]{1,0:T(8,128)(2,1)S(1)}, bf16[512,256]{1,0:T(8,128)(2,1)S(1)}, u32[]{:S(2)}, u32[]{:S(2)}) collective-permute-start(bf16[512,256]{1,0:T(8,128)(2,1)S(1)} %collective-permute-done.8.refs_1_), channel_id=1, source_target_pairs={{0,1},{1,0},{2,3},{3,2},{4,5},{5,4},{6,7},{7,6},{8,9},{9,8},{10,11... | collective-permute-start | bytes 786440 | tf_op jit(solution)/shard_map/ppermute | solution.py:239
  65.6 2.7 %collective-permute-start.18 = (bf16[512,256]{1,0:T(8,128)(2,1)S(1)}, bf16[512,256]{1,0:T(8,128)(2,1)S(1)}, u32[]{:S(2)}, u32[]{:S(2)}) collective-permute-start(bf16[512,256]{1,0:T(8,128)(2,1)S(1)} %collective-permute-done.13.refs_5_), channel_id=1, source_target_pairs={{0,6},{1,7},{2,0},{3,1},{4,2},{5,3},{6,4},{7,5},{8,14},{9,15},{10,... | collective-permute-start | bytes 786440 | tf_op jit(solution)/shard_map/ppermute | solution.py:239
  68.3 2.9 %collective-permute-start.7 = (bf16[512,256]{1,0:T(8,128)(2,1)S(1)}, bf16[512,256]{1,0:T(8,128)(2,1)S(1)}, u32[]{:S(2)}, u32[]{:S(2)}) collective-permute-start(bf16[512,256]{1,0:T(8,128)(2,1)S(1)} %get-tuple-element.30.refs_0_), channel_id=1, source_target_pairs={{0,1},{1,0},{2,3},{3,2},{4,5},{5,4},{6,7},{7,6},{8,9},{9,8},{10,11... | collective-permute-start | bytes 786440 | tf_op jit(solution)/shard_map/ppermute | solution.py:239
  71.3 1.2 %fold.1 = (f32[1024,512]{1,0:T(8,128)S(1)}, bf16[512,256]{1,0:T(8,128)(2,1)S(1)}, bf16[512,256]{1,0:T(8,128)(2,1)S(1)}) custom-call(bf16[512,256]{1,0:T(8,128)(2,1)S(1)} %get-tuple-element.30.refs_0_, bf16[512,256]{1,0:T(8,128)(2,1)S(1)} %collective-permute-done.8.refs_1_, bf16[512,256]{1,0:T(8,128)(2,1)S(1)} %collective-permute-done.11.refs_2_, ...), custom_call_target="tpu_custom_call" | custom-call | tf_op jit(solution)/shard_map/fold/pallas_call | solution.py:306
  73.1 2.5 %collective-permute-start.10 = (bf16[512,256]{1,0:T(8,128)(2,1)S(1)}, bf16[512,256]{1,0:T(8,128)(2,1)S(1)}, u32[]{:S(2)}, u32[]{:S(2)}) collective-permute-start(bf16[512,256]{1,0:T(8,128)(2,1)S(1)} %collective-permute-done.9.refs_1_), channel_id=1, source_target_pairs={{0,1},{1,0},{2,3},{3,2},{4,5},{5,4},{6,7},{7,6},{8,9},{9,8},{10,11... | collective-permute-start | bytes 786440 | tf_op jit(solution)/shard_map/ppermute | solution.py:239
  75.6 1.1 %collective-permute-done.10.refs_2_ = bf16[512,256]{1,0:T(8,128)(2,1)S(1)} collective-permute-done((bf16[512,256]{1,0:T(8,128)(2,1)S(1)}, bf16[512,256]{1,0:T(8,128)(2,1)S(1)}, u32[]{:S(2)}, u32[]{:S(2)}) %collective-permute-start.10) | collective-permute-done | bytes 262176 | tf_op jit(solution)/shard_map/ppermute | solution.py:239
  77.1 2.2 %project.1 = bf16[1024,512]{1,0:T(8,128)(2,1)} custom-call(bf16[512,256]{1,0:T(8,128)(2,1)S(1)} %collective-permute-done.7.refs_0_, bf16[512,256]{1,0:T(8,128)(2,1)S(1)} %collective-permute-done.9.refs_1_, bf16[512,256]{1,0:T(8,128)(2,1)S(1)} %collective-permute-done.10.refs_2_, bf16[512,256]{1,0:T(8,128)(2,1)S(1)} %collective-permute-done.16.refs_3_, ...), custom_call_target="tpu_custom_call" | custom-call | tf_op jit(solution)/shard_map/project/pallas_call | solution.py:335
  (64 shorter events, 8.3 us)
Async XLA Ops:
  2.7 23.7 %all-to-all-start = ((bf16[16,2,8,16,128]{4,3,2,1,0:T(8,128)(2,1)}), bf16[16,2,8,16,128]{4,3,2,1,0:T(8,128)(2,1)S(1)}, u32[]{:S(2)}, u32[]{:S(2)}) async-start(bf16[16,2,8,16,128]{4,3,2,1,0:T(8,128)(2,1)} %get-tuple-element.20), calls=%async_computation | async-start | bytes 2097152 | tf_op jit(solution)/shard_map/all_to_all | solution.py:348
  12.3 9.5 %collective-permute-start = (bf16[256,512]{1,0:T(8,128)(2,1)S(1)}, bf16[256,512]{1,0:T(8,128)(2,1)S(1)}, u32[]{:S(2)}, u32[]{:S(2)}) collective-permute-start(bf16[256,512]{1,0:T(8,128)(2,1)S(1)} %get-tuple-element.22), channel_id=1, source_target_pairs={{0,2},{1,3},{2,4},{3,5},{4,6},{5,7},{6,0},{7,1},{8,10},{9,11},{10,... | collective-permute-start | bytes 786440 | tf_op jit(solution)/shard_map/ppermute | solution.py:239
  14.0 12.0 %collective-permute-start.1 = (bf16[256,512]{1,0:T(8,128)(2,1)S(1)}, bf16[256,512]{1,0:T(8,128)(2,1)S(1)}, u32[]{:S(2)}, u32[]{:S(2)}) collective-permute-start(bf16[256,512]{1,0:T(8,128)(2,1)S(1)} %get-tuple-element.23), channel_id=1, source_target_pairs={{0,6},{1,7},{2,0},{3,1},{4,2},{5,3},{6,4},{7,5},{8,14},{9,15},{10,... | collective-permute-start | bytes 786440 | tf_op jit(solution)/shard_map/ppermute | solution.py:239
  16.1 25.4 %collective-permute-start.2 = (bf16[256,512]{1,0:T(8,128)(2,1)}, bf16[256,512]{1,0:T(8,128)(2,1)S(1)}, u32[]{:S(2)}, u32[]{:S(2)}) collective-permute-start(bf16[256,512]{1,0:T(8,128)(2,1)} %get-tuple-element.24), channel_id=1, source_target_pairs={{0,3},{1,2},{2,5},{3,4},{4,7},{5,6},{6,1},{7,0},{8,11},{9,10},{10,... | collective-permute-start | bytes 786440 | tf_op jit(solution)/shard_map/ppermute | solution.py:239
  16.8 24.7 %collective-permute-start.3 = (bf16[256,512]{1,0:T(8,128)(2,1)}, bf16[256,512]{1,0:T(8,128)(2,1)S(1)}, u32[]{:S(2)}, u32[]{:S(2)}) collective-permute-start(bf16[256,512]{1,0:T(8,128)(2,1)} %get-tuple-element.25), channel_id=1, source_target_pairs={{0,7},{1,6},{2,1},{3,0},{4,3},{5,2},{6,5},{7,4},{8,15},{9,14},{10,... | collective-permute-start | bytes 786440 | tf_op jit(solution)/shard_map/ppermute | solution.py:239
  19.1 22.5 %collective-permute-start.4 = (bf16[256,512]{1,0:T(8,128)(2,1)}, bf16[256,512]{1,0:T(8,128)(2,1)S(1)}, u32[]{:S(2)}, u32[]{:S(2)}) collective-permute-start(bf16[256,512]{1,0:T(8,128)(2,1)} %get-tuple-element.26), channel_id=1, source_target_pairs={{0,4},{1,5},{2,6},{3,7},{4,0},{5,1},{6,2},{7,3},{8,12},{9,13},{10,... | collective-permute-start | bytes 786440 | tf_op jit(solution)/shard_map/ppermute | solution.py:239
  21.8 19.7 %collective-permute-start.5 = (bf16[256,512]{1,0:T(8,128)(2,1)}, bf16[256,512]{1,0:T(8,128)(2,1)S(1)}, u32[]{:S(2)}, u32[]{:S(2)}) collective-permute-start(bf16[256,512]{1,0:T(8,128)(2,1)} %get-tuple-element.27), channel_id=1, source_target_pairs={{0,5},{1,4},{2,7},{3,6},{4,1},{5,0},{6,3},{7,2},{8,13},{9,12},{10,... | collective-permute-start | bytes 786440 | tf_op jit(solution)/shard_map/ppermute | solution.py:239
  26.0 16.3 %collective-permute-start.6 = (bf16[256,512]{1,0:T(8,128)(2,1)}, bf16[256,512]{1,0:T(8,128)(2,1)S(1)}, u32[]{:S(2)}, u32[]{:S(2)}) collective-permute-start(bf16[256,512]{1,0:T(8,128)(2,1)} %get-tuple-element.28), channel_id=1, source_target_pairs={{0,1},{1,0},{2,3},{3,2},{4,5},{5,4},{6,7},{7,6},{8,9},{9,8},{10,11... | collective-permute-start | bytes 786440 | tf_op jit(solution)/shard_map/ppermute | solution.py:239
  34.9 17.2 %all-to-all-start.1 = ((bf16[16,8,16,128]{3,2,1,0:T(8,128)(2,1)}), bf16[16,8,16,128]{3,2,1,0:T(8,128)(2,1)S(1)}, u32[]{:S(2)}, u32[]{:S(2)}) async-start(bf16[16,8,16,128]{3,2,1,0:T(8,128)(2,1)} %convolve.1), calls=%async_computation.1 | async-start | bytes 1048576 | tf_op jit(solution)/shard_map/all_to_all | solution.py:351
  52.6 24.5 %copy-start.6 = (bf16[256,512]{1,0:T(8,128)(2,1)S(1)}, bf16[256,512]{1,0:T(8,128)(2,1)}, u32[]{:S(2)}) copy-start(bf16[256,512]{1,0:T(8,128)(2,1)} %copy-done.4) | copy-start | bytes 786436
  52.7 7.2 %collective-permute-start.8 = (bf16[512,256]{1,0:T(8,128)(2,1)S(1)}, bf16[512,256]{1,0:T(8,128)(2,1)S(1)}, u32[]{:S(2)}, u32[]{:S(2)}) collective-permute-start(bf16[512,256]{1,0:T(8,128)(2,1)S(1)} %get-tuple-element.30.refs_0_), channel_id=1, source_target_pairs={{0,2},{1,3},{2,4},{3,5},{4,6},{5,7},{6,0},{7,1},{8,10},{9,11},{10,... | collective-permute-start | bytes 786440 | tf_op jit(solution)/shard_map/ppermute | solution.py:239
  53.5 11.6 %collective-permute-start.13 = (bf16[512,256]{1,0:T(8,128)(2,1)S(1)}, bf16[512,256]{1,0:T(8,128)(2,1)S(1)}, u32[]{:S(2)}, u32[]{:S(2)}) collective-permute-start(bf16[512,256]{1,0:T(8,128)(2,1)S(1)} %get-tuple-element.31.refs_4_), channel_id=1, source_target_pairs={{0,6},{1,7},{2,0},{3,1},{4,2},{5,3},{6,4},{7,5},{8,14},{9,15},{10,... | collective-permute-start | bytes 786440 | tf_op jit(solution)/shard_map/ppermute | solution.py:239
  55.4 10.2 %collective-permute-start.12 = (bf16[512,256]{1,0:T(8,128)(2,1)S(1)}, bf16[512,256]{1,0:T(8,128)(2,1)S(1)}, u32[]{:S(2)}, u32[]{:S(2)}) collective-permute-start(bf16[512,256]{1,0:T(8,128)(2,1)S(1)} %get-tuple-element.30.refs_0_), channel_id=1, source_target_pairs={{0,6},{1,7},{2,0},{3,1},{4,2},{5,3},{6,4},{7,5},{8,14},{9,15},{10,... | collective-permute-start | bytes 786440 | tf_op jit(solution)/shard_map/ppermute | solution.py:239
  55.4 10.2 %collective-permute-start.15 = (bf16[512,256]{1,0:T(8,128)(2,1)S(1)}, bf16[512,256]{1,0:T(8,128)(2,1)S(1)}, u32[]{:S(2)}, u32[]{:S(2)}) collective-permute-start(bf16[512,256]{1,0:T(8,128)(2,1)S(1)} %get-tuple-element.31.refs_4_), channel_id=1, source_target_pairs={{0,2},{1,3},{2,4},{3,5},{4,6},{5,7},{6,0},{7,1},{8,10},{9,11},{10,... | collective-permute-start | bytes 786440 | tf_op jit(solution)/shard_map/ppermute | solution.py:239
  59.8 8.5 %collective-permute-start.11 = (bf16[512,256]{1,0:T(8,128)(2,1)S(1)}, bf16[512,256]{1,0:T(8,128)(2,1)S(1)}, u32[]{:S(2)}, u32[]{:S(2)}) collective-permute-start(bf16[512,256]{1,0:T(8,128)(2,1)S(1)} %collective-permute-done.8.refs_1_), channel_id=1, source_target_pairs={{0,1},{1,0},{2,3},{3,2},{4,5},{5,4},{6,7},{7,6},{8,9},{9,8},{10,11... | collective-permute-start | bytes 786440 | tf_op jit(solution)/shard_map/ppermute | solution.py:239
  65.1 6.1 %collective-permute-start.14 = (bf16[512,256]{1,0:T(8,128)(2,1)S(1)}, bf16[512,256]{1,0:T(8,128)(2,1)S(1)}, u32[]{:S(2)}, u32[]{:S(2)}) collective-permute-start(bf16[512,256]{1,0:T(8,128)(2,1)S(1)} %collective-permute-done.13.refs_5_), channel_id=1, source_target_pairs={{0,1},{1,0},{2,3},{3,2},{4,5},{5,4},{6,7},{7,6},{8,9},{9,8},{10,11... | collective-permute-start | bytes 786440 | tf_op jit(solution)/shard_map/ppermute | solution.py:239
  65.1 7.5 %collective-permute-start.17 = (bf16[512,256]{1,0:T(8,128)(2,1)S(1)}, bf16[512,256]{1,0:T(8,128)(2,1)S(1)}, u32[]{:S(2)}, u32[]{:S(2)}) collective-permute-start(bf16[512,256]{1,0:T(8,128)(2,1)S(1)} %get-tuple-element.31.refs_4_), channel_id=1, source_target_pairs={{0,1},{1,0},{2,3},{3,2},{4,5},{5,4},{6,7},{7,6},{8,9},{9,8},{10,11... | collective-permute-start | bytes 786440 | tf_op jit(solution)/shard_map/ppermute | solution.py:239
  65.6 7.5 %collective-permute-start.9 = (bf16[512,256]{1,0:T(8,128)(2,1)S(1)}, bf16[512,256]{1,0:T(8,128)(2,1)S(1)}, u32[]{:S(2)}, u32[]{:S(2)}) collective-permute-start(bf16[512,256]{1,0:T(8,128)(2,1)S(1)} %collective-permute-done.8.refs_1_), channel_id=1, source_target_pairs={{0,2},{1,3},{2,4},{3,5},{4,6},{5,7},{6,0},{7,1},{8,10},{9,11},{10,... | collective-permute-start | bytes 786440 | tf_op jit(solution)/shard_map/ppermute | solution.py:239
  65.6 10.0 %collective-permute-start.18 = (bf16[512,256]{1,0:T(8,128)(2,1)S(1)}, bf16[512,256]{1,0:T(8,128)(2,1)S(1)}, u32[]{:S(2)}, u32[]{:S(2)}) collective-permute-start(bf16[512,256]{1,0:T(8,128)(2,1)S(1)} %collective-permute-done.13.refs_5_), channel_id=1, source_target_pairs={{0,6},{1,7},{2,0},{3,1},{4,2},{5,3},{6,4},{7,5},{8,14},{9,15},{10,... | collective-permute-start | bytes 786440 | tf_op jit(solution)/shard_map/ppermute | solution.py:239
  68.3 7.3 %collective-permute-start.7 = (bf16[512,256]{1,0:T(8,128)(2,1)S(1)}, bf16[512,256]{1,0:T(8,128)(2,1)S(1)}, u32[]{:S(2)}, u32[]{:S(2)}) collective-permute-start(bf16[512,256]{1,0:T(8,128)(2,1)S(1)} %get-tuple-element.30.refs_0_), channel_id=1, source_target_pairs={{0,1},{1,0},{2,3},{3,2},{4,5},{5,4},{6,7},{7,6},{8,9},{9,8},{10,11... | collective-permute-start | bytes 786440 | tf_op jit(solution)/shard_map/ppermute | solution.py:239
  72.5 3.1 %collective-permute-start.16 = (bf16[512,256]{1,0:T(8,128)(2,1)S(1)}, bf16[512,256]{1,0:T(8,128)(2,1)S(1)}, u32[]{:S(2)}, u32[]{:S(2)}) collective-permute-start(bf16[512,256]{1,0:T(8,128)(2,1)S(1)} %get-tuple-element.32), channel_id=1, source_target_pairs={{0,1},{1,0},{2,3},{3,2},{4,5},{5,4},{6,7},{7,6},{8,9},{9,8},{10,11... | collective-permute-start | bytes 786440 | tf_op jit(solution)/shard_map/ppermute | solution.py:239
  72.6 3.0 %collective-permute-start.20 = (bf16[512,256]{1,0:T(8,128)(2,1)S(1)}, bf16[512,256]{1,0:T(8,128)(2,1)S(1)}, u32[]{:S(2)}, u32[]{:S(2)}) collective-permute-start(bf16[512,256]{1,0:T(8,128)(2,1)S(1)} %get-tuple-element.33), channel_id=1, source_target_pairs={{0,1},{1,0},{2,3},{3,2},{4,5},{5,4},{6,7},{7,6},{8,9},{9,8},{10,11... | collective-permute-start | bytes 786440 | tf_op jit(solution)/shard_map/ppermute | solution.py:239
  73.1 3.6 %collective-permute-start.10 = (bf16[512,256]{1,0:T(8,128)(2,1)S(1)}, bf16[512,256]{1,0:T(8,128)(2,1)S(1)}, u32[]{:S(2)}, u32[]{:S(2)}) collective-permute-start(bf16[512,256]{1,0:T(8,128)(2,1)S(1)} %collective-permute-done.9.refs_1_), channel_id=1, source_target_pairs={{0,1},{1,0},{2,3},{3,2},{4,5},{5,4},{6,7},{7,6},{8,9},{9,8},{10,11... | collective-permute-start | bytes 786440 | tf_op jit(solution)/shard_map/ppermute | solution.py:239
  75.6 1.5 %collective-permute-start.19 = (bf16[512,256]{1,0:T(8,128)(2,1)S(1)}, bf16[512,256]{1,0:T(8,128)(2,1)S(1)}, u32[]{:S(2)}, u32[]{:S(2)}) collective-permute-start(bf16[512,256]{1,0:T(8,128)(2,1)S(1)} %collective-permute-done.18.refs_5_), channel_id=1, source_target_pairs={{0,1},{1,0},{2,3},{3,2},{4,5},{5,4},{6,7},{7,6},{8,9},{9,8},{10,11... | collective-permute-start | bytes 786440 | tf_op jit(solution)/shard_map/ppermute | solution.py:239
  (16 other events, 110.0 us)

commit v6 on v5

--- a/solution.py
+++ b/solution.py
@@ -171,7 +171,7 @@
         out[a] = total[part, :].astype(BF16).reshape(blocks, channels, TILE)
 
 
-def convolve(pairs, blocks, group=8):
+def convolve(pairs, blocks, group=16):
     channels, rows, _ = pairs.shape
     space = pl.BlockSpec(memory_space=pltpu.VMEM)
     return pl.pallas_call(

time: 79.8 us -> 79.6 us (level)
  transfers between devices with their start and end apart: 23 -> 23, of which waited for: 6 -> 6; matrix products, arithmetic and copies ran while one was open for 0% -> 0% of each run, Pallas kernels for 14% -> 13%
where the time goes in v6:
time: 79.6 us; the launch traced here: 79.2 us
  starting transfers between devices  45 us (57%)
  Pallas kernels  16 us (20%)
  waiting for transfers between devices  12.1 us (15%)
  local copies, waits for them, and re-layouts  5.2 us (7%)
  between operations  0.85 us (1%)
    ppermute x21, starting transfers between devices, toward(): return lax.ppermute(array, 'chan', pairs)  30.7 us
    all_to_all x1, starting transfers between devices, on_device(): lax.all_to_all(packed, 'seq', split_axis=0, concat_axis=0, tiled=True)  7.72 us
    pallas_call x1, Pallas kernels, convolve(): pl.pallas_call(functools.partial(conv_kernel, group), in_specs=[space] *...  7.07 us
    all_to_all x1, starting transfers between devices, on_device(): lax.all_to_all(convolve(unpack(data, weight[:2]), packed.shape[2]), 'seq'...  6.59 us
    all_to_all x1, waiting for transfers between devices, on_device(): lax.all_to_all(convolve(unpack(data, weight[:2]), packed.shape[2]), 'seq'...  6.21 us
    ppermute x21, waiting for transfers between devices, toward(): return lax.ppermute(array, 'chan', pairs)  5.5 us
    unnamed x34, local copies, waits for them, and re-layouts  5.2 us
    pallas_call x1, Pallas kernels, pack(): pl.pallas_call(pack_kernel, grid=(rows // (blocks * TILE),), in_specs=[bl...  2.66 us
  transfers between devices with their start and end apart: 23, of which 6 were waited for; matrix products, arithmetic and copies ran while one was open for 0% of the time, Pallas kernels for 13%

profile of v6, /device:TPU:1, one launch (start us, length us, event | category | flops | bytes accessed | tf_op | source)
XLA Modules:
  0.0 79.2 jit_solution(7467746539207053080)
XLA Ops:
  0.0 2.7 %pack.1 = (bf16[16,2,8,16,128]{4,3,2,1,0:T(8,128)(2,1)}, f32[8,128]{1,0:T(8,128)}) custom-call(bf16[1024,256]{1,0:T(8,128)(2,1)} %gate_in.3, bf16[1024,256]{1,0:T(8,128)(2,1)} %value_in.3, f32[1024,256]{1,0:T(8,128)} %taps.1), custom_call_target="tpu_custom_call" | custom-call | tf_op jit(solution)/shard_map/pack/pallas_call | solution.py:78
  2.7 7.7 %all-to-all-start = ((bf16[16,2,8,16,128]{4,3,2,1,0:T(8,128)(2,1)}), bf16[16,2,8,16,128]{4,3,2,1,0:T(8,128)(2,1)S(1)}, u32[]{:S(2)}, u32[]{:S(2)}) async-start(bf16[16,2,8,16,128]{4,3,2,1,0:T(8,128)(2,1)} %get-tuple-element.20), calls=%async_computation | async-start | bytes 2097152 | tf_op jit(solution)/shard_map/all_to_all | solution.py:348
  10.4 1.2 %split_weight.1 = (bf16[256,512]{1,0:T(8,128)(2,1)S(1)}, bf16[256,512]{1,0:T(8,128)(2,1)S(1)}, bf16[256,512]{1,0:T(8,128)(2,1)}, bf16[256,512]{1,0:T(8,128)(2,1)...) custom-call(bf16[256,4096]{1,0:T(8,128)(2,1)S(1)} %copy-done, ...), custom_call_target="tpu_custom_call" | custom-call | tf_op jit(solution)/shard_map/split_weight/pallas_call | solution.py:258
  12.3 1.6 %collective-permute-start = (bf16[256,512]{1,0:T(8,128)(2,1)S(1)}, bf16[256,512]{1,0:T(8,128)(2,1)S(1)}, u32[]{:S(2)}, u32[]{:S(2)}) collective-permute-start(bf16[256,512]{1,0:T(8,128)(2,1)S(1)} %get-tuple-element.22), channel_id=1, source_target_pairs={{0,2},{1,3},{2,4},{3,5},{4,6},{5,7},{6,0},{7,1},{8,10},{9,11},{10,... | collective-permute-start | bytes 786440 | tf_op jit(solution)/shard_map/ppermute | solution.py:239
  14.0 2.1 %collective-permute-start.1 = (bf16[256,512]{1,0:T(8,128)(2,1)S(1)}, bf16[256,512]{1,0:T(8,128)(2,1)S(1)}, u32[]{:S(2)}, u32[]{:S(2)}) collective-permute-start(bf16[256,512]{1,0:T(8,128)(2,1)S(1)} %get-tuple-element.23), channel_id=1, source_target_pairs={{0,6},{1,7},{2,0},{3,1},{4,2},{5,3},{6,4},{7,5},{8,14},{9,15},{10,... | collective-permute-start | bytes 786440 | tf_op jit(solution)/shard_map/ppermute | solution.py:239
  16.8 2.2 %collective-permute-start.3 = (bf16[256,512]{1,0:T(8,128)(2,1)}, bf16[256,512]{1,0:T(8,128)(2,1)S(1)}, u32[]{:S(2)}, u32[]{:S(2)}) collective-permute-start(bf16[256,512]{1,0:T(8,128)(2,1)} %get-tuple-element.25), channel_id=1, source_target_pairs={{0,7},{1,6},{2,1},{3,0},{4,3},{5,2},{6,5},{7,4},{8,15},{9,14},{10,... | collective-permute-start | bytes 786440 | tf_op jit(solution)/shard_map/ppermute | solution.py:239
  19.1 1.1 %collective-permute-start.4 = (bf16[256,512]{1,0:T(8,128)(2,1)}, bf16[256,512]{1,0:T(8,128)(2,1)S(1)}, u32[]{:S(2)}, u32[]{:S(2)}) collective-permute-start(bf16[256,512]{1,0:T(8,128)(2,1)} %get-tuple-element.26), channel_id=1, source_target_pairs={{0,4},{1,5},{2,6},{3,7},{4,0},{5,1},{6,2},{7,3},{8,12},{9,13},{10,... | collective-permute-start | bytes 786440 | tf_op jit(solution)/shard_map/ppermute | solution.py:239
  20.8 1.0 %collective-permute-done.rest_0_.refs_0_.refs_9_ = bf16[256,512]{1,0:T(8,128)(2,1)S(1)} collective-permute-done((bf16[256,512]{1,0:T(8,128)(2,1)S(1)}, bf16[256,512]{1,0:T(8,128)(2,1)S(1)}, u32[]{:S(2)}, u32[]{:S(2)}) %collective-permute-start) | collective-permute-done | bytes 262176 | tf_op jit(solution)/shard_map/ppermute | solution.py:239
  21.8 4.2 %collective-permute-start.5 = (bf16[256,512]{1,0:T(8,128)(2,1)}, bf16[256,512]{1,0:T(8,128)(2,1)S(1)}, u32[]{:S(2)}, u32[]{:S(2)}) collective-permute-start(bf16[256,512]{1,0:T(8,128)(2,1)} %get-tuple-element.27), channel_id=1, source_target_pairs={{0,5},{1,4},{2,7},{3,6},{4,1},{5,0},{6,3},{7,2},{8,13},{9,12},{10,... | collective-permute-start | bytes 786440 | tf_op jit(solution)/shard_map/ppermute | solution.py:239
  26.4 1.0 %unpack.1.pairs = bf16[16,128,256]{2,1,0:T(8,128)(2,1)S(1)} custom-call(bf16[16,2,8,16,128]{4,3,2,1,0:T(8,128)(2,1)S(1)} %all-to-all-done.data, bf16[256,512]{1,0:T(8,128)(2,1)S(1)} %collective-permute-done.rest_0_.refs_0_.refs_9_, bf16[256,512]{1,0:T(8,128)(2,1)S(1)} %collective-permute-done.1.rest_1_.refs_1_.refs_11_), custom_call_target="tpu_custom_call" | custom-call | tf_op jit(solution)/shard_map/unpack/pallas_call | solution.py:114
  27.6 7.1 %convolve.1 = bf16[16,8,16,128]{3,2,1,0:T(8,128)(2,1)} custom-call(bf16[16,128,256]{2,1,0:T(8,128)(2,1)S(1)} %unpack.1.pairs, bf16[2176,256]{1,0:T(8,128)(2,1)S(1)} %copy-done.15, f32[256,128]{1,0:T(8,128)S(1)} %copy-done.16), custom_call_target="tpu_custom_call" | custom-call | flops 10000000000 | bytes 4194304 | tf_op jit(solution)/shard_map/convolve/pallas_call | solution.py:177
  34.7 6.6 %all-to-all-start.1 = ((bf16[16,8,16,128]{3,2,1,0:T(8,128)(2,1)}), bf16[16,8,16,128]{3,2,1,0:T(8,128)(2,1)S(1)}, u32[]{:S(2)}, u32[]{:S(2)}) async-start(bf16[16,8,16,128]{3,2,1,0:T(8,128)(2,1)} %convolve.1), calls=%async_computation.1 | async-start | bytes 1048576 | tf_op jit(solution)/shard_map/all_to_all | solution.py:351
  42.8 0.9 %copy-done.5 = bf16[256,512]{1,0:T(8,128)(2,1)S(1)} copy-done((bf16[256,512]{1,0:T(8,128)(2,1)S(1)}, bf16[256,512]{1,0:T(8,128)(2,1)}, u32[]{:S(2)}) %copy-start.5) | copy-done | bytes 262168
  45.6 6.2 %all-to-all-done.1.conv = bf16[16,8,16,128]{3,2,1,0:T(8,128)(2,1)S(1)} async-done(((bf16[16,8,16,128]{3,2,1,0:T(8,128)(2,1)}), bf16[16,8,16,128]{3,2,1,0:T(8,128)(2,1)S(1)}, u32[]{:S(2)}, u32[]{:S(2)}) %all-to-all-start.1) | async-done | bytes 524320 | tf_op jit(solution)/shard_map/all_to_all | solution.py:351
  53.3 1.9 %collective-permute-start.13 = (bf16[512,256]{1,0:T(8,128)(2,1)S(1)}, bf16[512,256]{1,0:T(8,128)(2,1)S(1)}, u32[]{:S(2)}, u32[]{:S(2)}) collective-permute-start(bf16[512,256]{1,0:T(8,128)(2,1)S(1)} %get-tuple-element.31.refs_4_), channel_id=1, source_target_pairs={{0,6},{1,7},{2,0},{3,1},{4,2},{5,3},{6,4},{7,5},{8,14},{9,15},{10,... | collective-permute-start | bytes 786440 | tf_op jit(solution)/shard_map/ppermute | solution.py:239
  55.2 1.4 %collective-permute-start.15 = (bf16[512,256]{1,0:T(8,128)(2,1)S(1)}, bf16[512,256]{1,0:T(8,128)(2,1)S(1)}, u32[]{:S(2)}, u32[]{:S(2)}) collective-permute-start(bf16[512,256]{1,0:T(8,128)(2,1)S(1)} %get-tuple-element.31.refs_4_), channel_id=1, source_target_pairs={{0,2},{1,3},{2,4},{3,5},{4,6},{5,7},{6,0},{7,1},{8,10},{9,11},{10,... | collective-permute-start | bytes 786440 | tf_op jit(solution)/shard_map/ppermute | solution.py:239
  56.7 2.9 %collective-permute-done.8.refs_1_ = bf16[512,256]{1,0:T(8,128)(2,1)S(1)} collective-permute-done((bf16[512,256]{1,0:T(8,128)(2,1)S(1)}, bf16[512,256]{1,0:T(8,128)(2,1)S(1)}, u32[]{:S(2)}, u32[]{:S(2)}) %collective-permute-start.8) | collective-permute-done | bytes 262176 | tf_op jit(solution)/shard_map/ppermute | solution.py:239
  59.6 5.3 %collective-permute-start.11 = (bf16[512,256]{1,0:T(8,128)(2,1)S(1)}, bf16[512,256]{1,0:T(8,128)(2,1)S(1)}, u32[]{:S(2)}, u32[]{:S(2)}) collective-permute-start(bf16[512,256]{1,0:T(8,128)(2,1)S(1)} %collective-permute-done.8.refs_1_), channel_id=1, source_target_pairs={{0,1},{1,0},{2,3},{3,2},{4,5},{5,4},{6,7},{7,6},{8,9},{9,8},{10,11... | collective-permute-start | bytes 786440 | tf_op jit(solution)/shard_map/ppermute | solution.py:239
  65.4 2.7 %collective-permute-start.18 = (bf16[512,256]{1,0:T(8,128)(2,1)S(1)}, bf16[512,256]{1,0:T(8,128)(2,1)S(1)}, u32[]{:S(2)}, u32[]{:S(2)}) collective-permute-start(bf16[512,256]{1,0:T(8,128)(2,1)S(1)} %collective-permute-done.13.refs_5_), channel_id=1, source_target_pairs={{0,6},{1,7},{2,0},{3,1},{4,2},{5,3},{6,4},{7,5},{8,14},{9,15},{10,... | collective-permute-start | bytes 786440 | tf_op jit(solution)/shard_map/ppermute | solution.py:239
  68.1 2.9 %collective-permute-start.7 = (bf16[512,256]{1,0:T(8,128)(2,1)S(1)}, bf16[512,256]{1,0:T(8,128)(2,1)S(1)}, u32[]{:S(2)}, u32[]{:S(2)}) collective-permute-start(bf16[512,256]{1,0:T(8,128)(2,1)S(1)} %get-tuple-element.30.refs_0_), channel_id=1, source_target_pairs={{0,1},{1,0},{2,3},{3,2},{4,5},{5,4},{6,7},{7,6},{8,9},{9,8},{10,11... | collective-permute-start | bytes 786440 | tf_op jit(solution)/shard_map/ppermute | solution.py:239
  71.1 1.2 %fold.1 = (f32[1024,512]{1,0:T(8,128)S(1)}, bf16[512,256]{1,0:T(8,128)(2,1)S(1)}, bf16[512,256]{1,0:T(8,128)(2,1)S(1)}) custom-call(bf16[512,256]{1,0:T(8,128)(2,1)S(1)} %get-tuple-element.30.refs_0_, bf16[512,256]{1,0:T(8,128)(2,1)S(1)} %collective-permute-done.8.refs_1_, bf16[512,256]{1,0:T(8,128)(2,1)S(1)} %collective-permute-done.11.refs_2_, ...), custom_call_target="tpu_custom_call" | custom-call | tf_op jit(solution)/shard_map/fold/pallas_call | solution.py:306
  72.9 2.5 %collective-permute-start.10 = (bf16[512,256]{1,0:T(8,128)(2,1)S(1)}, bf16[512,256]{1,0:T(8,128)(2,1)S(1)}, u32[]{:S(2)}, u32[]{:S(2)}) collective-permute-start(bf16[512,256]{1,0:T(8,128)(2,1)S(1)} %collective-permute-done.9.refs_1_), channel_id=1, source_target_pairs={{0,1},{1,0},{2,3},{3,2},{4,5},{5,4},{6,7},{7,6},{8,9},{9,8},{10,11... | collective-permute-start | bytes 786440 | tf_op jit(solution)/shard_map/ppermute | solution.py:239
  75.4 1.1 %collective-permute-done.10.refs_2_ = bf16[512,256]{1,0:T(8,128)(2,1)S(1)} collective-permute-done((bf16[512,256]{1,0:T(8,128)(2,1)S(1)}, bf16[512,256]{1,0:T(8,128)(2,1)S(1)}, u32[]{:S(2)}, u32[]{:S(2)}) %collective-permute-start.10) | collective-permute-done | bytes 262176 | tf_op jit(solution)/shard_map/ppermute | solution.py:239
  76.9 2.2 %project.1 = bf16[1024,512]{1,0:T(8,128)(2,1)} custom-call(bf16[512,256]{1,0:T(8,128)(2,1)S(1)} %collective-permute-done.7.refs_0_, bf16[512,256]{1,0:T(8,128)(2,1)S(1)} %collective-permute-done.9.refs_1_, bf16[512,256]{1,0:T(8,128)(2,1)S(1)} %collective-permute-done.10.refs_2_, bf16[512,256]{1,0:T(8,128)(2,1)S(1)} %collective-permute-done.16.refs_3_, ...), custom_call_target="tpu_custom_call" | custom-call | tf_op jit(solution)/shard_map/project/pallas_call | solution.py:335
  (64 shorter events, 8.3 us)
Async XLA Ops:
  2.7 23.7 %all-to-all-start = ((bf16[16,2,8,16,128]{4,3,2,1,0:T(8,128)(2,1)}), bf16[16,2,8,16,128]{4,3,2,1,0:T(8,128)(2,1)S(1)}, u32[]{:S(2)}, u32[]{:S(2)}) async-start(bf16[16,2,8,16,128]{4,3,2,1,0:T(8,128)(2,1)} %get-tuple-element.20), calls=%async_computation | async-start | bytes 2097152 | tf_op jit(solution)/shard_map/all_to_all | solution.py:348
  12.3 9.5 %collective-permute-start = (bf16[256,512]{1,0:T(8,128)(2,1)S(1)}, bf16[256,512]{1,0:T(8,128)(2,1)S(1)}, u32[]{:S(2)}, u32[]{:S(2)}) collective-permute-start(bf16[256,512]{1,0:T(8,128)(2,1)S(1)} %get-tuple-element.22), channel_id=1, source_target_pairs={{0,2},{1,3},{2,4},{3,5},{4,6},{5,7},{6,0},{7,1},{8,10},{9,11},{10,... | collective-permute-start | bytes 786440 | tf_op jit(solution)/shard_map/ppermute | solution.py:239
  14.0 12.0 %collective-permute-start.1 = (bf16[256,512]{1,0:T(8,128)(2,1)S(1)}, bf16[256,512]{1,0:T(8,128)(2,1)S(1)}, u32[]{:S(2)}, u32[]{:S(2)}) collective-permute-start(bf16[256,512]{1,0:T(8,128)(2,1)S(1)} %get-tuple-element.23), channel_id=1, source_target_pairs={{0,6},{1,7},{2,0},{3,1},{4,2},{5,3},{6,4},{7,5},{8,14},{9,15},{10,... | collective-permute-start | bytes 786440 | tf_op jit(solution)/shard_map/ppermute | solution.py:239
  16.1 25.2 %collective-permute-start.2 = (bf16[256,512]{1,0:T(8,128)(2,1)}, bf16[256,512]{1,0:T(8,128)(2,1)S(1)}, u32[]{:S(2)}, u32[]{:S(2)}) collective-permute-start(bf16[256,512]{1,0:T(8,128)(2,1)} %get-tuple-element.24), channel_id=1, source_target_pairs={{0,3},{1,2},{2,5},{3,4},{4,7},{5,6},{6,1},{7,0},{8,11},{9,10},{10,... | collective-permute-start | bytes 786440 | tf_op jit(solution)/shard_map/ppermute | solution.py:239
  16.8 24.5 %collective-permute-start.3 = (bf16[256,512]{1,0:T(8,128)(2,1)}, bf16[256,512]{1,0:T(8,128)(2,1)S(1)}, u32[]{:S(2)}, u32[]{:S(2)}) collective-permute-start(bf16[256,512]{1,0:T(8,128)(2,1)} %get-tuple-element.25), channel_id=1, source_target_pairs={{0,7},{1,6},{2,1},{3,0},{4,3},{5,2},{6,5},{7,4},{8,15},{9,14},{10,... | collective-permute-start | bytes 786440 | tf_op jit(solution)/shard_map/ppermute | solution.py:239
  19.1 22.3 %collective-permute-start.4 = (bf16[256,512]{1,0:T(8,128)(2,1)}, bf16[256,512]{1,0:T(8,128)(2,1)S(1)}, u32[]{:S(2)}, u32[]{:S(2)}) collective-permute-start(bf16[256,512]{1,0:T(8,128)(2,1)} %get-tuple-element.26), channel_id=1, source_target_pairs={{0,4},{1,5},{2,6},{3,7},{4,0},{5,1},{6,2},{7,3},{8,12},{9,13},{10,... | collective-permute-start | bytes 786440 | tf_op jit(solution)/shard_map/ppermute | solution.py:239
  21.8 19.5 %collective-permute-start.5 = (bf16[256,512]{1,0:T(8,128)(2,1)}, bf16[256,512]{1,0:T(8,128)(2,1)S(1)}, u32[]{:S(2)}, u32[]{:S(2)}) collective-permute-start(bf16[256,512]{1,0:T(8,128)(2,1)} %get-tuple-element.27), channel_id=1, source_target_pairs={{0,5},{1,4},{2,7},{3,6},{4,1},{5,0},{6,3},{7,2},{8,13},{9,12},{10,... | collective-permute-start | bytes 786440 | tf_op jit(solution)/shard_map/ppermute | solution.py:239
  26.0 16.1 %collective-permute-start.6 = (bf16[256,512]{1,0:T(8,128)(2,1)}, bf16[256,512]{1,0:T(8,128)(2,1)S(1)}, u32[]{:S(2)}, u32[]{:S(2)}) collective-permute-start(bf16[256,512]{1,0:T(8,128)(2,1)} %get-tuple-element.28), channel_id=1, source_target_pairs={{0,1},{1,0},{2,3},{3,2},{4,5},{5,4},{6,7},{7,6},{8,9},{9,8},{10,11... | collective-permute-start | bytes 786440 | tf_op jit(solution)/shard_map/ppermute | solution.py:239
  34.7 17.2 %all-to-all-start.1 = ((bf16[16,8,16,128]{3,2,1,0:T(8,128)(2,1)}), bf16[16,8,16,128]{3,2,1,0:T(8,128)(2,1)S(1)}, u32[]{:S(2)}, u32[]{:S(2)}) async-start(bf16[16,8,16,128]{3,2,1,0:T(8,128)(2,1)} %convolve.1), calls=%async_computation.1 | async-start | bytes 1048576 | tf_op jit(solution)/shard_map/all_to_all | solution.py:351
  52.4 24.5 %copy-start.6 = (bf16[256,512]{1,0:T(8,128)(2,1)S(1)}, bf16[256,512]{1,0:T(8,128)(2,1)}, u32[]{:S(2)}) copy-start(bf16[256,512]{1,0:T(8,128)(2,1)} %copy-done.4) | copy-start | bytes 786436
  52.5 7.2 %collective-permute-start.8 = (bf16[512,256]{1,0:T(8,128)(2,1)S(1)}, bf16[512,256]{1,0:T(8,128)(2,1)S(1)}, u32[]{:S(2)}, u32[]{:S(2)}) collective-permute-start(bf16[512,256]{1,0:T(8,128)(2,1)S(1)} %get-tuple-element.30.refs_0_), channel_id=1, source_target_pairs={{0,2},{1,3},{2,4},{3,5},{4,6},{5,7},{6,0},{7,1},{8,10},{9,11},{10,... | collective-permute-start | bytes 786440 | tf_op jit(solution)/shard_map/ppermute | solution.py:239
  53.3 11.6 %collective-permute-start.13 = (bf16[512,256]{1,0:T(8,128)(2,1)S(1)}, bf16[512,256]{1,0:T(8,128)(2,1)S(1)}, u32[]{:S(2)}, u32[]{:S(2)}) collective-permute-start(bf16[512,256]{1,0:T(8,128)(2,1)S(1)} %get-tuple-element.31.refs_4_), channel_id=1, source_target_pairs={{0,6},{1,7},{2,0},{3,1},{4,2},{5,3},{6,4},{7,5},{8,14},{9,15},{10,... | collective-permute-start | bytes 786440 | tf_op jit(solution)/shard_map/ppermute | solution.py:239
  55.2 10.2 %collective-permute-start.12 = (bf16[512,256]{1,0:T(8,128)(2,1)S(1)}, bf16[512,256]{1,0:T(8,128)(2,1)S(1)}, u32[]{:S(2)}, u32[]{:S(2)}) collective-permute-start(bf16[512,256]{1,0:T(8,128)(2,1)S(1)} %get-tuple-element.30.refs_0_), channel_id=1, source_target_pairs={{0,6},{1,7},{2,0},{3,1},{4,2},{5,3},{6,4},{7,5},{8,14},{9,15},{10,... | collective-permute-start | bytes 786440 | tf_op jit(solution)/shard_map/ppermute | solution.py:239
  55.2 10.2 %collective-permute-start.15 = (bf16[512,256]{1,0:T(8,128)(2,1)S(1)}, bf16[512,256]{1,0:T(8,128)(2,1)S(1)}, u32[]{:S(2)}, u32[]{:S(2)}) collective-permute-start(bf16[512,256]{1,0:T(8,128)(2,1)S(1)} %get-tuple-element.31.refs_4_), channel_id=1, source_target_pairs={{0,2},{1,3},{2,4},{3,5},{4,6},{5,7},{6,0},{7,1},{8,10},{9,11},{10,... | collective-permute-start | bytes 786440 | tf_op jit(solution)/shard_map/ppermute | solution.py:239
  59.6 8.5 %collective-permute-start.11 = (bf16[512,256]{1,0:T(8,128)(2,1)S(1)}, bf16[512,256]{1,0:T(8,128)(2,1)S(1)}, u32[]{:S(2)}, u32[]{:S(2)}) collective-permute-start(bf16[512,256]{1,0:T(8,128)(2,1)S(1)} %collective-permute-done.8.refs_1_), channel_id=1, source_target_pairs={{0,1},{1,0},{2,3},{3,2},{4,5},{5,4},{6,7},{7,6},{8,9},{9,8},{10,11... | collective-permute-start | bytes 786440 | tf_op jit(solution)/shard_map/ppermute | solution.py:239
  64.9 6.1 %collective-permute-start.14 = (bf16[512,256]{1,0:T(8,128)(2,1)S(1)}, bf16[512,256]{1,0:T(8,128)(2,1)S(1)}, u32[]{:S(2)}, u32[]{:S(2)}) collective-permute-start(bf16[512,256]{1,0:T(8,128)(2,1)S(1)} %collective-permute-done.13.refs_5_), channel_id=1, source_target_pairs={{0,1},{1,0},{2,3},{3,2},{4,5},{5,4},{6,7},{7,6},{8,9},{9,8},{10,11... | collective-permute-start | bytes 786440 | tf_op jit(solution)/shard_map/ppermute | solution.py:239
  64.9 7.5 %collective-permute-start.17 = (bf16[512,256]{1,0:T(8,128)(2,1)S(1)}, bf16[512,256]{1,0:T(8,128)(2,1)S(1)}, u32[]{:S(2)}, u32[]{:S(2)}) collective-permute-start(bf16[512,256]{1,0:T(8,128)(2,1)S(1)} %get-tuple-element.31.refs_4_), channel_id=1, source_target_pairs={{0,1},{1,0},{2,3},{3,2},{4,5},{5,4},{6,7},{7,6},{8,9},{9,8},{10,11... | collective-permute-start | bytes 786440 | tf_op jit(solution)/shard_map/ppermute | solution.py:239
  65.4 7.5 %collective-permute-start.9 = (bf16[512,256]{1,0:T(8,128)(2,1)S(1)}, bf16[512,256]{1,0:T(8,128)(2,1)S(1)}, u32[]{:S(2)}, u32[]{:S(2)}) collective-permute-start(bf16[512,256]{1,0:T(8,128)(2,1)S(1)} %collective-permute-done.8.refs_1_), channel_id=1, source_target_pairs={{0,2},{1,3},{2,4},{3,5},{4,6},{5,7},{6,0},{7,1},{8,10},{9,11},{10,... | collective-permute-start | bytes 786440 | tf_op jit(solution)/shard_map/ppermute | solution.py:239
  65.4 10.0 %collective-permute-start.18 = (bf16[512,256]{1,0:T(8,128)(2,1)S(1)}, bf16[512,256]{1,0:T(8,128)(2,1)S(1)}, u32[]{:S(2)}, u32[]{:S(2)}) collective-permute-start(bf16[512,256]{1,0:T(8,128)(2,1)S(1)} %collective-permute-done.13.refs_5_), channel_id=1, source_target_pairs={{0,6},{1,7},{2,0},{3,1},{4,2},{5,3},{6,4},{7,5},{8,14},{9,15},{10,... | collective-permute-start | bytes 786440 | tf_op jit(solution)/shard_map/ppermute | solution.py:239
  68.1 7.3 %collective-permute-start.7 = (bf16[512,256]{1,0:T(8,128)(2,1)S(1)}, bf16[512,256]{1,0:T(8,128)(2,1)S(1)}, u32[]{:S(2)}, u32[]{:S(2)}) collective-permute-start(bf16[512,256]{1,0:T(8,128)(2,1)S(1)} %get-tuple-element.30.refs_0_), channel_id=1, source_target_pairs={{0,1},{1,0},{2,3},{3,2},{4,5},{5,4},{6,7},{7,6},{8,9},{9,8},{10,11... | collective-permute-start | bytes 786440 | tf_op jit(solution)/shard_map/ppermute | solution.py:239
  72.3 3.1 %collective-permute-start.16 = (bf16[512,256]{1,0:T(8,128)(2,1)S(1)}, bf16[512,256]{1,0:T(8,128)(2,1)S(1)}, u32[]{:S(2)}, u32[]{:S(2)}) collective-permute-start(bf16[512,256]{1,0:T(8,128)(2,1)S(1)} %get-tuple-element.32), channel_id=1, source_target_pairs={{0,1},{1,0},{2,3},{3,2},{4,5},{5,4},{6,7},{7,6},{8,9},{9,8},{10,11... | collective-permute-start | bytes 786440 | tf_op jit(solution)/shard_map/ppermute | solution.py:239
  72.4 3.0 %collective-permute-start.20 = (bf16[512,256]{1,0:T(8,128)(2,1)S(1)}, bf16[512,256]{1,0:T(8,128)(2,1)S(1)}, u32[]{:S(2)}, u32[]{:S(2)}) collective-permute-start(bf16[512,256]{1,0:T(8,128)(2,1)S(1)} %get-tuple-element.33), channel_id=1, source_target_pairs={{0,1},{1,0},{2,3},{3,2},{4,5},{5,4},{6,7},{7,6},{8,9},{9,8},{10,11... | collective-permute-start | bytes 786440 | tf_op jit(solution)/shard_map/ppermute | solution.py:239
  72.9 3.6 %collective-permute-start.10 = (bf16[512,256]{1,0:T(8,128)(2,1)S(1)}, bf16[512,256]{1,0:T(8,128)(2,1)S(1)}, u32[]{:S(2)}, u32[]{:S(2)}) collective-permute-start(bf16[512,256]{1,0:T(8,128)(2,1)S(1)} %collective-permute-done.9.refs_1_), channel_id=1, source_target_pairs={{0,1},{1,0},{2,3},{3,2},{4,5},{5,4},{6,7},{7,6},{8,9},{9,8},{10,11... | collective-permute-start | bytes 786440 | tf_op jit(solution)/shard_map/ppermute | solution.py:239
  75.4 1.5 %collective-permute-start.19 = (bf16[512,256]{1,0:T(8,128)(2,1)S(1)}, bf16[512,256]{1,0:T(8,128)(2,1)S(1)}, u32[]{:S(2)}, u32[]{:S(2)}) collective-permute-start(bf16[512,256]{1,0:T(8,128)(2,1)S(1)} %collective-permute-done.18.refs_5_), channel_id=1, source_target_pairs={{0,1},{1,0},{2,3},{3,2},{4,5},{5,4},{6,7},{7,6},{8,9},{9,8},{10,11... | collective-permute-start | bytes 786440 | tf_op jit(solution)/shard_map/ppermute | solution.py:239
  (16 other events, 110.0 us)

commit v7 on v5

--- a/solution.py
+++ b/solution.py
@@ -286,7 +286,7 @@
 
 def fold_kernel(*refs):
     top, low, weight = refs[:4], refs[4:8], refs[8:13]
-    partial, first, second = refs[13:]
+    partial, late = refs[13:]
     rows = top[0].shape[0]
     for half, pieces in enumerate((top, low)):
         total = None
@@ -294,53 +294,74 @@
             term = matmul(piece[...], weight[k][...])
             total = term if total is None else total + term
         partial[half * rows : half * rows + rows] = total
-    first[...] = top[3][...]
-    second[...] = low[3][...]
+    late[:rows] = top[3][...]
+    late[rows:] = low[3][...]
 
 
 def fold(top, low, weight):
     rows = top[0].shape[0]
     features = weight[0].shape[1]
     space = pl.BlockSpec(memory_space=pltpu.VMEM)
-    piece = jax.ShapeDtypeStruct(top[0].shape, BF16)
+    late = jax.ShapeDtypeStruct((2 * rows, top[0].shape[1]), BF16)
     return pl.pallas_call(
         fold_kernel,
         in_specs=[space] * 13,
-        out_specs=[space] * 3,
-        out_shape=[jax.ShapeDtypeStruct((2 * rows, features), F32), piece, piece],
+        out_specs=[space] * 2,
+        out_shape=[jax.ShapeDtypeStruct((2 * rows, features), F32), late],
         compiler_params=pltpu.CompilerParams(vmem_limit_bytes=12 << 20),
         cost_estimate=pl.CostEstimate(flops=0, bytes_accessed=0, transcendentals=0),
         name="fold",
     )(*top, *low, *weight)
 
 
+def join_kernel(first, second, out):
+    rows = first.shape[0]
+    out[:rows] = first[...]
+    out[rows:] = second[...]
+
+
+def join(first, second):
+    rows, channels = first.shape
+    space = pl.BlockSpec(memory_space=pltpu.VMEM)
+    return pl.pallas_call(
+        join_kernel,
+        in_specs=[space] * 2,
+        out_specs=space,
+        out_shape=jax.ShapeDtypeStruct((2 * rows, channels), BF16),
+        compiler_params=pltpu.CompilerParams(vmem_limit_bytes=12 << 20),
+        name="join",
+    )(first, second)
+
+
 def project_kernel(*refs):
-    mixed, weight, partial, out = refs[:8], refs[8:13], refs[13], refs[14]
+    others, fars, (far_other, late_other) = refs[:2], refs[2:4], refs[4:6]
+    weight, partial, out = refs[6:11], refs[11], refs[12]
     rows = out.shape[0]
 
     def fill(half):
-        total = partial[half * rows : half * rows + rows]
-        places = ((0, 1, 2, 3), (0, 1, 2, 4))[half]
-        for piece, k in zip(mixed[4 * half : 4 * half + 4], places):
-            total = total + matmul(piece[...], weight[k][...])
+        part = slice(half * rows, half * rows + rows)
+        total = partial[part] + matmul(others[half][...], weight[0][...])
+        total = total + matmul(fars[half][...], weight[1][...])
+        total = total + matmul(far_other[part], weight[2][...])
+        total = total + matmul(late_other[part], weight[3 + half][...])
         out[...] = total.astype(BF16)
 
     for half in range(2):
         pl.when(pl.program_id(0) == half)(functools.partial(fill, half))
 
 
-def project(top, low, weight, partial):
-    rows = top[0].shape[0]
+def project(mixed, weight, partial):
+    rows = mixed[0].shape[0]
     features = weight[0].shape[1]
     return pl.pallas_call(
         project_kernel,
         grid=(2,),
-        in_specs=[pl.BlockSpec(memory_space=pltpu.VMEM)] * 14,
+        in_specs=[pl.BlockSpec(memory_space=pltpu.VMEM)] * 12,
         out_specs=pl.BlockSpec((rows, features), lambda i: (i, 0)),
         out_shape=jax.ShapeDtypeStruct((2 * rows, features), BF16),
         compiler_params=pltpu.CompilerParams(vmem_limit_bytes=12 << 20),
         name="project",
-    )(*top, *low, *weight, partial)
+    )(*mixed, *weight, partial)
 
 
 def on_device(gate_out, gate_in, value_in, filter_taps, skip_bias, resume_at, out_weight):
@@ -356,13 +377,13 @@
     up_top_other, down_low_other = toward(up_top, 0, 1), toward(down_low, 0, 1)
     weight = {route: weight[ROUTES.index(route)] for route in ROUTES}
     factors = [weight[route] for route in ((0, 0), (1, 0), (1, 1), (3, 0), (3, 1))]
-    partial, down_top, up_low = fold(
+    partial, late = fold(
         [top, up_top, up_top_other, down_top], [low, down_low, down_low_other, up_low], factors
     )
-    tops = [toward(top, 0, 1), far_top, toward(far_top, 0, 1), toward(down_top, 0, 1)]
-    lows = [toward(low, 0, 1), far_low, toward(far_low, 0, 1), toward(up_low, 0, 1)]
+    far_other = toward(join(far_top, far_low), 0, 1)
+    mixed = [toward(top, 0, 1), toward(low, 0, 1), far_top, far_low, far_other, toward(late, 0, 1)]
     factors = [weight[route] for route in ((0, 1), (2, 0), (2, 1), (3, 1), (1, 1))]
-    return project(tops, lows, factors, partial)
+    return project(mixed, factors, partial)
 
 
 def solution(mesh):

time: 79.8 us -> 80.5 us (level)
  waiting for transfers between devices: 12.1 us -> 14 us
  starting transfers between devices: 45 us -> 43.7 us
    ppermute x21 -> x19, waiting for transfers between devices: 5.5 us -> 7.44 us  [toward(): return lax.ppermute(array, 'chan', pairs)]
    ppermute x21 -> x19, starting transfers between devices: 30.7 us -> 29.4 us  [toward(): return lax.ppermute(array, 'chan', pairs)]
  transfers between devices with their start and end apart: 23 -> 21, of which waited for: 6 -> 7; matrix products, arithmetic and copies ran while one was open for 0% -> 0% of each run, Pallas kernels for 14% -> 14%
where the time goes in v7:
time: 80.5 us; the launch traced here: 80 us
  starting transfers between devices  43.7 us (54%)
  Pallas kernels  16.3 us (20%)
  waiting for transfers between devices  14 us (17%)
  local copies, waits for them, and re-layouts  5.18 us (6%)
  between operations  0.84 us (1%)
    ppermute x19, starting transfers between devices, toward(): return lax.ppermute(array, 'chan', pairs)  29.4 us
    all_to_all x1, starting transfers between devices, on_device(): lax.all_to_all(packed, 'seq', split_axis=0, concat_axis=0, tiled=True)  7.72 us
    ppermute x19, waiting for transfers between devices, toward(): return lax.ppermute(array, 'chan', pairs)  7.44 us
    pallas_call x1, Pallas kernels, convolve(): pl.pallas_call(functools.partial(conv_kernel, group), in_specs=[space] *...  7.28 us
    all_to_all x1, starting transfers between devices, on_device(): lax.all_to_all(convolve(unpack(data, weight[:2]), packed.shape[2]), 'seq'...  6.6 us
    all_to_all x1, waiting for transfers between devices, on_device(): lax.all_to_all(convolve(unpack(data, weight[:2]), packed.shape[2]), 'seq'...  6.23 us
    unnamed x34, local copies, waits for them, and re-layouts  5.18 us
    pallas_call x1, Pallas kernels, pack(): pl.pallas_call(pack_kernel, grid=(rows // (blocks * TILE),), in_specs=[bl...  2.66 us
  transfers between devices with their start and end apart: 21, of which 7 were waited for; matrix products, arithmetic and copies ran while one was open for 0% of the time, Pallas kernels for 14%

profile of v7, /device:TPU:1, one launch (start us, length us, event | category | flops | bytes accessed | tf_op | source)
XLA Modules:
  0.0 80.0 jit_solution(11748432162634285547)
XLA Ops:
  0.0 2.7 %pack.1 = (bf16[16,2,8,16,128]{4,3,2,1,0:T(8,128)(2,1)}, f32[8,128]{1,0:T(8,128)}) custom-call(bf16[1024,256]{1,0:T(8,128)(2,1)} %gate_in.3, bf16[1024,256]{1,0:T(8,128)(2,1)} %value_in.3, f32[1024,256]{1,0:T(8,128)} %taps.1), custom_call_target="tpu_custom_call" | custom-call | tf_op jit(solution)/shard_map/pack/pallas_call | solution.py:78
  2.7 7.7 %all-to-all-start = ((bf16[16,2,8,16,128]{4,3,2,1,0:T(8,128)(2,1)}), bf16[16,2,8,16,128]{4,3,2,1,0:T(8,128)(2,1)S(1)}, u32[]{:S(2)}, u32[]{:S(2)}) async-start(bf16[16,2,8,16,128]{4,3,2,1,0:T(8,128)(2,1)} %get-tuple-element.19), calls=%async_computation | async-start | bytes 2097152 | tf_op jit(solution)/shard_map/all_to_all | solution.py:369
  10.4 1.2 %split_weight.1 = (bf16[256,512]{1,0:T(8,128)(2,1)S(1)}, bf16[256,512]{1,0:T(8,128)(2,1)S(1)}, bf16[256,512]{1,0:T(8,128)(2,1)}, bf16[256,512]{1,0:T(8,128)(2,1)...) custom-call(bf16[256,4096]{1,0:T(8,128)(2,1)S(1)} %copy-done, ...), custom_call_target="tpu_custom_call" | custom-call | tf_op jit(solution)/shard_map/split_weight/pallas_call | solution.py:258
  12.3 1.6 %collective-permute-start = (bf16[256,512]{1,0:T(8,128)(2,1)S(1)}, bf16[256,512]{1,0:T(8,128)(2,1)S(1)}, u32[]{:S(2)}, u32[]{:S(2)}) collective-permute-start(bf16[256,512]{1,0:T(8,128)(2,1)S(1)} %get-tuple-element.21), channel_id=1, source_target_pairs={{0,2},{1,3},{2,4},{3,5},{4,6},{5,7},{6,0},{7,1},{8,10},{9,11},{10,... | collective-permute-start | bytes 786440 | tf_op jit(solution)/shard_map/ppermute | solution.py:239
  14.0 2.1 %collective-permute-start.1 = (bf16[256,512]{1,0:T(8,128)(2,1)S(1)}, bf16[256,512]{1,0:T(8,128)(2,1)S(1)}, u32[]{:S(2)}, u32[]{:S(2)}) collective-permute-start(bf16[256,512]{1,0:T(8,128)(2,1)S(1)} %get-tuple-element.22), channel_id=1, source_target_pairs={{0,6},{1,7},{2,0},{3,1},{4,2},{5,3},{6,4},{7,5},{8,14},{9,15},{10,... | collective-permute-start | bytes 786440 | tf_op jit(solution)/shard_map/ppermute | solution.py:239
  16.8 2.2 %collective-permute-start.3 = (bf16[256,512]{1,0:T(8,128)(2,1)}, bf16[256,512]{1,0:T(8,128)(2,1)S(1)}, u32[]{:S(2)}, u32[]{:S(2)}) collective-permute-start(bf16[256,512]{1,0:T(8,128)(2,1)} %get-tuple-element.24), channel_id=1, source_target_pairs={{0,7},{1,6},{2,1},{3,0},{4,3},{5,2},{6,5},{7,4},{8,15},{9,14},{10,... | collective-permute-start | bytes 786440 | tf_op jit(solution)/shard_map/ppermute | solution.py:239
  19.1 1.1 %collective-permute-start.4 = (bf16[256,512]{1,0:T(8,128)(2,1)}, bf16[256,512]{1,0:T(8,128)(2,1)S(1)}, u32[]{:S(2)}, u32[]{:S(2)}) collective-permute-start(bf16[256,512]{1,0:T(8,128)(2,1)} %get-tuple-element.25), channel_id=1, source_target_pairs={{0,4},{1,5},{2,6},{3,7},{4,0},{5,1},{6,2},{7,3},{8,12},{9,13},{10,... | collective-permute-start | bytes 786440 | tf_op jit(solution)/shard_map/ppermute | solution.py:239
  20.8 1.0 %collective-permute-done.rest_0_.refs_0_.refs_9_ = bf16[256,512]{1,0:T(8,128)(2,1)S(1)} collective-permute-done((bf16[256,512]{1,0:T(8,128)(2,1)S(1)}, bf16[256,512]{1,0:T(8,128)(2,1)S(1)}, u32[]{:S(2)}, u32[]{:S(2)}) %collective-permute-start) | collective-permute-done | bytes 262176 | tf_op jit(solution)/shard_map/ppermute | solution.py:239
  21.8 4.2 %collective-permute-start.5 = (bf16[256,512]{1,0:T(8,128)(2,1)}, bf16[256,512]{1,0:T(8,128)(2,1)S(1)}, u32[]{:S(2)}, u32[]{:S(2)}) collective-permute-start(bf16[256,512]{1,0:T(8,128)(2,1)} %get-tuple-element.26), channel_id=1, source_target_pairs={{0,5},{1,4},{2,7},{3,6},{4,1},{5,0},{6,3},{7,2},{8,13},{9,12},{10,... | collective-permute-start | bytes 786440 | tf_op jit(solution)/shard_map/ppermute | solution.py:239
  26.4 1.0 %unpack.1.pairs = bf16[16,128,256]{2,1,0:T(8,128)(2,1)S(1)} custom-call(bf16[16,2,8,16,128]{4,3,2,1,0:T(8,128)(2,1)S(1)} %all-to-all-done.data, bf16[256,512]{1,0:T(8,128)(2,1)S(1)} %collective-permute-done.rest_0_.refs_0_.refs_9_, bf16[256,512]{1,0:T(8,128)(2,1)S(1)} %collective-permute-done.1.rest_1_.refs_1_.refs_11_), custom_call_target="tpu_custom_call" | custom-call | tf_op jit(solution)/shard_map/unpack/pallas_call | solution.py:114
  27.6 7.3 %convolve.1 = bf16[16,8,16,128]{3,2,1,0:T(8,128)(2,1)} custom-call(bf16[16,128,256]{2,1,0:T(8,128)(2,1)S(1)} %unpack.1.pairs, bf16[2176,256]{1,0:T(8,128)(2,1)S(1)} %copy-done.15, f32[256,128]{1,0:T(8,128)S(1)} %copy-done.16), custom_call_target="tpu_custom_call" | custom-call | flops 10000000000 | bytes 4194304 | tf_op jit(solution)/shard_map/convolve/pallas_call | solution.py:177
  34.9 6.6 %all-to-all-start.1 = ((bf16[16,8,16,128]{3,2,1,0:T(8,128)(2,1)}), bf16[16,8,16,128]{3,2,1,0:T(8,128)(2,1)S(1)}, u32[]{:S(2)}, u32[]{:S(2)}) async-start(bf16[16,8,16,128]{3,2,1,0:T(8,128)(2,1)} %convolve.1), calls=%async_computation.1 | async-start | bytes 1048576 | tf_op jit(solution)/shard_map/all_to_all | solution.py:372
  45.8 6.2 %all-to-all-done.1.conv = bf16[16,8,16,128]{3,2,1,0:T(8,128)(2,1)S(1)} async-done(((bf16[16,8,16,128]{3,2,1,0:T(8,128)(2,1)}), bf16[16,8,16,128]{3,2,1,0:T(8,128)(2,1)S(1)}, u32[]{:S(2)}, u32[]{:S(2)}) %all-to-all-start.1) | async-done | bytes 524320 | tf_op jit(solution)/shard_map/all_to_all | solution.py:372
  53.5 1.9 %collective-permute-start.11 = (bf16[512,256]{1,0:T(8,128)(2,1)S(1)}, bf16[512,256]{1,0:T(8,128)(2,1)S(1)}, u32[]{:S(2)}, u32[]{:S(2)}) collective-permute-start(bf16[512,256]{1,0:T(8,128)(2,1)S(1)} %get-tuple-element.30.refs_4_), channel_id=1, source_target_pairs={{0,6},{1,7},{2,0},{3,1},{4,2},{5,3},{6,4},{7,5},{8,14},{9,15},{10,... | collective-permute-start | bytes 786440 | tf_op jit(solution)/shard_map/ppermute | solution.py:239
  55.4 1.4 %collective-permute-start.17 = (bf16[512,256]{1,0:T(8,128)(2,1)S(1)}, bf16[512,256]{1,0:T(8,128)(2,1)S(1)}, u32[]{:S(2)}, u32[]{:S(2)}) collective-permute-start(bf16[512,256]{1,0:T(8,128)(2,1)S(1)} %get-tuple-element.30.refs_4_), channel_id=1, source_target_pairs={{0,2},{1,3},{2,4},{3,5},{4,6},{5,7},{6,0},{7,1},{8,10},{9,11},{10,... | collective-permute-start | bytes 786440 | tf_op jit(solution)/shard_map/ppermute | solution.py:239
  56.9 2.9 %collective-permute-done.9.refs_1_ = bf16[512,256]{1,0:T(8,128)(2,1)S(1)} collective-permute-done((bf16[512,256]{1,0:T(8,128)(2,1)S(1)}, bf16[512,256]{1,0:T(8,128)(2,1)S(1)}, u32[]{:S(2)}, u32[]{:S(2)}) %collective-permute-start.9) | collective-permute-done | bytes 262176 | tf_op jit(solution)/shard_map/ppermute | solution.py:239
  59.8 5.3 %collective-permute-start.14 = (bf16[512,256]{1,0:T(8,128)(2,1)S(1)}, bf16[512,256]{1,0:T(8,128)(2,1)S(1)}, u32[]{:S(2)}, u32[]{:S(2)}) collective-permute-start(bf16[512,256]{1,0:T(8,128)(2,1)S(1)} %collective-permute-done.9.refs_1_), channel_id=1, source_target_pairs={{0,1},{1,0},{2,3},{3,2},{4,5},{5,4},{6,7},{7,6},{8,9},{9,8},{10,11... | collective-permute-start | bytes 786440 | tf_op jit(solution)/shard_map/ppermute | solution.py:239
  65.3 2.8 %collective-permute-start.12 = (bf16[512,256]{1,0:T(8,128)(2,1)S(1)}, bf16[512,256]{1,0:T(8,128)(2,1)S(1)}, u32[]{:S(2)}, u32[]{:S(2)}) collective-permute-start(bf16[512,256]{1,0:T(8,128)(2,1)S(1)} %collective-permute-done.11.refs_5_), channel_id=1, source_target_pairs={{0,6},{1,7},{2,0},{3,1},{4,2},{5,3},{6,4},{7,5},{8,14},{9,15},{10,... | collective-permute-start | bytes 786440 | tf_op jit(solution)/shard_map/ppermute | solution.py:239
  68.1 1.2 %fold.1 = (f32[1024,512]{1,0:T(8,128)S(1)}, bf16[1024,256]{1,0:T(8,128)(2,1)S(1)}) custom-call(bf16[512,256]{1,0:T(8,128)(2,1)S(1)} %get-tuple-element.29.refs_0_, bf16[512,256]{1,0:T(8,128)(2,1)S(1)} %collective-permute-done.9.refs_1_, bf16[512,256]{1,0:T(8,128)(2,1)S(1)} %collective-permute-done.14.refs_2_, ...), custom_call_target="tpu_custom_call" | custom-call | tf_op jit(solution)/shard_map/fold/pallas_call | solution.py:306
  69.3 3.2 %collective-permute-start.18 = (bf16[1024,256]{1,0:T(8,128)(2,1)S(1)}, bf16[1024,256]{1,0:T(8,128)(2,1)S(1)}, u32[]{:S(2)}, u32[]{:S(2)}) collective-permute-start(bf16[1024,256]{1,0:T(8,128)(2,1)S(1)} %get-tuple-element.31), channel_id=1, source_target_pairs={{0,1},{1,0},{2,3},{3,2},{4,5},{5,4},{6,7},{7,6},{8,9},{9,8},{10,11... | collective-permute-start | bytes 1572872 | tf_op jit(solution)/shard_map/ppermute | solution.py:239
  72.6 1.7 %collective-permute-done.10.first.refs_2_ = bf16[512,256]{1,0:T(8,128)(2,1)S(1)} collective-permute-done((bf16[512,256]{1,0:T(8,128)(2,1)S(1)}, bf16[512,256]{1,0:T(8,128)(2,1)S(1)}, u32[]{:S(2)}, u32[]{:S(2)}) %collective-permute-start.10) | collective-permute-done | bytes 262176 | tf_op jit(solution)/shard_map/ppermute | solution.py:239
  74.3 1.1 %collective-permute-start.13 = (bf16[1024,256]{1,0:T(8,128)(2,1)S(1)}, bf16[1024,256]{1,0:T(8,128)(2,1)S(1)}, u32[]{:S(2)}, u32[]{:S(2)}) collective-permute-start(bf16[1024,256]{1,0:T(8,128)(2,1)S(1)} %join.1), channel_id=1, source_target_pairs={{0,1},{1,0},{2,3},{3,2},{4,5},{5,4},{6,7},{7,6},{8,9},{9,8},{10,11... | collective-permute-start | bytes 1572872 | tf_op jit(solution)/shard_map/ppermute | solution.py:239
  76.0 1.4 %collective-permute-done.7.refs_0_ = bf16[512,256]{1,0:T(8,128)(2,1)S(1)} collective-permute-done((bf16[512,256]{1,0:T(8,128)(2,1)S(1)}, bf16[512,256]{1,0:T(8,128)(2,1)S(1)}, u32[]{:S(2)}, u32[]{:S(2)}) %collective-permute-start.7) | collective-permute-done | bytes 262176 | tf_op jit(solution)/shard_map/ppermute | solution.py:239
  77.8 2.3 %project.1 = bf16[1024,512]{1,0:T(8,128)(2,1)} custom-call(bf16[512,256]{1,0:T(8,128)(2,1)S(1)} %collective-permute-done.7.refs_0_, bf16[512,256]{1,0:T(8,128)(2,1)S(1)} %collective-permute-done.8.refs_1_, bf16[512,256]{1,0:T(8,128)(2,1)S(1)} %collective-permute-done.10.first.refs_2_, bf16[512,256]{1,0:T(8,128)(2,1)S(1)} %collective-permute-done.12.second.refs_3_, ...), custom_call_target="tpu_custom_call" | custom-call | tf_op jit(solution)/shard_map/project/pallas_call | solution.py:356
  (61 shorter events, 8.8 us)
Async XLA Ops:
  2.7 23.7 %all-to-all-start = ((bf16[16,2,8,16,128]{4,3,2,1,0:T(8,128)(2,1)}), bf16[16,2,8,16,128]{4,3,2,1,0:T(8,128)(2,1)S(1)}, u32[]{:S(2)}, u32[]{:S(2)}) async-start(bf16[16,2,8,16,128]{4,3,2,1,0:T(8,128)(2,1)} %get-tuple-element.19), calls=%async_computation | async-start | bytes 2097152 | tf_op jit(solution)/shard_map/all_to_all | solution.py:369
  10.4 17.0 %copy-start.16 = (f32[256,128]{1,0:T(8,128)S(1)}, f32[256,128]{1,0:T(8,128)}, u32[]{:S(2)}) copy-start(f32[256,128]{1,0:T(8,128)} %constant.5.clone.twists) | copy-start | bytes 393220
  12.3 9.5 %collective-permute-start = (bf16[256,512]{1,0:T(8,128)(2,1)S(1)}, bf16[256,512]{1,0:T(8,128)(2,1)S(1)}, u32[]{:S(2)}, u32[]{:S(2)}) collective-permute-start(bf16[256,512]{1,0:T(8,128)(2,1)S(1)} %get-tuple-element.21), channel_id=1, source_target_pairs={{0,2},{1,3},{2,4},{3,5},{4,6},{5,7},{6,0},{7,1},{8,10},{9,11},{10,... | collective-permute-start | bytes 786440 | tf_op jit(solution)/shard_map/ppermute | solution.py:239
  14.0 12.0 %collective-permute-start.1 = (bf16[256,512]{1,0:T(8,128)(2,1)S(1)}, bf16[256,512]{1,0:T(8,128)(2,1)S(1)}, u32[]{:S(2)}, u32[]{:S(2)}) collective-permute-start(bf16[256,512]{1,0:T(8,128)(2,1)S(1)} %get-tuple-element.22), channel_id=1, source_target_pairs={{0,6},{1,7},{2,0},{3,1},{4,2},{5,3},{6,4},{7,5},{8,14},{9,15},{10,... | collective-permute-start | bytes 786440 | tf_op jit(solution)/shard_map/ppermute | solution.py:239
  16.1 25.4 %collective-permute-start.2 = (bf16[256,512]{1,0:T(8,128)(2,1)}, bf16[256,512]{1,0:T(8,128)(2,1)S(1)}, u32[]{:S(2)}, u32[]{:S(2)}) collective-permute-start(bf16[256,512]{1,0:T(8,128)(2,1)} %get-tuple-element.23), channel_id=1, source_target_pairs={{0,3},{1,2},{2,5},{3,4},{4,7},{5,6},{6,1},{7,0},{8,11},{9,10},{10,... | collective-permute-start | bytes 786440 | tf_op jit(solution)/shard_map/ppermute | solution.py:239
  16.8 24.7 %collective-permute-start.3 = (bf16[256,512]{1,0:T(8,128)(2,1)}, bf16[256,512]{1,0:T(8,128)(2,1)S(1)}, u32[]{:S(2)}, u32[]{:S(2)}) collective-permute-start(bf16[256,512]{1,0:T(8,128)(2,1)} %get-tuple-element.24), channel_id=1, source_target_pairs={{0,7},{1,6},{2,1},{3,0},{4,3},{5,2},{6,5},{7,4},{8,15},{9,14},{10,... | collective-permute-start | bytes 786440 | tf_op jit(solution)/shard_map/ppermute | solution.py:239
  19.1 22.5 %collective-permute-start.4 = (bf16[256,512]{1,0:T(8,128)(2,1)}, bf16[256,512]{1,0:T(8,128)(2,1)S(1)}, u32[]{:S(2)}, u32[]{:S(2)}) collective-permute-start(bf16[256,512]{1,0:T(8,128)(2,1)} %get-tuple-element.25), channel_id=1, source_target_pairs={{0,4},{1,5},{2,6},{3,7},{4,0},{5,1},{6,2},{7,3},{8,12},{9,13},{10,... | collective-permute-start | bytes 786440 | tf_op jit(solution)/shard_map/ppermute | solution.py:239
  21.8 19.7 %collective-permute-start.5 = (bf16[256,512]{1,0:T(8,128)(2,1)}, bf16[256,512]{1,0:T(8,128)(2,1)S(1)}, u32[]{:S(2)}, u32[]{:S(2)}) collective-permute-start(bf16[256,512]{1,0:T(8,128)(2,1)} %get-tuple-element.26), channel_id=1, source_target_pairs={{0,5},{1,4},{2,7},{3,6},{4,1},{5,0},{6,3},{7,2},{8,13},{9,12},{10,... | collective-permute-start | bytes 786440 | tf_op jit(solution)/shard_map/ppermute | solution.py:239
  26.0 16.2 %collective-permute-start.6 = (bf16[256,512]{1,0:T(8,128)(2,1)}, bf16[256,512]{1,0:T(8,128)(2,1)S(1)}, u32[]{:S(2)}, u32[]{:S(2)}) collective-permute-start(bf16[256,512]{1,0:T(8,128)(2,1)} %get-tuple-element.27), channel_id=1, source_target_pairs={{0,1},{1,0},{2,3},{3,2},{4,5},{5,4},{6,7},{7,6},{8,9},{9,8},{10,11... | collective-permute-start | bytes 786440 | tf_op jit(solution)/shard_map/ppermute | solution.py:239
  34.9 17.2 %all-to-all-start.1 = ((bf16[16,8,16,128]{3,2,1,0:T(8,128)(2,1)}), bf16[16,8,16,128]{3,2,1,0:T(8,128)(2,1)S(1)}, u32[]{:S(2)}, u32[]{:S(2)}) async-start(bf16[16,8,16,128]{3,2,1,0:T(8,128)(2,1)} %convolve.1), calls=%async_computation.1 | async-start | bytes 1048576 | tf_op jit(solution)/shard_map/all_to_all | solution.py:372
  52.6 7.1 %collective-permute-start.9 = (bf16[512,256]{1,0:T(8,128)(2,1)S(1)}, bf16[512,256]{1,0:T(8,128)(2,1)S(1)}, u32[]{:S(2)}, u32[]{:S(2)}) collective-permute-start(bf16[512,256]{1,0:T(8,128)(2,1)S(1)} %get-tuple-element.29.refs_0_), channel_id=1, source_target_pairs={{0,2},{1,3},{2,4},{3,5},{4,6},{5,7},{6,0},{7,1},{8,10},{9,11},{10,... | collective-permute-start | bytes 786440 | tf_op jit(solution)/shard_map/ppermute | solution.py:239
  53.5 24.3 %copy-start.6 = (bf16[256,512]{1,0:T(8,128)(2,1)S(1)}, bf16[256,512]{1,0:T(8,128)(2,1)}, u32[]{:S(2)}) copy-start(bf16[256,512]{1,0:T(8,128)(2,1)} %copy-done.4) | copy-start | bytes 786436
  53.5 24.3 %copy-start.9 = (bf16[256,512]{1,0:T(8,128)(2,1)S(1)}, bf16[256,512]{1,0:T(8,128)(2,1)}, u32[]{:S(2)}) copy-start(bf16[256,512]{1,0:T(8,128)(2,1)} %copy-done.7) | copy-start | bytes 786436
  53.5 11.6 %collective-permute-start.11 = (bf16[512,256]{1,0:T(8,128)(2,1)S(1)}, bf16[512,256]{1,0:T(8,128)(2,1)S(1)}, u32[]{:S(2)}, u32[]{:S(2)}) collective-permute-start(bf16[512,256]{1,0:T(8,128)(2,1)S(1)} %get-tuple-element.30.refs_4_), channel_id=1, source_target_pairs={{0,6},{1,7},{2,0},{3,1},{4,2},{5,3},{6,4},{7,5},{8,14},{9,15},{10,... | collective-permute-start | bytes 786440 | tf_op jit(solution)/shard_map/ppermute | solution.py:239
  55.4 9.9 %collective-permute-start.15 = (bf16[512,256]{1,0:T(8,128)(2,1)S(1)}, bf16[512,256]{1,0:T(8,128)(2,1)S(1)}, u32[]{:S(2)}, u32[]{:S(2)}) collective-permute-start(bf16[512,256]{1,0:T(8,128)(2,1)S(1)} %get-tuple-element.29.refs_0_), channel_id=1, source_target_pairs={{0,6},{1,7},{2,0},{3,1},{4,2},{5,3},{6,4},{7,5},{8,14},{9,15},{10,... | collective-permute-start | bytes 786440 | tf_op jit(solution)/shard_map/ppermute | solution.py:239
  55.4 12.6 %collective-permute-start.17 = (bf16[512,256]{1,0:T(8,128)(2,1)S(1)}, bf16[512,256]{1,0:T(8,128)(2,1)S(1)}, u32[]{:S(2)}, u32[]{:S(2)}) collective-permute-start(bf16[512,256]{1,0:T(8,128)(2,1)S(1)} %get-tuple-element.30.refs_4_), channel_id=1, source_target_pairs={{0,2},{1,3},{2,4},{3,5},{4,6},{5,7},{6,0},{7,1},{8,10},{9,11},{10,... | collective-permute-start | bytes 786440 | tf_op jit(solution)/shard_map/ppermute | solution.py:239
  59.8 8.3 %collective-permute-start.14 = (bf16[512,256]{1,0:T(8,128)(2,1)S(1)}, bf16[512,256]{1,0:T(8,128)(2,1)S(1)}, u32[]{:S(2)}, u32[]{:S(2)}) collective-permute-start(bf16[512,256]{1,0:T(8,128)(2,1)S(1)} %collective-permute-done.9.refs_1_), channel_id=1, source_target_pairs={{0,1},{1,0},{2,3},{3,2},{4,5},{5,4},{6,7},{7,6},{8,9},{9,8},{10,11... | collective-permute-start | bytes 786440 | tf_op jit(solution)/shard_map/ppermute | solution.py:239
  65.1 3.0 %collective-permute-start.16 = (bf16[512,256]{1,0:T(8,128)(2,1)S(1)}, bf16[512,256]{1,0:T(8,128)(2,1)S(1)}, u32[]{:S(2)}, u32[]{:S(2)}) collective-permute-start(bf16[512,256]{1,0:T(8,128)(2,1)S(1)} %collective-permute-done.11.refs_5_), channel_id=1, source_target_pairs={{0,1},{1,0},{2,3},{3,2},{4,5},{5,4},{6,7},{7,6},{8,9},{9,8},{10,11... | collective-permute-start | bytes 786440 | tf_op jit(solution)/shard_map/ppermute | solution.py:239
  65.1 9.2 %collective-permute-start.10 = (bf16[512,256]{1,0:T(8,128)(2,1)S(1)}, bf16[512,256]{1,0:T(8,128)(2,1)S(1)}, u32[]{:S(2)}, u32[]{:S(2)}) collective-permute-start(bf16[512,256]{1,0:T(8,128)(2,1)S(1)} %collective-permute-done.9.refs_1_), channel_id=1, source_target_pairs={{0,2},{1,3},{2,4},{3,5},{4,6},{5,7},{6,0},{7,1},{8,10},{9,11},{10,... | collective-permute-start | bytes 786440 | tf_op jit(solution)/shard_map/ppermute | solution.py:239
  65.3 9.0 %collective-permute-start.12 = (bf16[512,256]{1,0:T(8,128)(2,1)S(1)}, bf16[512,256]{1,0:T(8,128)(2,1)S(1)}, u32[]{:S(2)}, u32[]{:S(2)}) collective-permute-start(bf16[512,256]{1,0:T(8,128)(2,1)S(1)} %collective-permute-done.11.refs_5_), channel_id=1, source_target_pairs={{0,6},{1,7},{2,0},{3,1},{4,2},{5,3},{6,4},{7,5},{8,14},{9,15},{10,... | collective-permute-start | bytes 786440 | tf_op jit(solution)/shard_map/ppermute | solution.py:239
  69.3 8.4 %collective-permute-start.18 = (bf16[1024,256]{1,0:T(8,128)(2,1)S(1)}, bf16[1024,256]{1,0:T(8,128)(2,1)S(1)}, u32[]{:S(2)}, u32[]{:S(2)}) collective-permute-start(bf16[1024,256]{1,0:T(8,128)(2,1)S(1)} %get-tuple-element.31), channel_id=1, source_target_pairs={{0,1},{1,0},{2,3},{3,2},{4,5},{5,4},{6,7},{7,6},{8,9},{9,8},{10,11... | collective-permute-start | bytes 1572872 | tf_op jit(solution)/shard_map/ppermute | solution.py:239
  74.3 3.4 %collective-permute-start.13 = (bf16[1024,256]{1,0:T(8,128)(2,1)S(1)}, bf16[1024,256]{1,0:T(8,128)(2,1)S(1)}, u32[]{:S(2)}, u32[]{:S(2)}) collective-permute-start(bf16[1024,256]{1,0:T(8,128)(2,1)S(1)} %join.1), channel_id=1, source_target_pairs={{0,1},{1,0},{2,3},{3,2},{4,5},{5,4},{6,7},{7,6},{8,9},{9,8},{10,11... | collective-permute-start | bytes 1572872 | tf_op jit(solution)/shard_map/ppermute | solution.py:239
  75.4 1.9 %collective-permute-start.7 = (bf16[512,256]{1,0:T(8,128)(2,1)S(1)}, bf16[512,256]{1,0:T(8,128)(2,1)S(1)}, u32[]{:S(2)}, u32[]{:S(2)}) collective-permute-start(bf16[512,256]{1,0:T(8,128)(2,1)S(1)} %get-tuple-element.29.refs_0_), channel_id=1, source_target_pairs={{0,1},{1,0},{2,3},{3,2},{4,5},{5,4},{6,7},{7,6},{8,9},{9,8},{10,11... | collective-permute-start | bytes 786440 | tf_op jit(solution)/shard_map/ppermute | solution.py:239
  75.5 2.2 %collective-permute-start.8 = (bf16[512,256]{1,0:T(8,128)(2,1)S(1)}, bf16[512,256]{1,0:T(8,128)(2,1)S(1)}, u32[]{:S(2)}, u32[]{:S(2)}) collective-permute-start(bf16[512,256]{1,0:T(8,128)(2,1)S(1)} %get-tuple-element.30.refs_4_), channel_id=1, source_target_pairs={{0,1},{1,0},{2,3},{3,2},{4,5},{5,4},{6,7},{7,6},{8,9},{9,8},{10,11... | collective-permute-start | bytes 786440 | tf_op jit(solution)/shard_map/ppermute | solution.py:239
  (14 other events, 65.4 us)
